TPU v7x, 32 devices: a whole 2x2x4 slice. The times are simulated.
32 devices in a mesh: dp: 8 (over y, x, core), tensor: 4 (over z).
Axes of the slice: x: 2, y: 2, z: 4, core: 2. Of those that a mesh axis runs over, the one named last changes fastest.
Arguments:
- prefix_tokens: bfloat16 [16, 256, 5120], P('dp'), may hold values from -6 to 6
- prefix_len: int32 [16], P('dp'), may hold values from 64 to 256, as said below
- causal_start: int32 [16], P('dp'), may hold values from 32 to 64
- span_sample: int32 [64], P('dp'), may hold values from 0 to 1
- bb_wq: bfloat16 [5120, 4096], P('dp', 'tensor'), may hold values from -4 to 4
- bb_wk: bfloat16 [5120, 1024], P('dp', 'tensor'), may hold values from -1 to 1
- bb_wv: bfloat16 [5120, 1024], P('dp', 'tensor'), may hold values from -0.078125 to 0.078125
- bb_wo: bfloat16 [4096, 5120], P('tensor', 'dp'), may hold values from -0.09375 to 0.09375
- action_tokens: bfloat16 [64, 50, 1024], P('dp'), may hold values from -6 to 6
- ex_wq: bfloat16 [1024, 2048], P(None, 'tensor'), may hold values from -8 to 8
- ex_wk: bfloat16 [1024, 1024], P(None, 'tensor'), may hold values from -1 to 1
- ex_wv: bfloat16 [1024, 1024], P(None, 'tensor'), may hold values from -0.1875 to 0.1875
- ex_wo: bfloat16 [2048, 1024], P('tensor'), may hold values from -0.125 to 0.125
- action_cot: bfloat16 [64, 50, 1024], P('dp'), may hold values from -6 to 6
Outputs:
- prefix_out: bfloat16 [16, 256, 5120], P('dp', None, 'tensor')
- grad_wq: float32 [1024, 2048], P(None, 'tensor')
- grad_wk: float32 [1024, 1024], P(None, 'tensor')
- grad_wv: float32 [1024, 1024], P(None, 'tensor')
- grad_wo: float32 [2048, 1024], P('tensor')
Inputs may be any that keep to these rules, and one draw needn't show every extreme that they name: `prefix_len`: some sample has all 256 positions valid.
All inputs are finite; a program needn't handle non-finite values.
Results may differ from a plain program's by a relative error of at most 0.003.
The roundings to bfloat16 on the way count: a program that leaves them out, or rounds other values in their place, can miss the bound.
Values may be sent and summed in bfloat16 or wider, within the bound.
No kernel may reach another device: no remote copies, remote signals or barrier semaphores. Data moves between devices by JAX's collectives and lax.ppermute only.
A program may use at most 192 MiB of HBM per device.

v0:
```python
import math

import jax
import jax.numpy as jnp
from jax import lax
from jax.sharding import PartitionSpec as P

HD = 128
STEPS = 50


def body(
    prefix_tokens,
    prefix_len,
    causal_start,
    span_sample,
    bb_wq,
    bb_wk,
    bb_wv,
    bb_wo,
    action_tokens,
    ex_wq,
    ex_wk,
    ex_wv,
    ex_wo,
    action_cot,
):
    samples, positions, width = prefix_tokens.shape
    factor = 1.0 / math.sqrt(HD)
    kv_local = bb_wk.shape[1] // HD
    group = bb_wq.shape[1] // bb_wk.shape[1]
    egroup = ex_wq.shape[1] // ex_wk.shape[1]
    count = samples * positions
    flat = prefix_tokens.reshape(count, width)
    widened = flat.astype(jnp.float32)
    normed = (
        widened * lax.rsqrt(jnp.mean(widened * widened, axis=-1, keepdims=True) + 1e-06)
    ).astype(jnp.bfloat16)
    pieces = (
        lax.all_gather(bb_wq, "dp", axis=0, tiled=True),
        lax.all_gather(bb_wk, "dp", axis=0, tiled=True),
        lax.all_gather(bb_wv, "dp", axis=0, tiled=True),
    )
    query_sum, key_sum, value_sum = tuple(
        (jnp.dot(normed, piece, preferred_element_type=jnp.float32) for piece in pieces)
    )
    query = query_sum.astype(jnp.bfloat16).reshape(samples, positions, kv_local, group, HD)
    keys = key_sum.astype(jnp.bfloat16).reshape(samples, positions, kv_local, HD)
    values = value_sum.astype(jnp.bfloat16).reshape(samples, positions, kv_local, HD)
    scores = (
        jnp.einsum("sigeh,sjgh->sgeij", query, keys, preferred_element_type=jnp.float32) * factor
    )
    places = jnp.arange(positions, dtype=jnp.int32)
    length_view = prefix_len[:, None, None, None, None]
    start_view = causal_start[:, None, None, None, None]
    visible = (places[None, None, None, None, :] < length_view) & (
        (places[None, None, None, None, :] < start_view)
        | (places[None, None, None, None, :] <= places[None, None, None, :, None])
    )
    scores = jnp.where(visible, scores, -1e30)
    top = jnp.max(scores, axis=-1, keepdims=True)
    weights = jnp.where(visible, jnp.exp(scores - top), 0.0)
    weights = (weights / jnp.sum(weights, axis=-1, keepdims=True)).astype(jnp.bfloat16)
    context = (
        jnp.einsum("sgeij,sjgh->sigeh", weights, values, preferred_element_type=jnp.float32)
        .astype(jnp.bfloat16)
        .reshape(count, bb_wq.shape[1])
    )
    partial_out = jnp.dot(
        context, lax.all_gather(bb_wo, "dp", axis=1, tiled=True), preferred_element_type=jnp.float32
    )
    summed = lax.psum_scatter(partial_out, "tensor", scatter_dimension=1, tiled=True)
    share = summed.shape[1]
    residual = lax.dynamic_slice_in_dim(widened, lax.axis_index("tensor") * share, share, 1)
    prefix_out = (residual + summed).astype(jnp.bfloat16).reshape(samples, positions, share)
    spans = action_tokens.shape[0]
    rows = spans * STEPS
    action_flat = action_tokens.reshape(rows, action_tokens.shape[2])
    cot_flat = action_cot.reshape(rows, action_cot.shape[2])
    pre_keys = jnp.take(keys, span_sample, axis=0)
    pre_values = jnp.take(values, span_sample, axis=0)
    span_length = jnp.take(prefix_len, span_sample, axis=0)
    equery = (
        jnp.dot(action_flat, ex_wq, preferred_element_type=jnp.float32)
        .astype(jnp.bfloat16)
        .reshape(spans, STEPS, kv_local, egroup, HD)
    )
    own_keys = (
        jnp.dot(action_flat, ex_wk, preferred_element_type=jnp.float32)
        .astype(jnp.bfloat16)
        .reshape(spans, STEPS, kv_local, HD)
    )
    own_values = (
        jnp.dot(action_flat, ex_wv, preferred_element_type=jnp.float32)
        .astype(jnp.bfloat16)
        .reshape(spans, STEPS, kv_local, HD)
    )
    valid = (places[None, :] < span_length[:, None])[:, None, None, None, :]
    score_pre = (
        jnp.einsum("ctgeh,cpgh->cgetp", equery, pre_keys, preferred_element_type=jnp.float32)
        * factor
    )
    score_pre = jnp.where(valid, score_pre, -1e30)
    score_own = (
        jnp.einsum("ctgeh,cugh->cgetu", equery, own_keys, preferred_element_type=jnp.float32)
        * factor
    )
    peak = jnp.maximum(jnp.max(score_pre, axis=-1), jnp.max(score_own, axis=-1))[..., None]
    exp_pre = jnp.where(valid, jnp.exp(score_pre - peak), 0.0)
    exp_own = jnp.exp(score_own - peak)
    total = jnp.sum(exp_pre, axis=-1, keepdims=True) + jnp.sum(exp_own, axis=-1, keepdims=True)
    prob_pre = exp_pre / total
    prob_own = exp_own / total
    half_pre = prob_pre.astype(jnp.bfloat16)
    half_own = prob_own.astype(jnp.bfloat16)
    econtext = (
        jnp.einsum("cgetp,cpgh->ctgeh", half_pre, pre_values, preferred_element_type=jnp.float32)
        + jnp.einsum("cgetu,cugh->ctgeh", half_own, own_values, preferred_element_type=jnp.float32)
    ).astype(jnp.bfloat16)
    econtext_flat = econtext.reshape(rows, ex_wq.shape[1])
    grad_out_local = jnp.einsum(
        "ti,tj->ij", econtext_flat, cot_flat, preferred_element_type=jnp.float32
    )
    dcontext = (
        jnp.einsum("tj,ij->ti", cot_flat, ex_wo, preferred_element_type=jnp.float32)
        .astype(jnp.bfloat16)
        .reshape(spans, STEPS, kv_local, egroup, HD)
    )
    dprob_pre = jnp.einsum(
        "ctgeh,cpgh->cgetp", dcontext, pre_values, preferred_element_type=jnp.float32
    )
    dprob_own = jnp.einsum(
        "ctgeh,cugh->cgetu", dcontext, own_values, preferred_element_type=jnp.float32
    )
    delta = (jnp.sum(prob_pre * dprob_pre, axis=-1) + jnp.sum(prob_own * dprob_own, axis=-1))[
        ..., None
    ]
    dscore_pre = (prob_pre * (dprob_pre - delta) * factor).astype(jnp.bfloat16)
    dscore_own = (prob_own * (dprob_own - delta) * factor).astype(jnp.bfloat16)
    dquery = (
        jnp.einsum("cgetp,cpgh->ctgeh", dscore_pre, pre_keys, preferred_element_type=jnp.float32)
        + jnp.einsum("cgetu,cugh->ctgeh", dscore_own, own_keys, preferred_element_type=jnp.float32)
    ).astype(jnp.bfloat16)
    dkeys = jnp.einsum(
        "cgetu,ctgeh->cugh", dscore_own, equery, preferred_element_type=jnp.float32
    ).astype(jnp.bfloat16)
    dvalues = jnp.einsum(
        "cgetu,ctgeh->cugh", half_own, dcontext, preferred_element_type=jnp.float32
    ).astype(jnp.bfloat16)
    grad_query_local = jnp.einsum(
        "ti,tj->ij",
        action_flat,
        dquery.reshape(rows, ex_wq.shape[1]),
        preferred_element_type=jnp.float32,
    )
    grad_key_local = jnp.einsum(
        "ti,tj->ij",
        action_flat,
        dkeys.reshape(rows, ex_wk.shape[1]),
        preferred_element_type=jnp.float32,
    )
    grad_value_local = jnp.einsum(
        "ti,tj->ij",
        action_flat,
        dvalues.reshape(rows, ex_wv.shape[1]),
        preferred_element_type=jnp.float32,
    )
    grad_wq, grad_wk, grad_wv, grad_wo = lax.psum(
        (grad_query_local, grad_key_local, grad_value_local, grad_out_local), "dp"
    )
    return (prefix_out, grad_wq, grad_wk, grad_wv, grad_wo)


def solution(mesh):
    in_specs = (
        P("dp", None, None),
        P("dp"),
        P("dp"),
        P("dp"),
        P("dp", "tensor"),
        P("dp", "tensor"),
        P("dp", "tensor"),
        P("tensor", "dp"),
        P("dp", None, None),
        P(None, "tensor"),
        P(None, "tensor"),
        P(None, "tensor"),
        P("tensor", None),
        P("dp", None, None),
    )
    out_specs = (
        P("dp", None, "tensor"),
        P(None, "tensor"),
        P(None, "tensor"),
        P(None, "tensor"),
        P("tensor", None),
    )
    return jax.shard_map(body, mesh=mesh, in_specs=in_specs, out_specs=out_specs, check_vma=False)
```

profile of v0, /device:TPU:0, one launch (start us, length us, event | category | flops | bytes accessed | tf_op | source)
XLA Modules:
  0.0 507.0 jit_solution(2984603232401404835)
XLA Ops:
  10.0 3.7 multiply_reduce_fusion
  14.4 1.3 convolution_convert_fusion.2
  16.9 1.4 convolution_convert_fusion.6
  19.1 2.2 convolution_convert_fusion.1
  22.2 1.4 convolution_convert_fusion.5
  26.7 10.2 %multiply_convert_fusion = (bf16[512,5120]{1,0:T(8,128)(2,1)}, f32[2,256,5120]{2,1,0:T(8,128)}) fusion(f32[512]{0:T(512)S(1)} %bitcast.150, bf16[2,256,5120]{2,1,0:T(8,128)(2,1)} %param.16), kind=kLoop, calls=%fused_computation.4 | loop fusion | flops 7864320 | bytes 20973568 | tf_op jit(solution)/shard_map/convert_element_type | solution.py:38
  37.0 5.9 %all-gather.7.cloned.1.call-done = bf16[5120,256]{1,0:T(8,128)(2,1)} async-done(((bf16[640,256]{1,0:T(8,128)(2,1)}), bf16[5120,256]{1,0:T(8,128)(2,1)}) %all-gather.7.cloned.1.call-update) | async-done | bytes 2621456 | tf_op jit(solution)/shard_map/all_gather | solution.py:41
  42.8 4.8 convolution_convert_fusion.3
  47.7 27.1 %all-gather.5.cloned.1.call-done = bf16[5120,256]{1,0:T(8,128)(2,1)} async-done(((bf16[640,256]{1,0:T(8,128)(2,1)}), bf16[5120,256]{1,0:T(8,128)(2,1)}) %all-gather.5.cloned.1.call-update) | async-done | bytes 2621456 | tf_op jit(solution)/shard_map/all_gather | solution.py:42
  74.8 4.8 convolution_convert_fusion.4
  79.8 1.7 gather_fusion.1
  81.5 1.7 gather_fusion.2
  83.1 2.3 bitcast_reduce_fusion
  88.3 1.9 fusion.6
  91.5 1.6 fusion.29
  94.5 1.9 reshape.201
  97.6 1.5 fusion.23
  99.9 1.4 fusion.25
  102.3 1.4 convolution_bitcast_fusion.2
  103.7 1.4 convolution_bitcast_fusion.1
  105.2 2.1 convolution_bitcast_fusion
  107.2 2.1 fusion.73
  109.4 30.6 %all-gather.9.cloned.1.call-done = bf16[5120,1024]{1,0:T(8,128)(2,1)} async-done(((bf16[640,1024]{1,0:T(8,128)(2,1)}), bf16[5120,1024]{1,0:T(8,128)(2,1)}) %all-gather.9.cloned.1.call-update) | async-done | bytes 10485776 | tf_op jit(solution)/shard_map/all_gather | solution.py:40
  140.0 9.8 %convolution_convert_fusion = bf16[512,1024]{1,0:T(8,128)(2,1)S(1)} fusion(bf16[512,5120]{1,0:T(8,128)(2,1)} %get-tuple-element.22, bf16[5120,1024]{1,0:T(8,128)(2,1)} %all-gather.9.cloned.1.call-done), kind=kOutput, calls=%fused_computation.28 | convolution fusion | flops 5369233408 | bytes 16777216 | tf_op jit(solution)/shard_map/dot_general | solution.py:45
  151.5 1.5 fusion.70
  155.1 49.8 %all-gather.11.cloned.1.call-done = bf16[1024,5120]{1,0:T(8,128)(2,1)} async-done(((bf16[1024,640]{1,0:T(8,128)(2,1)}), bf16[1024,5120]{1,0:T(8,128)(2,1)}) %all-gather.11.cloned.1.call-update) | async-done | bytes 10485776 | tf_op jit(solution)/shard_map/all_gather | solution.py:70
  204.9 12.1 %fusion.72 = f32[512,5120]{1,0:T(8,128)} fusion(bf16[512,1024]{1,0:T(8,128)(2,1)S(1)} %reshape.193, bf16[1024,5120]{1,0:T(8,128)(2,1)} %all-gather.11.cloned.1.call-done), kind=kOutput, calls=%fused_computation.112 | convolution fusion | flops 5368709120 | bytes 22020096 | tf_op jit(solution)/shard_map/dot_general | solution.py:69
  217.1 96.7 %all-reduce.3.cloned.1.call-done = (f32[1024,512]{0,1:T(8,128)}, f32[1024,256]{0,1:T(8,128)}, f32[1024,256]{0,1:T(8,128)}, f32[512,1024]{1,0:T(8,128)}) async-done(((f32[1024,512]{0,1:T(8,128)}, f32[1024,256]{0,1:T(8,128)}, f32[1024,256]{0,1:T(8,128)}, f32[512,1024]{1,0:T(8,128)}), (f32[1024,512]{0,1:T(8,128)}, f32[1024,256]{0,1:T(8,128)}, f32[1024,256]{0,1:T(8,128)}, ...) | async-done | bytes 6291472 | tf_op jit(solution)/shard_map/psum | solution.py:168
  313.8 3.0 copy.63
  319.4 174.9 %reduce-scatter.2.cloned.1.call-done = f32[512,1280]{1,0:T(8,128)} async-done(((f32[512,5120]{1,0:T(8,128)}), f32[512,1280]{1,0:T(8,128)}) %reduce-scatter.2.cloned.1.call-update) | async-done | bytes 2621456 | tf_op jit(solution)/shard_map/reduce_scatter | solution.py:72
  494.2 4.0 add_convert_fusion
  498.2 1.3 copy.144
  (109 shorter events, 24.9 us)
Async XLA Ops:
  7.2 7.2 %copy-start = (bf16[1024,512]{1,0:T(8,128)(2,1)S(1)}, bf16[1024,512]{1,0:T(8,128)(2,1)}, u32[]{:S(2)}) copy-start(bf16[1024,512]{1,0:T(8,128)(2,1)} %param.25) | copy-start | bytes 3145732
  7.2 35.6 %all-gather.7.cloned.1.call-start = ((), (), s32[]{:S(2)}) async-start(), calls=%async_computation.2 | async-start | bytes 2949120 | tf_op jit(solution)/shard_map/all_gather | solution.py:41
  7.9 66.9 %all-gather.5.cloned.1.call-start = ((), (), s32[]{:S(2)}) async-start(), calls=%async_computation.1 | async-start | bytes 2949120 | tf_op jit(solution)/shard_map/all_gather | solution.py:42
  8.7 131.4 %all-gather.9.cloned.1.call-start = ((), (), s32[]{:S(2)}) async-start(), calls=%async_computation.3 | async-start | bytes 11796480 | tf_op jit(solution)/shard_map/all_gather | solution.py:40
  9.4 195.5 %all-gather.11.cloned.1.call-start = ((), (), s32[]{:S(2)}) async-start(), calls=%async_computation.4 | async-start | bytes 11796480 | tf_op jit(solution)/shard_map/all_gather | solution.py:70
  10.0 3.7 copy-start.16
  10.0 303.8 %all-reduce.3.cloned.1.call-start = ((), (), s32[]{:S(2)}) async-start(), calls=%async_computation.6 | async-start | bytes 12582912 | tf_op jit(solution)/shard_map/psum | solution.py:168
  14.4 3.9 copy-start.17
  18.4 7.7 %copy-start.5 = (bf16[8,50,2,128]{3,2,1,0:T(2,128)(2,1)}, bf16[8,50,2,128]{3,2,1,0:T(2,128)(2,1)S(1)}, u32[]{:S(2)}) copy-start(bf16[8,50,2,128]{3,2,1,0:T(2,128)(2,1)S(1)} %reshape.197) | copy-start | bytes 614404
  19.1 4.5 copy-start.3
  19.1 5.3 %copy-start.24 = (s32[8]{0:T(128)S(1)}, s32[8]{0:T(128)}, u32[]{:S(2)}) copy-start(s32[8]{0:T(128)} %param.19) | copy-start | bytes 100
  19.1 5.3 %copy-start.2 = (s32[2]{0:T(128)S(1)}, s32[2]{0:T(128)}, u32[]{:S(2)}) copy-start(s32[2]{0:T(128)} %param.17) | copy-start | bytes 28
  21.3 3.8 copy-start.25
  85.4 5.2 %copy-start.8 = (f32[8,2,256,50,2]{2,3,4,1,0:T(8,128)}, f32[8,2,256,50,2]{2,3,4,1,0:T(8,128)S(1)}, u32[]{:S(2)}) copy-start(f32[8,2,256,50,2]{2,3,4,1,0:T(8,128)S(1)} %get-tuple-element.27) | copy-start | bytes 4915204
  85.5 1.3 copy-start.20
  85.5 1.6 copy-start.21
  87.1 1.2 copy-start.11
  90.3 1.2 copy-start.13
  91.5 1.6 copy-start.6
  97.6 2.3 copy-start.9
  97.6 2.3 copy-start.12
  99.9 1.4 copy-start.22
  101.4 0.9 copy-start.18
  101.8 2.0 copy-start.19
  102.3 2.9 copy-start.10
  105.2 2.1 copy-start.4
  109.4 384.9 %reduce-scatter.2.cloned.1.call-start = ((), (), s32[]{:S(2)}) async-start(), calls=%async_computation.5 | async-start | bytes 13107200 | tf_op jit(solution)/shard_map/reduce_scatter | solution.py:72
  150.6 0.9 copy-start.23
  313.8 3.0 copy-start.15
  316.7 1.3 copy-start.14
  494.2 4.0 copy-start.7
  498.2 2.0 copy-start.1
Sparse Core Ops, SparseCore 0:
  9.9 32.8 all-gather.6
  44.7 30.1 all-gather.4
  76.7 63.2 all-gather.8
  141.8 63.1 all-gather.10
  209.0 104.7 all-reduce.2
  316.1 178.0 reduce-scatter.1
where the time goes:
time: 508 us; the launch traced here: 507 us
  waiting for transfers between devices  388 us (76%)
  matrix products  57.2 us (11%)
  local copies, waits for them, and re-layouts  25.6 us (5%)
  other arithmetic  21.8 us (4%)
  between operations  14.6 us (3%)
    reduce_scatter x1, waiting for transfers between devices, body(): lax.psum_scatter(partial_out, 'tensor', scatter_dimension=1, tiled=True)  175 us
    psum x1, waiting for transfers between devices, body(): lax.psum((grad_query_local, grad_key_local, grad_value_local, grad_out_lo...  96.7 us
    all_gather x1, waiting for transfers between devices, body(): lax.all_gather(bb_wo, 'dp', axis=1, tiled=True)  49.8 us
    all_gather x1, waiting for transfers between devices, body(): lax.all_gather(bb_wq, 'dp', axis=0, tiled=True)  30.6 us
    all_gather x1, waiting for transfers between devices, body(): lax.all_gather(bb_wv, 'dp', axis=0, tiled=True)  27.1 us
    dot_general x3, matrix products, body(): jnp.dot(normed, piece, preferred_element_type=jnp.float32)  19.5 us
    dot_general x1, matrix products, body(): jnp.dot(context, lax.all_gather(bb_wo, 'dp', axis=1, tiled=True), preferr...  12.1 us
    unnamed x59, local copies, waits for them, and re-layouts  10.8 us
  transfers between devices with their start and end apart: 6, of which 6 were waited for; matrix products, arithmetic and copies ran while one was open for 19% of the time, Pallas kernels for 0%

commit v1 on v0

--- a/solution.py
+++ b/solution.py
@@ -1,15 +1,18 @@
+import functools
 import math
 
 import jax
 import jax.numpy as jnp
 from jax import lax
+from jax.experimental import pallas as pl
+from jax.experimental.pallas import tpu as pltpu
 from jax.sharding import PartitionSpec as P
 
 HD = 128
 STEPS = 50
 
 
-def body(
+def general_body(
     prefix_tokens,
     prefix_len,
     causal_start,
@@ -171,6 +174,593 @@
     return (prefix_out, grad_wq, grad_wk, grad_wv, grad_wo)
 
 
+NEG = -1e30
+PAD = 64
+HIGH = 56 * 1024 * 1024
+
+
+def params():
+    return pltpu.CompilerParams(vmem_limit_bytes=HIGH)
+
+
+def cost(flops, moved):
+    return pl.CostEstimate(flops=int(flops), bytes_accessed=int(moved), transcendentals=0)
+
+
+def whole():
+    return pl.BlockSpec(memory_space=pltpu.VMEM)
+
+
+def nt(a, b):
+    return lax.dot_general(a, b, (((1,), (1,)), ((), ())), preferred_element_type=jnp.float32)
+
+
+def tn(a, b):
+    return lax.dot_general(a, b, (((0,), (0,)), ((), ())), preferred_element_type=jnp.float32)
+
+
+def nn(a, b):
+    return jnp.dot(a, b, preferred_element_type=jnp.float32)
+
+
+def norm_kernel(meta, x_ref, out_ref):
+    chip = meta[0]
+    parts, rows, wide = out_ref.shape
+    x = x_ref[...].astype(jnp.float32)
+    scale = lax.rsqrt(jnp.mean(x * x, axis=-1, keepdims=True) + 1e-06)
+    for j in range(parts):
+        at = pl.multiple_of((chip ^ j) * wide, wide)
+        piece = x_ref[:, pl.ds(at, wide)].astype(jnp.float32)
+        out_ref[j] = (piece * scale).astype(jnp.bfloat16)
+
+
+def normalise(meta, flat, parts):
+    count, width = flat.shape
+    block = 128
+    return pl.pallas_call(
+        norm_kernel,
+        grid_spec=pltpu.PrefetchScalarGridSpec(
+            num_scalar_prefetch=1,
+            grid=(count // block,),
+            in_specs=[pl.BlockSpec((block, width), lambda i, m: (i, 0))],
+            out_specs=pl.BlockSpec((parts, block, width // parts), lambda i, m: (0, i, 0)),
+        ),
+        out_shape=jax.ShapeDtypeStruct((parts, count, width // parts), jnp.bfloat16),
+        compiler_params=params(),
+        cost_estimate=cost(4 * count * width, 4 * count * width),
+        name="normalise",
+    )(meta, flat)
+
+
+def product(x, weights):
+    w0, w1, w2, wx, wy = weights
+    half = wx.shape[0]
+    total = nn(x(0), w0[...])
+    total += nn(x(1), w1[...])
+    total += nn(x(2), w2[...])
+    last = x(3)
+    total += nn(last[:, :half], wx[...])
+    total += nn(last[:, half:], wy[...])
+    return total
+
+
+def kv_kernel(own_ref, sib_ref, w0, w1, w2, wx, wy, out_ref):
+    step = pl.program_id(0)
+    half = pl.num_programs(0) // 2
+    weights = (w0, w1, w2, wx, wy)
+
+    @pl.when(step < half)
+    def _():
+        out_ref[...] = product(lambda j: own_ref[j], weights).astype(jnp.bfloat16)
+
+    @pl.when(step >= half)
+    def _():
+        out_ref[...] = product(lambda j: sib_ref[j], weights).astype(jnp.bfloat16)
+
+
+def pair_specs(parts, block, wide, steps):
+    own = pl.BlockSpec(
+        (parts, block, wide), lambda i, *m: (0, jnp.minimum(i, steps // 2 - 1), 0)
+    )
+    sib = pl.BlockSpec((parts, block, wide), lambda i, *m: (0, jnp.maximum(i - steps // 2, 0), 0))
+    return [own, sib]
+
+
+def project_kv(own, sib, weights):
+    parts, count, wide = own.shape
+    columns = weights[0].shape[1]
+    block = 256
+    steps = 2 * count // block
+    return pl.pallas_call(
+        kv_kernel,
+        grid=(steps,),
+        in_specs=pair_specs(parts, block, wide, steps) + [whole()] * 5,
+        out_specs=pl.BlockSpec((block, columns), lambda i: (i, 0)),
+        out_shape=jax.ShapeDtypeStruct((2 * count, columns), jnp.bfloat16),
+        compiler_params=params(),
+        cost_estimate=cost(4 * count * parts * wide * columns, 4 * count * parts * wide),
+        name="project_kv",
+    )(own, sib, *weights)
+
+
+def attend_kernel(factor, meta, own_ref, sib_ref, w0, w1, w2, wx, wy, kv_ref, out_ref, query):
+    step = pl.program_id(0)
+    half = pl.num_programs(0) // 2
+    weights = (w0, w1, w2, wx, wy)
+
+    @pl.when(step < half)
+    def _():
+        query[...] = product(lambda j: own_ref[j], weights).astype(jnp.bfloat16)
+
+    @pl.when(step >= half)
+    def _():
+        query[...] = product(lambda j: sib_ref[j], weights).astype(jnp.bfloat16)
+
+    length = meta[4 + step]
+    start = meta[8 + step]
+    positions = out_ref.shape[0]
+    keys = kv_ref[:, :HD]
+    values = kv_ref[:, HD:]
+    row = lax.broadcasted_iota(jnp.int32, (positions, positions), 0)
+    column = lax.broadcasted_iota(jnp.int32, (positions, positions), 1)
+    visible = (column < length) & ((column < start) | (column <= row))
+    for head in range(out_ref.shape[1] // HD):
+        at = slice(head * HD, (head + 1) * HD)
+        scores = jnp.where(visible, nt(query[:, at], keys) * factor, NEG)
+        top = jnp.max(scores, axis=-1, keepdims=True)
+        weight = jnp.where(visible, jnp.exp(scores - top), 0.0)
+        weight = (weight / jnp.sum(weight, axis=-1, keepdims=True)).astype(jnp.bfloat16)
+        out_ref[:, at] = nn(weight, values).astype(jnp.bfloat16)
+
+
+def attend(meta, own, sib, weights, kv, positions, factor):
+    parts, count, wide = own.shape
+    columns = weights[0].shape[1]
+    steps = 2 * count // positions
+    return pl.pallas_call(
+        functools.partial(attend_kernel, factor),
+        grid_spec=pltpu.PrefetchScalarGridSpec(
+            num_scalar_prefetch=1,
+            grid=(steps,),
+            in_specs=pair_specs(parts, positions, wide, steps)
+            + [whole()] * 5
+            + [pl.BlockSpec((positions, 2 * HD), lambda i, m: (i, 0))],
+            out_specs=pl.BlockSpec((positions, columns), lambda i, m: (i, 0)),
+            scratch_shapes=[pltpu.VMEM((positions, columns), jnp.bfloat16)],
+        ),
+        out_shape=jax.ShapeDtypeStruct((2 * count, columns), jnp.bfloat16),
+        compiler_params=params(),
+        cost_estimate=cost(8 * count * parts * wide * columns, 4 * count * parts * wide),
+        name="attend",
+    )(meta, own, sib, *weights, kv)
+
+
+def expert_project_kernel(meta, own_ref, sib_ref, wq, wk, wv, wo, out_ref, cot_ref):
+    step = pl.program_id(0)
+    half = pl.num_programs(0) // 2
+
+    def run(ref):
+        action = ref[0]
+        q, k = wq.shape[1], wk.shape[1]
+        out_ref[:, :q] = nn(action, wq[...]).astype(jnp.bfloat16)
+        out_ref[:, q : q + k] = nn(action, wk[...]).astype(jnp.bfloat16)
+        out_ref[:, q + k :] = nn(action, wv[...]).astype(jnp.bfloat16)
+        cot_ref[...] = nt(ref[1], wo[...]).astype(jnp.bfloat16)
+
+    @pl.when(step < half)
+    def _():
+        run(own_ref)
+
+    @pl.when(step >= half)
+    def _():
+        run(sib_ref)
+
+
+def expert_project(meta, own, sib, wq, wk, wv, wo):
+    _, rows, width = own.shape
+    block = 256
+    steps = 2 * rows // block
+    q, k = wq.shape[1] // 2, wk.shape[1] // 2
+    return pl.pallas_call(
+        expert_project_kernel,
+        grid_spec=pltpu.PrefetchScalarGridSpec(
+            num_scalar_prefetch=1,
+            grid=(steps,),
+            in_specs=pair_specs(2, block, width, steps)
+            + [
+                pl.BlockSpec((width, q), lambda i, m: (0, m[1])),
+                pl.BlockSpec((width, k), lambda i, m: (0, m[1])),
+                pl.BlockSpec((width, k), lambda i, m: (0, m[1])),
+                pl.BlockSpec((q, width), lambda i, m: (m[1], 0)),
+            ],
+            out_specs=[
+                pl.BlockSpec((block, q + 2 * k), lambda i, m: (i, 0)),
+                pl.BlockSpec((block, q), lambda i, m: (i, 0)),
+            ],
+        ),
+        out_shape=[
+            jax.ShapeDtypeStruct((2 * rows, q + 2 * k), jnp.bfloat16),
+            jax.ShapeDtypeStruct((2 * rows, q), jnp.bfloat16),
+        ],
+        compiler_params=params(),
+        cost_estimate=cost(4 * rows * width * (2 * q + 2 * k), 8 * rows * width),
+        name="expert_project",
+    )(meta, own, sib, wq, wk, wv, wo)
+
+
+def expert_kernel(factor, spans, meta, proj_ref, dctx_ref, kv_ref, ctx_ref, grad_ref):
+    step = pl.program_id(0)
+    positions = meta.shape[0] and 256
+    width = dctx_ref.shape[1]
+    heads = width // HD
+    rows = heads * PAD
+    own_column = lax.broadcasted_iota(jnp.int32, (rows, PAD), 1)
+    pre_column = lax.broadcasted_iota(jnp.int32, (rows, positions), 1)
+    for s in range(spans):
+        sample = meta[12 + step * spans + s]
+        valid = pre_column < meta[4 + sample]
+        own_valid = own_column < STEPS
+        at = slice(s * PAD, (s + 1) * PAD)
+        base = pl.multiple_of(sample * positions, positions)
+        pre_keys = kv_ref[pl.ds(base, positions), :HD]
+        pre_values = kv_ref[pl.ds(base, positions), HD:]
+        stack = lambda ref: jnp.concatenate(
+            [ref[at, h * HD : (h + 1) * HD] for h in range(heads)], axis=0
+        )
+        query = stack(proj_ref)
+        cot = stack(dctx_ref)
+        own_keys = proj_ref[at, width : width + HD]
+        own_values = proj_ref[at, width + HD :]
+        score_pre = jnp.where(valid, nt(query, pre_keys) * factor, NEG)
+        score_own = jnp.where(own_valid, nt(query, own_keys) * factor, NEG)
+        peak = jnp.maximum(
+            jnp.max(score_pre, axis=-1, keepdims=True), jnp.max(score_own, axis=-1, keepdims=True)
+        )
+        exp_pre = jnp.where(valid, jnp.exp(score_pre - peak), 0.0)
+        exp_own = jnp.where(own_valid, jnp.exp(score_own - peak), 0.0)
+        total = jnp.sum(exp_pre, axis=-1, keepdims=True) + jnp.sum(exp_own, axis=-1, keepdims=True)
+        prob_pre = exp_pre / total
+        prob_own = exp_own / total
+        half_pre = prob_pre.astype(jnp.bfloat16)
+        half_own = prob_own.astype(jnp.bfloat16)
+        context = (nn(half_pre, pre_values) + nn(half_own, own_values)).astype(jnp.bfloat16)
+        dprob_pre = nt(cot, pre_values)
+        dprob_own = nt(cot, own_values)
+        delta = jnp.sum(prob_pre * dprob_pre, axis=-1, keepdims=True) + jnp.sum(
+            prob_own * dprob_own, axis=-1, keepdims=True
+        )
+        dscore_pre = (prob_pre * (dprob_pre - delta) * factor).astype(jnp.bfloat16)
+        dscore_own = (prob_own * (dprob_own - delta) * factor).astype(jnp.bfloat16)
+        dquery = (nn(dscore_pre, pre_keys) + nn(dscore_own, own_keys)).astype(jnp.bfloat16)
+        for h in range(heads):
+            part = slice(h * PAD, (h + 1) * PAD)
+            ctx_ref[at, h * HD : (h + 1) * HD] = context[part]
+            grad_ref[at, h * HD : (h + 1) * HD] = dquery[part]
+        grad_ref[at, width : width + HD] = tn(dscore_own, query).astype(jnp.bfloat16)
+        grad_ref[at, width + HD :] = tn(half_own, cot).astype(jnp.bfloat16)
+
+
+def expert_attend(meta, proj, dctx, kv, factor):
+    rows, columns = proj.shape
+    width = dctx.shape[1]
+    spans = 4
+    steps = rows // (PAD * spans)
+    block = PAD * spans
+    return pl.pallas_call(
+        functools.partial(expert_kernel, factor, spans),
+        grid_spec=pltpu.PrefetchScalarGridSpec(
+            num_scalar_prefetch=1,
+            grid=(steps,),
+            in_specs=[
+                pl.BlockSpec((block, columns), lambda i, m: (i, 0)),
+                pl.BlockSpec((block, width), lambda i, m: (i, 0)),
+                whole(),
+            ],
+            out_specs=[
+                pl.BlockSpec((block, width), lambda i, m: (i, 0)),
+                pl.BlockSpec((block, columns), lambda i, m: (i, 0)),
+            ],
+        ),
+        out_shape=[
+            jax.ShapeDtypeStruct((rows, width), jnp.bfloat16),
+            jax.ShapeDtypeStruct((rows, columns), jnp.bfloat16),
+        ],
+        compiler_params=params(),
+        cost_estimate=cost(40 * rows * 320 * width, 8 * rows * columns),
+        name="expert_attend",
+    )(meta, proj, dctx, kv)
+
+
+def grads_kernel(meta, own_ref, sib_ref, ctx_ref, grad_ref, ax_ref, ak_ref, by_ref, bk_ref):
+    chip = meta[0]
+    step = pl.program_id(0)
+    rows = own_ref.shape[1]
+    tall = ax_ref.shape[1]
+    wide = grad_ref.shape[1]
+    heads = ctx_ref.shape[1] // HD
+
+    def piece(route, j, ref):
+        at = pl.ds(pl.multiple_of((route * 4 + (chip ^ j)) * tall, tall), tall)
+        ref[0, :, :wide] = tn(own_ref[0, :, at], grad_ref[:rows]) + tn(
+            sib_ref[0, :, at], grad_ref[rows:]
+        )
+        for h in range(heads):
+            cut = slice(h * HD, (h + 1) * HD)
+            ref[0, :, wide + h * tall : wide + (h + 1) * tall] = tn(
+                ctx_ref[:rows, cut], own_ref[1, :, at]
+            ) + tn(ctx_ref[rows:, cut], sib_ref[1, :, at])
+
+    piece(0, 1 + 2 * step, ax_ref)
+    piece(1, 2 + step, by_ref)
+    piece(0, 2 * step, ak_ref)
+    piece(1, step, bk_ref)
+
+
+def weight_grads(meta, own, sib, ctx, grad):
+    _, rows, width = own.shape
+    tall = width // 8
+    columns = grad.shape[1] + ctx.shape[1] // HD * tall
+    out = jax.ShapeDtypeStruct((2, tall, columns), jnp.float32)
+    return pl.pallas_call(
+        grads_kernel,
+        grid_spec=pltpu.PrefetchScalarGridSpec(
+            num_scalar_prefetch=1,
+            grid=(2,),
+            in_specs=[whole()] * 4,
+            out_specs=[pl.BlockSpec((1, tall, columns), lambda i, m: (i, 0, 0))] * 4,
+        ),
+        out_shape=[out] * 4,
+        compiler_params=params(),
+        cost_estimate=cost(4 * rows * width * columns, 16 * width * columns),
+        name="weight_grads",
+    )(meta, own, sib, ctx, grad)
+
+
+def place_kernel(meta, *refs):
+    own, sib, outs = refs[:5], refs[5:10], refs[10:]
+    step = pl.program_id(0)
+    first = meta[1] == 0
+    wq, wk, wv, wo = outs
+    tall = wq.shape[0]
+    q, k = wq.shape[1] // 2, wk.shape[1] // 2
+    heads = wo.shape[0] // (2 * HD)
+
+    def pick(group, route, j):
+        if j < 3:
+            return group[j][route]
+        return group[3 + route][...]
+
+    for route in range(2):
+        for j in range(4):
+
+            @pl.when(step == route * 4 + j)
+            def _():
+                mine, other = pick(own, route, j), pick(sib, route, j)
+                for side, block in enumerate(
+                    (jnp.where(first, mine, other), jnp.where(first, other, mine))
+                ):
+                    wq[:, side * q : (side + 1) * q] = block[:, :q]
+                    wk[:, side * k : (side + 1) * k] = block[:, q : q + k]
+                    wv[:, side * k : (side + 1) * k] = block[:, q + k : q + 2 * k]
+                    for h in range(heads):
+                        row = (side * heads + h) * HD
+                        cut = q + 2 * k + h * tall
+                        wo[row : row + HD] = block[:, cut : cut + tall]
+
+
+def place_grads(meta, own, sib, shapes):
+    tall = own[0].shape[1]
+
+    def spot(i, m):
+        return (i // 4) * 4 + (m[0] ^ (i % 4))
+
+    rows = lambda s: pl.BlockSpec((tall, s[1]), lambda i, m: (spot(i, m), 0))
+    specs = [rows(s) for s in shapes[:3]]
+    specs.append(pl.BlockSpec((shapes[3][0], tall), lambda i, m: (0, spot(i, m))))
+    return pl.pallas_call(
+        place_kernel,
+        grid_spec=pltpu.PrefetchScalarGridSpec(
+            num_scalar_prefetch=1,
+            grid=(8,),
+            in_specs=[whole()] * 10,
+            out_specs=specs,
+        ),
+        out_shape=[jax.ShapeDtypeStruct(s, jnp.float32) for s in shapes],
+        compiler_params=params(),
+        cost_estimate=cost(0, 2 * 4 * sum(s[0] * s[1] for s in shapes)),
+        name="place_grads",
+    )(meta, *own, *sib)
+
+
+def output_kernel(meta, tok_ref, mid, u1, u2, u3, d1, d2, d3, *refs):
+    wos, out_ref, ctx = refs[:10], refs[10], refs[11]
+    chip, plane = meta[0], meta[2]
+    step = pl.program_id(0)
+    quarter = wos[0].shape[1]
+
+    @pl.when(step == 0)
+    def _():
+        ctx[plane] = mid[...]
+        for k, (up, down) in enumerate(((u1, d1), (u2, d2), (u3, d3)), 1):
+
+            @pl.when(plane >= k)
+            def _():
+                ctx[plane - k] = up[...]
+
+            @pl.when(plane + k <= 3)
+            def _():
+                ctx[plane + k] = down[...]
+
+    def run(group):
+        total = tok_ref[...].astype(jnp.float32)
+        for j in range(4):
+            column = pl.multiple_of((chip ^ j) * quarter, quarter)
+            for r in range(4):
+                source = (chip ^ j) ^ plane ^ r
+                if j < 3:
+                    weight = group[j][r]
+                else:
+                    weight = group[3 + r // 2][r % 2]
+                total += nn(ctx[source, :, pl.ds(column, quarter)], weight)
+        out_ref[...] = total.astype(jnp.bfloat16)
+
+    @pl.when(step == 0)
+    def _():
+        run(wos[:5])
+
+    @pl.when(step == 1)
+    def _():
+        run(wos[5:])
+
+
+def output(meta, flat, contexts, own, sib):
+    count = flat.shape[0]
+    half = own[0].shape[2]
+    wide = contexts[0].shape[1]
+    return pl.pallas_call(
+        output_kernel,
+        grid_spec=pltpu.PrefetchScalarGridSpec(
+            num_scalar_prefetch=1,
+            grid=(2,),
+            in_specs=[pl.BlockSpec((count, half), lambda i, m: (0, 2 * m[2] + (m[1] ^ i)))]
+            + [whole()] * 17,
+            out_specs=pl.BlockSpec((count, half), lambda i, m: (0, m[1] ^ i)),
+            scratch_shapes=[pltpu.VMEM((4, count, wide), jnp.bfloat16)],
+        ),
+        out_shape=jax.ShapeDtypeStruct((count, 2 * half), jnp.bfloat16),
+        compiler_params=params(),
+        cost_estimate=cost(16 * count * wide * half, 32 * wide * half),
+        name="output",
+    )(meta, flat, *contexts, *own, *sib)
+
+
+def plane_body(
+    prefix_tokens,
+    prefix_len,
+    causal_start,
+    span_sample,
+    bb_wq,
+    bb_wk,
+    bb_wv,
+    bb_wo,
+    action_tokens,
+    ex_wq,
+    ex_wk,
+    ex_wv,
+    ex_wo,
+    action_cot,
+):
+    samples, positions, width = prefix_tokens.shape
+    factor = 1.0 / math.sqrt(HD)
+    count = samples * positions
+    flat = prefix_tokens.reshape(count, width)
+    device = lax.axis_index("dp")
+    chip, core = device // 2, device % 2
+    plane = lax.axis_index("tensor")
+
+    def across(mask):
+        return lambda x: lax.ppermute(x, "dp", [(i, i ^ mask) for i in range(8)])
+
+    swap, over_x, over_y = across(1), across(2), across(4)
+
+    def spread(x):
+        from_x, from_y = over_x(x), over_y(x)
+        half = x.shape[0] // 2
+        return x, from_x, from_y, over_x(from_y[:half]), over_y(from_x[half:])
+
+    local = jnp.concatenate([prefix_len, causal_start, span_sample])
+    remote = swap(local)
+    meta = jnp.concatenate(
+        [
+            jnp.stack([chip, core, plane, 0]).astype(jnp.int32),
+            local[:2],
+            remote[:2],
+            local[2:4],
+            remote[2:4],
+            local[4:],
+            remote[4:] + samples,
+        ]
+    )
+    chip_meta = jnp.stack([chip, core, plane, 0]).astype(jnp.int32)
+
+    def halves(weight):
+        size = weight.shape[1] // 2
+        mine = lax.dynamic_slice_in_dim(weight, core * size, size, 1)
+        other = lax.dynamic_slice_in_dim(weight, (1 - core) * size, size, 1)
+        return mine, other
+
+    def joined(mine, got):
+        return jnp.where(
+            core == 0, jnp.concatenate([mine, got]), jnp.concatenate([got, mine])
+        )
+
+    k_mine, k_other = halves(bb_wk)
+    v_mine, v_other = halves(bb_wv)
+    kv_got = swap(jnp.concatenate([k_other, v_other], axis=1))
+    kv_shard = joined(jnp.concatenate([k_mine, v_mine], axis=1), kv_got)
+    q_mine, q_other = halves(bb_wq)
+    q_shard = joined(q_mine, swap(q_other))
+    kv_weights = spread(kv_shard)
+    q_weights = spread(q_shard)
+
+    normed = normalise(chip_meta, flat, 4)
+    normed_sib = swap(normed)
+
+    spans = action_tokens.shape[0]
+    pad = ((0, 0), (0, PAD - STEPS), (0, 0))
+    pair = jnp.stack([jnp.pad(action_tokens, pad), jnp.pad(action_cot, pad)])
+    pair = pair.reshape(2, spans * PAD, action_tokens.shape[2])
+    pair_sib = swap(pair)
+    proj, dctx = expert_project(chip_meta, pair, pair_sib, ex_wq, ex_wk, ex_wv, ex_wo)
+
+    kv = project_kv(normed, normed_sib, kv_weights)
+    ectx, egrad = expert_attend(meta, proj, dctx, kv, factor)
+    ax, ak, by, bk = weight_grads(chip_meta, pair, pair_sib, ectx, egrad)
+    a_sum = ak + over_x(ax)
+    b_sum = bk + over_y(by)
+    mine = jnp.stack([a_sum[0] + over_y(a_sum[1]), b_sum[0] + over_x(b_sum[1])])
+    from_x, from_y = over_x(mine), over_y(mine)
+    full = (mine, from_x, from_y, over_x(from_y[0]), over_y(from_x[1]))
+    full_sib = tuple(swap(x) for x in full)
+    shapes = (ex_wq.shape, ex_wk.shape, ex_wv.shape, ex_wo.shape)
+    grads = place_grads(chip_meta, full, full_sib, shapes)
+
+    quarter = bb_wo.shape[0] // 4
+    got = []
+    for r in range(4):
+        to = chip ^ plane ^ r
+        perm = [
+            (((a * 2 + k) * 4 + z), (((a ^ z ^ r) * 2 + k) * 4 + a))
+            for a in range(4)
+            for k in range(2)
+            for z in range(4)
+        ]
+        piece = lax.dynamic_slice_in_dim(bb_wo, to * quarter, quarter, 0)
+        got.append(lax.ppermute(piece, ("dp", "tensor"), perm))
+    wo_own = spread(jnp.stack(got))
+    wo_sib = tuple(swap(x) for x in wo_own)
+
+    ctx = attend(meta, normed, normed_sib, q_weights, kv, positions, factor)
+    ctx_own, ctx_other = ctx[:count], ctx[count:]
+    ctx_got = swap(ctx_other)
+    ctx_rows = jnp.where(
+        core == 0,
+        jnp.concatenate([ctx_own, ctx_got], axis=1),
+        jnp.concatenate([ctx_got, ctx_own], axis=1),
+    )
+    up = lambda x: lax.ppermute(x, "tensor", [(0, 1), (1, 2), (2, 3)])
+    down = lambda x: lax.ppermute(x, "tensor", [(3, 2), (2, 1), (1, 0)])
+    u1, d1 = up(ctx_rows), down(ctx_rows)
+    u2, d2 = up(u1), down(d1)
+    u3, d3 = up(u2), down(d2)
+    out = output(chip_meta, flat, (ctx_rows, u1, u2, u3, d1, d2, d3), wo_own, wo_sib)
+    return (out.reshape(samples, positions, -1), *grads)
+
+
+def fits_plane(mesh):
+    return mesh.shape["dp"] == 8 and mesh.shape["tensor"] == 4
+
+
 def solution(mesh):
     in_specs = (
         P("dp", None, None),
@@ -195,4 +785,5 @@
         P(None, "tensor"),
         P("tensor", None),
     )
+    body = plane_body if fits_plane(mesh) else general_body
     return jax.shard_map(body, mesh=mesh, in_specs=in_specs, out_specs=out_specs, check_vma=False)

time: 508 us -> 325 us (0.64)
  waiting for transfers between devices: 388 us -> 122 us
  starting transfers between devices: 0.23 us -> 97.5 us
  Pallas kernels: 0 us -> 83 us
  matrix products: 57.2 us -> 0 us
  other arithmetic: 21.8 us -> 7.91 us
  between operations: 14.6 us -> 1.36 us
  local copies, waits for them, and re-layouts: 25.6 us -> 12.5 us
    reduce_scatter x1 -> x0, waiting for transfers between devices: 175 us -> none  [body(): lax.psum_scatter(partial_out, 'tensor', scatter_dimension=1, tiled=True)]
    ppermute x0 -> x46, waiting for transfers between devices: none -> 122 us  [the longest x36 58.9 us: across(): return lambda x: lax.ppermute(x, 'dp', [(i, i ^ mask) for i in range(8)])]
    all_gather x4 -> x0, waiting for transfers between devices: 113 us -> none  [the longest x1 49.8 us: body(): lax.all_gather(bb_wo, 'dp', axis=1, tiled=True)]
    ppermute x0 -> x46, starting transfers between devices: none -> 97.5 us  [the longest x36 70.4 us: across(): return lambda x: lax.ppermute(x, 'dp', [(i, i ^ mask) for i in range(8)])]
    psum x1 -> x0, waiting for transfers between devices: 96.7 us -> none  [body(): lax.psum((grad_query_local, grad_key_local, grad_value_local, grad_out_lo...]
    pallas_call x0 -> x8, Pallas kernels: none -> 83 us  [the longest x1 16.5 us: attend(): pl.pallas_call(functools.partial(attend_kernel, factor), grid_spec=pltpu....]
    dot_general x24 -> x0, matrix products: 57.2 us -> none  [the longest x3 19.5 us: body(): jnp.dot(normed, piece, preferred_element_type=jnp.float32)]
    convert_element_type x3 -> x0, other arithmetic: 14.5 us -> none  [the longest x1 10.2 us: body(): normed = (widened * lax.rsqrt(jnp.mean(widened * widened, axis=-1, keepdi...]
  transfers between devices with their start and end apart: 6 -> 46, of which waited for: 6 -> 16; matrix products, arithmetic and copies ran while one was open for 19% -> 6% of each run, Pallas kernels for 0% -> 19%
where the time goes in v1:
time: 325 us; the launch traced here: 324 us
  waiting for transfers between devices  122 us (38%)
  starting transfers between devices  97.5 us (30%)
  Pallas kernels  83 us (26%)
  local copies, waits for them, and re-layouts  12.5 us (4%)
  other arithmetic  7.91 us (2%)
    ppermute x36, starting transfers between devices, across(): return lambda x: lax.ppermute(x, 'dp', [(i, i ^ mask) for i in range(8)])  70.4 us
    ppermute x36, waiting for transfers between devices, across(): return lambda x: lax.ppermute(x, 'dp', [(i, i ^ mask) for i in range(8)])  58.9 us
    ppermute x4, waiting for transfers between devices, plane_body(): got.append(lax.ppermute(piece, ('dp', 'tensor'), perm))  22.6 us
    ppermute x3, waiting for transfers between devices, plane_body(): up = lambda x: lax.ppermute(x, 'tensor', [(0, 1), (1, 2), (2, 3)])  20.4 us
    ppermute x3, waiting for transfers between devices, plane_body(): down = lambda x: lax.ppermute(x, 'tensor', [(3, 2), (2, 1), (1, 0)])  20.2 us
    pallas_call x1, Pallas kernels, attend(): pl.pallas_call(functools.partial(attend_kernel, factor), grid_spec=pltpu....  16.5 us
    pallas_call x1, Pallas kernels, output(): pl.pallas_call(output_kernel, grid_spec=pltpu.PrefetchScalarGridSpec(num_...  15.1 us
    pallas_call x1, Pallas kernels, expert_attend(): pl.pallas_call(functools.partial(expert_kernel, factor, spans), grid_spec...  13.7 us
  transfers between devices with their start and end apart: 46, of which 16 were waited for; matrix products, arithmetic and copies ran while one was open for 6% of the time, Pallas kernels for 19%

profile of v1, /device:TPU:0, one launch (start us, length us, event | category | flops | bytes accessed | tf_op | source)
XLA Modules:
  0.0 324.5 jit_solution(32531137371483253)
XLA Ops:
  1.3 7.4 %normalise.1.own_ref = bf16[4,512,1280]{2,1,0:T(8,128)(2,1)} custom-call(s32[4]{0:T(128)} %pad_add_fusion.meta, bf16[512,5120]{1,0:T(8,128)(2,1)} %bitcast.35), custom_call_target="tpu_custom_call" | custom-call | flops 10485760 | bytes 10485760 | tf_op jit(solution)/shard_map/normalise/pallas_call | solution.py:220
  12.9 5.9 %collective-permute-start.22 = (bf16[256,640]{1,0:T(8,128)(2,1)}, bf16[256,640]{1,0:T(8,128)(2,1)S(1)}, u32[]{:S(2)}, u32[]{:S(2)}) collective-permute-start(bf16[256,640]{1,0:T(8,128)(2,1)} %get-tuple-element.31), channel_id=1, source_target_pairs={{0,24},{1,16},{2,8},{3,0},{4,28},{5,20},{6,12},{7,4},{8,17},{9,25}... | collective-permute-start | bytes 983048 | tf_op jit(solution)/shard_map/ppermute | solution.py:739
  20.2 4.6 %collective-permute-start.21 = (bf16[256,640]{1,0:T(8,128)(2,1)}, bf16[256,640]{1,0:T(8,128)(2,1)S(1)}, u32[]{:S(2)}, u32[]{:S(2)}) collective-permute-start(bf16[256,640]{1,0:T(8,128)(2,1)} %get-tuple-element.32), channel_id=1, source_target_pairs={{0,16},{1,24},{2,0},{3,8},{4,20},{5,28},{6,4},{7,12},{8,25},{9,17}... | collective-permute-start | bytes 983048 | tf_op jit(solution)/shard_map/ppermute | solution.py:739
  26.2 2.7 collective-permute-done.22
  28.8 15.0 %collective-permute-start.8 = (bf16[1280,256]{1,0:T(8,128)(2,1)S(1)}, bf16[1280,256]{1,0:T(8,128)(2,1)S(1)}, u32[]{:S(2)}, u32[]{:S(2)}) collective-permute-start(bf16[1280,256]{1,0:T(8,128)(2,1)S(1)} %maximum_select_fusion.2.w0), channel_id=1, source_target_pairs={{0,8},{4,12},{8,0},{12,4},{16,24},{20,28},{24,16},{28,20},{1,9},{5... | collective-permute-start | bytes 1966088 | tf_op jit(solution)/shard_map/ppermute | solution.py:662
  45.8 2.8 maximum_select_fusion.w0
  49.2 15.0 %collective-permute-start.4 = (bf16[1280,512]{1,0:T(8,128)(2,1)}, bf16[1280,512]{1,0:T(8,128)(2,1)}, u32[]{:S(2)}, u32[]{:S(2)}) collective-permute-start(bf16[1280,512]{1,0:T(8,128)(2,1)} %maximum_select_fusion.w0), channel_id=1, source_target_pairs={{0,16},{4,20},{8,24},{12,28},{16,0},{20,4},{24,8},{28,12},{1,17},{... | collective-permute-start | bytes 3932168 | tf_op jit(solution)/shard_map/ppermute | solution.py:662
  64.2 19.3 %collective-permute-done.20 = bf16[256,640]{1,0:T(8,128)(2,1)} collective-permute-done((bf16[256,640]{1,0:T(8,128)(2,1)S(1)}, bf16[256,640]{1,0:T(8,128)(2,1)}, u32[]{:S(2)}, u32[]{:S(2)}) %collective-permute-start.20) | collective-permute-done | bytes 327712 | tf_op jit(solution)/shard_map/ppermute | solution.py:739
  83.6 26.4 %collective-permute-done.9.w2 = bf16[1280,256]{1,0:T(8,128)(2,1)S(1)} collective-permute-done((bf16[1280,256]{1,0:T(8,128)(2,1)S(1)}, bf16[1280,256]{1,0:T(8,128)(2,1)S(1)}, u32[]{:S(2)}, u32[]{:S(2)}) %collective-permute-start.9) | collective-permute-done | bytes 655392 | tf_op jit(solution)/shard_map/ppermute | solution.py:662
  112.5 22.4 %collective-permute-start.10 = (bf16[640,256]{1,0:T(8,128)(2,1)}, bf16[640,256]{1,0:T(8,128)(2,1)}, u32[]{:S(2)}, u32[]{:S(2)}) collective-permute-start(bf16[640,256]{1,0:T(8,128)(2,1)} %slice.70), channel_id=1, source_target_pairs={{0,8},{4,12},{8,0},{12,4},{16,24},{20,28},{24,16},{28,20},{1,9},{5... | collective-permute-start | bytes 983048 | tf_op jit(solution)/shard_map/ppermute | solution.py:662
  137.2 2.4 slice.68
  139.7 2.0 slice.69
  141.7 2.1 collective-permute-start.24
  143.7 7.0 %expert_project.1 = (bf16[1024,512]{1,0:T(8,128)(2,1)}, bf16[1024,256]{1,0:T(8,128)(2,1)}) custom-call(s32[4]{0:T(128)} %pad_add_fusion.meta, bf16[2,512,1024]{2,1,0:T(8,128)(2,1)} %copy-done, bf16[2,512,1024]{2,1,0:T(8,128)(2,1)} %collective-permute-done.32.sib_ref, bf16[1024,512]{1,0:T(8,128)(2,1)} %wq.1, bf16[1024,256]{1,0:T(8,128)(2,1)} %wk.1, ...), custom_call_target="tpu_custom_call" | custom-call | flops 1610612736 | bytes 4194304 | tf_op jit(solution)/shard_map/expert_project/pallas_call | solution.py:364
  150.9 2.0 collective-permute-start.5
  153.1 8.4 %project_kv.1.kv_ref = bf16[1024,256]{1,0:T(8,128)(2,1)} custom-call(bf16[4,512,1280]{2,1,0:T(8,128)(2,1)} %normalise.1.own_ref, bf16[4,512,1280]{2,1,0:T(8,128)(2,1)} %collective-permute-done.1.sib_ref, bf16[1280,256]{1,0:T(8,128)(2,1)} %copy-done.6, bf16[1280,256]{1,0:T(8,128)(2,1)} %copy-done.9, bf16[1280,256]{1,0:T(8,128)(2,1)} %copy-done.10, ...), custom_call_target="tpu_custom_call" | custom-call | flops 2684354560 | bytes 10485760 | tf_op jit(solution)/shard_map/project_kv/pallas_call | solution.py:274
  161.5 13.7 %expert_attend.1 = (bf16[1024,256]{1,0:T(8,128)(2,1)}, bf16[1024,512]{1,0:T(8,128)(2,1)}) custom-call(s32[28]{0:T(128)} %concatenate.32.meta, bf16[1024,512]{1,0:T(8,128)(2,1)} %get-tuple-element.17.proj_ref, bf16[1024,256]{1,0:T(8,128)(2,1)} %get-tuple-element.18.dctx_ref, bf16[1024,256]{1,0:T(8,128)(2,1)} %project_kv.1.kv_ref), custom_call_target="tpu_custom_call" | custom-call | flops 3355443200 | bytes 4194304 | tf_op jit(solution)/shard_map/expert_attend/pallas_call | solution.py:449
  175.2 7.3 %weight_grads.1 = (f32[2,128,768]{2,1,0:T(8,128)}, f32[2,128,768]{2,1,0:T(8,128)}, f32[2,128,768]{2,1,0:T(8,128)}, f32[2,128,768]{2,1,0:T(8,128)}) custom-call(s32[4]{0:T(128)} %pad_add_fusion.meta, bf16[2,512,1024]{2,1,0:T(8,128)(2,1)} %copy-done, bf16[2,512,1024]{2,1,0:T(8,128)(2,1)} %collective-permute-done.32.sib_ref, ...), custom_call_target="tpu_custom_call" | custom-call | flops 1610612736 | bytes 12582912 | tf_op jit(solution)/shard_map/weight_grads/pallas_call | solution.py:504
  184.6 16.5 %attend.1 = bf16[1024,512]{1,0:T(8,128)(2,1)} custom-call(s32[28]{0:T(128)} %concatenate.32.meta, bf16[4,512,1280]{2,1,0:T(8,128)(2,1)} %normalise.1.own_ref, bf16[4,512,1280]{2,1,0:T(8,128)(2,1)} %collective-permute-done.1.sib_ref, bf16[1280,512]{1,0:T(8,128)(2,1)} %maximum_select_fusion.w0, bf16[1280,512]{1,0:T(8,128)(2,1)} %collective-permute-done.3.w1, ...), custom_call_target="tpu_custom_call" | custom-call | flops 10737418240 | bytes 10485760 | tf_op jit(solution)/shard_map/attend/pallas_call | solution.py:320
  208.6 7.2 %collective-permute-done.36 = f32[128,768]{1,0:T(8,128)S(1)} collective-permute-done((f32[128,768]{1,0:T(8,128)S(1)}, f32[128,768]{1,0:T(8,128)S(1)}, u32[]{:S(2)}, u32[]{:S(2)}) %collective-permute-start.36) | collective-permute-done | bytes 393248 | tf_op jit(solution)/shard_map/ppermute | solution.py:662
  219.4 9.0 %collective-permute-done.25.refs_3_ = bf16[2,256,640]{2,1,0:T(8,128)(2,1)S(1)} collective-permute-done((bf16[2,256,640]{2,1,0:T(8,128)(2,1)S(1)}, bf16[2,256,640]{2,1,0:T(8,128)(2,1)S(1)}, u32[]{:S(2)}, u32[]{:S(2)}) %collective-permute-start.25) | collective-permute-done | bytes 655392 | tf_op jit(solution)/shard_map/ppermute | solution.py:662
  230.9 7.4 %collective-permute-done.13.u1 = bf16[512,1024]{1,0:T(8,128)(2,1)S(1)} collective-permute-done((bf16[512,1024]{1,0:T(8,128)(2,1)S(1)}, bf16[512,1024]{1,0:T(8,128)(2,1)S(1)}, u32[]{:S(2)}, u32[]{:S(2)}) %collective-permute-start.13) | collective-permute-done | bytes 1048608 | tf_op jit(solution)/shard_map/ppermute | solution.py:751
  238.4 9.9 %collective-permute-done.16.d1 = bf16[512,1024]{1,0:T(8,128)(2,1)S(1)} collective-permute-done((bf16[512,1024]{1,0:T(8,128)(2,1)S(1)}, bf16[512,1024]{1,0:T(8,128)(2,1)S(1)}, u32[]{:S(2)}, u32[]{:S(2)}) %collective-permute-start.16) | collective-permute-done | bytes 1048608 | tf_op jit(solution)/shard_map/ppermute | solution.py:752
  248.2 5.1 %collective-permute-start.14 = (bf16[512,1024]{1,0:T(8,128)(2,1)S(1)}, bf16[512,1024]{1,0:T(8,128)(2,1)}, u32[]{:S(2)}, u32[]{:S(2)}) collective-permute-start(bf16[512,1024]{1,0:T(8,128)(2,1)S(1)} %collective-permute-done.13.u1), channel_id=1, source_target_pairs={{0,1},{1,2},{2,3},{4,5},{5,6},{6,7},{8,9},{9,10},{10,11},{12,13},{... | collective-permute-start | bytes 3145736 | tf_op jit(solution)/shard_map/ppermute | solution.py:751
  256.2 7.8 %collective-permute-done.39.refs_3_ = f32[128,768]{1,0:T(8,128)S(1)} collective-permute-done((f32[128,768]{1,0:T(8,128)S(1)}, f32[128,768]{1,0:T(8,128)S(1)}, u32[]{:S(2)}, u32[]{:S(2)}) %collective-permute-start.39) | collective-permute-done | bytes 393248 | tf_op jit(solution)/shard_map/ppermute | solution.py:662
  265.8 6.5 %collective-permute-done.40.refs_4_ = f32[128,768]{1,0:T(8,128)S(1)} collective-permute-done((f32[128,768]{1,0:T(8,128)S(1)}, f32[128,768]{1,0:T(8,128)S(1)}, u32[]{:S(2)}, u32[]{:S(2)}) %collective-permute-start.40) | collective-permute-done | bytes 393248 | tf_op jit(solution)/shard_map/ppermute | solution.py:662
  273.2 5.2 %collective-permute-done.17.d2 = bf16[512,1024]{1,0:T(8,128)(2,1)} collective-permute-done((bf16[512,1024]{1,0:T(8,128)(2,1)S(1)}, bf16[512,1024]{1,0:T(8,128)(2,1)}, u32[]{:S(2)}, u32[]{:S(2)}) %collective-permute-start.17) | collective-permute-done | bytes 1048608 | tf_op jit(solution)/shard_map/ppermute | solution.py:752
  279.0 3.4 %collective-permute-start.15 = (bf16[512,1024]{1,0:T(8,128)(2,1)}, bf16[512,1024]{1,0:T(8,128)(2,1)}, u32[]{:S(2)}, u32[]{:S(2)}) collective-permute-start(bf16[512,1024]{1,0:T(8,128)(2,1)} %collective-permute-done.14.u2), channel_id=1, source_target_pairs={{0,1},{1,2},{2,3},{4,5},{5,6},{6,7},{8,9},{9,10},{10,11},{12,13},{... | collective-permute-start | bytes 3145736 | tf_op jit(solution)/shard_map/ppermute | solution.py:751
  284.5 7.6 %place_grads.1 = (f32[1024,512]{1,0:T(8,128)}, f32[1024,256]{1,0:T(8,128)}, f32[1024,256]{1,0:T(8,128)}, f32[512,1024]{1,0:T(8,128)}) custom-call(s32[4]{0:T(128)} %pad_add_fusion.meta, f32[2,128,768]{2,1,0:T(8,128)} %copy-done.3, f32[2,128,768]{2,1,0:T(8,128)} %copy-done.8, f32[2,128,768]{2,1,0:T(8,128)} %copy-done.7, f32[128,768]{1,0:T(8,128)} %copy-done.28, ...), custom_call_target="tpu_custom_call" | custom-call | bytes 12582912 | tf_op jit(solution)/shard_map/place_grads/pallas_call | solution.py:560
  292.2 12.1 %collective-permute-done.15.u3 = bf16[512,1024]{1,0:T(8,128)(2,1)} collective-permute-done((bf16[512,1024]{1,0:T(8,128)(2,1)}, bf16[512,1024]{1,0:T(8,128)(2,1)}, u32[]{:S(2)}, u32[]{:S(2)}) %collective-permute-start.15) | collective-permute-done | bytes 1048608 | tf_op jit(solution)/shard_map/ppermute | solution.py:751
  304.3 5.1 %collective-permute-done.18.d3 = bf16[512,1024]{1,0:T(8,128)(2,1)} collective-permute-done((bf16[512,1024]{1,0:T(8,128)(2,1)}, bf16[512,1024]{1,0:T(8,128)(2,1)}, u32[]{:S(2)}, u32[]{:S(2)}) %collective-permute-start.18) | collective-permute-done | bytes 1048608 | tf_op jit(solution)/shard_map/ppermute | solution.py:752
  309.4 15.1 %output.1 = bf16[512,1280]{1,0:T(8,128)(2,1)} custom-call(s32[4]{0:T(128)} %pad_add_fusion.meta, bf16[512,5120]{1,0:T(8,128)(2,1)} %bitcast.36, bf16[512,1024]{1,0:T(8,128)(2,1)} %copy-done.2, bf16[512,1024]{1,0:T(8,128)(2,1)} %copy-done.15, bf16[512,1024]{1,0:T(8,128)(2,1)} %collective-permute-done.14.u2, bf16[512,1024]{1,0:T(8,128)(2,1)} %collective-permute-done.15.u3, ...), custom_call_target="tpu_custom_call" | custom-call | flops 5368709120 | bytes 20971520 | tf_op jit(solution)/shard_map/output/pallas_call | solution.py:620
  (188 shorter events, 38.8 us)
Async XLA Ops:
  8.7 144.2 %collective-permute-start.1 = (bf16[4,512,1280]{2,1,0:T(8,128)(2,1)}, bf16[4,512,1280]{2,1,0:T(8,128)(2,1)}, u32[]{:S(2)}, u32[]{:S(2)}) collective-permute-start(bf16[4,512,1280]{2,1,0:T(8,128)(2,1)} %normalise.1.own_ref), channel_id=1, source_target_pairs={{0,4},{4,0},{8,12},{12,8},{16,20},{20,16},{24,28},{28,24},{1,5},{5... | collective-permute-start | bytes 15728648 | tf_op jit(solution)/shard_map/ppermute | solution.py:662
  10.1 33.7 %collective-permute-start.2 = (bf16[640,512]{1,0:T(8,128)(2,1)}, bf16[640,512]{1,0:T(8,128)(2,1)}, u32[]{:S(2)}, u32[]{:S(2)}) collective-permute-start(bf16[640,512]{1,0:T(8,128)(2,1)} %get-tuple-element.34), channel_id=1, source_target_pairs={{0,4},{4,0},{8,12},{12,8},{16,20},{20,16},{24,28},{28,24},{1,5},{5... | collective-permute-start | bytes 1966088 | tf_op jit(solution)/shard_map/ppermute | solution.py:662
  20.2 29.0 %collective-permute-start.21 = (bf16[256,640]{1,0:T(8,128)(2,1)}, bf16[256,640]{1,0:T(8,128)(2,1)S(1)}, u32[]{:S(2)}, u32[]{:S(2)}) collective-permute-start(bf16[256,640]{1,0:T(8,128)(2,1)} %get-tuple-element.32), channel_id=1, source_target_pairs={{0,16},{1,24},{2,0},{3,8},{4,20},{5,28},{6,4},{7,12},{8,25},{9,17}... | collective-permute-start | bytes 983048 | tf_op jit(solution)/shard_map/ppermute | solution.py:739
  24.8 116.9 %collective-permute-start.32 = (bf16[2,512,1024]{2,1,0:T(8,128)(2,1)S(1)}, bf16[2,512,1024]{2,1,0:T(8,128)(2,1)}, u32[]{:S(2)}, u32[]{:S(2)}) collective-permute-start(bf16[2,512,1024]{2,1,0:T(8,128)(2,1)S(1)} %pad_maximum_fusion.own_ref), channel_id=1, source_target_pairs={{0,4},{4,0},{8,12},{12,8},{16,20},{20,16},{24,28},{28,24},{1,5},{5... | collective-permute-start | bytes 6291464 | tf_op jit(solution)/shard_map/ppermute | solution.py:662
  28.8 54.7 %collective-permute-start.8 = (bf16[1280,256]{1,0:T(8,128)(2,1)S(1)}, bf16[1280,256]{1,0:T(8,128)(2,1)S(1)}, u32[]{:S(2)}, u32[]{:S(2)}) collective-permute-start(bf16[1280,256]{1,0:T(8,128)(2,1)S(1)} %maximum_select_fusion.2.w0), channel_id=1, source_target_pairs={{0,8},{4,12},{8,0},{12,4},{16,24},{20,28},{24,16},{28,20},{1,9},{5... | collective-permute-start | bytes 1966088 | tf_op jit(solution)/shard_map/ppermute | solution.py:662
  43.8 39.7 %collective-permute-start.20 = (bf16[256,640]{1,0:T(8,128)(2,1)S(1)}, bf16[256,640]{1,0:T(8,128)(2,1)}, u32[]{:S(2)}, u32[]{:S(2)}) collective-permute-start(bf16[256,640]{1,0:T(8,128)(2,1)S(1)} %copy-done.35), channel_id=1, source_target_pairs={{0,8},{1,0},{2,24},{3,16},{4,12},{5,4},{6,28},{7,20},{8,1},{9,9},{... | collective-permute-start | bytes 983048 | tf_op jit(solution)/shard_map/ppermute | solution.py:739
  49.2 85.7 %collective-permute-start.4 = (bf16[1280,512]{1,0:T(8,128)(2,1)}, bf16[1280,512]{1,0:T(8,128)(2,1)}, u32[]{:S(2)}, u32[]{:S(2)}) collective-permute-start(bf16[1280,512]{1,0:T(8,128)(2,1)} %maximum_select_fusion.w0), channel_id=1, source_target_pairs={{0,16},{4,20},{8,24},{12,28},{16,0},{20,4},{24,8},{28,12},{1,17},{... | collective-permute-start | bytes 3932168 | tf_op jit(solution)/shard_map/ppermute | solution.py:662
  83.5 26.5 %collective-permute-start.9 = (bf16[1280,256]{1,0:T(8,128)(2,1)S(1)}, bf16[1280,256]{1,0:T(8,128)(2,1)S(1)}, u32[]{:S(2)}, u32[]{:S(2)}) collective-permute-start(bf16[1280,256]{1,0:T(8,128)(2,1)S(1)} %maximum_select_fusion.2.w0), channel_id=1, source_target_pairs={{0,16},{4,20},{8,24},{12,28},{16,0},{20,4},{24,8},{28,12},{1,17},{... | collective-permute-start | bytes 1966088 | tf_op jit(solution)/shard_map/ppermute | solution.py:662
  83.6 56.0 %collective-permute-start.3 = (bf16[1280,512]{1,0:T(8,128)(2,1)}, bf16[1280,512]{1,0:T(8,128)(2,1)}, u32[]{:S(2)}, u32[]{:S(2)}) collective-permute-start(bf16[1280,512]{1,0:T(8,128)(2,1)} %maximum_select_fusion.w0), channel_id=1, source_target_pairs={{0,8},{4,12},{8,0},{12,4},{16,24},{20,28},{24,16},{28,20},{1,9},{5... | collective-permute-start | bytes 3932168 | tf_op jit(solution)/shard_map/ppermute | solution.py:662
  112.5 38.2 %collective-permute-start.10 = (bf16[640,256]{1,0:T(8,128)(2,1)}, bf16[640,256]{1,0:T(8,128)(2,1)}, u32[]{:S(2)}, u32[]{:S(2)}) collective-permute-start(bf16[640,256]{1,0:T(8,128)(2,1)} %slice.70), channel_id=1, source_target_pairs={{0,8},{4,12},{8,0},{12,4},{16,24},{20,28},{24,16},{28,20},{1,9},{5... | collective-permute-start | bytes 983048 | tf_op jit(solution)/shard_map/ppermute | solution.py:662
  139.6 66.1 %collective-permute-start.23 = (bf16[4,256,640]{2,1,0:T(8,128)(2,1)S(1)}, bf16[4,256,640]{2,1,0:T(8,128)(2,1)S(1)}, u32[]{:S(2)}, u32[]{:S(2)}) collective-permute-start(bf16[4,256,640]{2,1,0:T(8,128)(2,1)S(1)} %pad_maximum_fusion.1.refs_0_), channel_id=1, source_target_pairs={{0,8},{4,12},{8,0},{12,4},{16,24},{20,28},{24,16},{28,20},{1,9},{5... | collective-permute-start | bytes 3932168 | tf_op jit(solution)/shard_map/ppermute | solution.py:662
  141.7 63.1 %collective-permute-start.24 = (bf16[4,256,640]{2,1,0:T(8,128)(2,1)S(1)}, bf16[4,256,640]{2,1,0:T(8,128)(2,1)S(1)}, u32[]{:S(2)}, u32[]{:S(2)}) collective-permute-start(bf16[4,256,640]{2,1,0:T(8,128)(2,1)S(1)} %pad_maximum_fusion.1.refs_0_), channel_id=1, source_target_pairs={{0,16},{4,20},{8,24},{12,28},{16,0},{20,4},{24,8},{28,12},{1,17},{... | collective-permute-start | bytes 3932168 | tf_op jit(solution)/shard_map/ppermute | solution.py:662
  150.8 67.8 %collective-permute-start.27 = (bf16[4,256,640]{2,1,0:T(8,128)(2,1)S(1)}, bf16[4,256,640]{2,1,0:T(8,128)(2,1)S(1)}, u32[]{:S(2)}, u32[]{:S(2)}) collective-permute-start(bf16[4,256,640]{2,1,0:T(8,128)(2,1)S(1)} %pad_maximum_fusion.1.refs_0_), channel_id=1, source_target_pairs={{0,4},{4,0},{8,12},{12,8},{16,20},{20,16},{24,28},{28,24},{1,5},{5... | collective-permute-start | bytes 3932168 | tf_op jit(solution)/shard_map/ppermute | solution.py:662
  150.9 31.6 %collective-permute-start.5 = (bf16[640,512]{1,0:T(8,128)(2,1)S(1)}, bf16[640,512]{1,0:T(8,128)(2,1)S(1)}, u32[]{:S(2)}, u32[]{:S(2)}) collective-permute-start(bf16[640,512]{1,0:T(8,128)(2,1)S(1)} %copy-done.24), channel_id=1, source_target_pairs={{0,8},{4,12},{8,0},{12,4},{16,24},{20,28},{24,16},{28,20},{1,9},{5... | collective-permute-start | bytes 1966088 | tf_op jit(solution)/shard_map/ppermute | solution.py:662
  152.9 31.6 %collective-permute-start.6 = (bf16[640,512]{1,0:T(8,128)(2,1)S(1)}, bf16[640,512]{1,0:T(8,128)(2,1)}, u32[]{:S(2)}, u32[]{:S(2)}) collective-permute-start(bf16[640,512]{1,0:T(8,128)(2,1)S(1)} %copy-done.25), channel_id=1, source_target_pairs={{0,16},{4,20},{8,24},{12,28},{16,0},{20,4},{24,8},{28,12},{1,17},{... | collective-permute-start | bytes 1966088 | tf_op jit(solution)/shard_map/ppermute | solution.py:662
  182.5 19.9 %collective-permute-start.35 = (f32[2,128,768]{2,1,0:T(8,128)}, f32[2,128,768]{2,1,0:T(8,128)S(1)}, u32[]{:S(2)}, u32[]{:S(2)}) collective-permute-start(f32[2,128,768]{2,1,0:T(8,128)} %get-tuple-element.24), channel_id=1, source_target_pairs={{0,16},{4,20},{8,24},{12,28},{16,0},{20,4},{24,8},{28,12},{1,17},{... | collective-permute-start | bytes 2359304 | tf_op jit(solution)/shard_map/ppermute | solution.py:662
  184.5 19.2 %collective-permute-start.33 = (f32[2,128,768]{2,1,0:T(8,128)}, f32[2,128,768]{2,1,0:T(8,128)S(1)}, u32[]{:S(2)}, u32[]{:S(2)}) collective-permute-start(f32[2,128,768]{2,1,0:T(8,128)} %get-tuple-element.22), channel_id=1, source_target_pairs={{0,8},{4,12},{8,0},{12,4},{16,24},{20,28},{24,16},{28,20},{1,9},{5... | collective-permute-start | bytes 2359304 | tf_op jit(solution)/shard_map/ppermute | solution.py:662
  205.7 22.7 %collective-permute-start.25 = (bf16[2,256,640]{2,1,0:T(8,128)(2,1)S(1)}, bf16[2,256,640]{2,1,0:T(8,128)(2,1)S(1)}, u32[]{:S(2)}, u32[]{:S(2)}) collective-permute-start(bf16[2,256,640]{2,1,0:T(8,128)(2,1)S(1)} %slice.74), channel_id=1, source_target_pairs={{0,8},{4,12},{8,0},{12,4},{16,24},{20,28},{24,16},{28,20},{1,9},{5... | collective-permute-start | bytes 1966088 | tf_op jit(solution)/shard_map/ppermute | solution.py:662
  207.0 24.0 %collective-permute-start.26 = (bf16[2,256,640]{2,1,0:T(8,128)(2,1)S(1)}, bf16[2,256,640]{2,1,0:T(8,128)(2,1)}, u32[]{:S(2)}, u32[]{:S(2)}) collective-permute-start(bf16[2,256,640]{2,1,0:T(8,128)(2,1)S(1)} %slice.75), channel_id=1, source_target_pairs={{0,16},{4,20},{8,24},{12,28},{16,0},{20,4},{24,8},{28,12},{1,17},{... | collective-permute-start | bytes 1966088 | tf_op jit(solution)/shard_map/ppermute | solution.py:662
  215.7 22.6 %collective-permute-start.13 = (bf16[512,1024]{1,0:T(8,128)(2,1)S(1)}, bf16[512,1024]{1,0:T(8,128)(2,1)S(1)}, u32[]{:S(2)}, u32[]{:S(2)}) collective-permute-start(bf16[512,1024]{1,0:T(8,128)(2,1)S(1)} %maximum_select_fusion.1.mid), channel_id=1, source_target_pairs={{0,1},{1,2},{2,3},{4,5},{5,6},{6,7},{8,9},{9,10},{10,11},{12,13},{... | collective-permute-start | bytes 3145736 | tf_op jit(solution)/shard_map/ppermute | solution.py:751
  217.1 31.1 %collective-permute-start.16 = (bf16[512,1024]{1,0:T(8,128)(2,1)S(1)}, bf16[512,1024]{1,0:T(8,128)(2,1)S(1)}, u32[]{:S(2)}, u32[]{:S(2)}) collective-permute-start(bf16[512,1024]{1,0:T(8,128)(2,1)S(1)} %maximum_select_fusion.1.mid), channel_id=1, source_target_pairs={{3,2},{2,1},{1,0},{7,6},{6,5},{5,4},{11,10},{10,9},{9,8},{15,14},{... | collective-permute-start | bytes 3145736 | tf_op jit(solution)/shard_map/ppermute | solution.py:752
  218.6 34.7 %collective-permute-start.38 = (f32[2,128,768]{2,1,0:T(8,128)S(1)}, f32[2,128,768]{2,1,0:T(8,128)S(1)}, u32[]{:S(2)}, u32[]{:S(2)}) collective-permute-start(f32[2,128,768]{2,1,0:T(8,128)S(1)} %pad_maximum_fusion.2.refs_0_), channel_id=1, source_target_pairs={{0,16},{4,20},{8,24},{12,28},{16,0},{20,4},{24,8},{28,12},{1,17},{... | collective-permute-start | bytes 2359304 | tf_op jit(solution)/shard_map/ppermute | solution.py:662
  228.4 26.5 %collective-permute-start.37 = (f32[2,128,768]{2,1,0:T(8,128)S(1)}, f32[2,128,768]{2,1,0:T(8,128)S(1)}, u32[]{:S(2)}, u32[]{:S(2)}) collective-permute-start(f32[2,128,768]{2,1,0:T(8,128)S(1)} %pad_maximum_fusion.2.refs_0_), channel_id=1, source_target_pairs={{0,8},{4,12},{8,0},{12,4},{16,24},{20,28},{24,16},{28,20},{1,9},{5... | collective-permute-start | bytes 2359304 | tf_op jit(solution)/shard_map/ppermute | solution.py:662
  230.9 24.8 %collective-permute-start.41 = (f32[2,128,768]{2,1,0:T(8,128)S(1)}, f32[2,128,768]{2,1,0:T(8,128)S(1)}, u32[]{:S(2)}, u32[]{:S(2)}) collective-permute-start(f32[2,128,768]{2,1,0:T(8,128)S(1)} %pad_maximum_fusion.2.refs_0_), channel_id=1, source_target_pairs={{0,4},{4,0},{8,12},{12,8},{16,20},{20,16},{24,28},{28,24},{1,5},{5... | collective-permute-start | bytes 2359304 | tf_op jit(solution)/shard_map/ppermute | solution.py:662
  238.4 17.3 %collective-permute-start.30 = (bf16[2,256,640]{2,1,0:T(8,128)(2,1)S(1)}, bf16[2,256,640]{2,1,0:T(8,128)(2,1)S(1)}, u32[]{:S(2)}, u32[]{:S(2)}) collective-permute-start(bf16[2,256,640]{2,1,0:T(8,128)(2,1)S(1)} %collective-permute-done.25.refs_3_), channel_id=1, source_target_pairs={{0,4},{4,0},{8,12},{12,8},{16,20},{20,16},{24,28},{28,24},{1,5},{5... | collective-permute-start | bytes 1966088 | tf_op jit(solution)/shard_map/ppermute | solution.py:662
  248.2 25.0 %collective-permute-start.14 = (bf16[512,1024]{1,0:T(8,128)(2,1)S(1)}, bf16[512,1024]{1,0:T(8,128)(2,1)}, u32[]{:S(2)}, u32[]{:S(2)}) collective-permute-start(bf16[512,1024]{1,0:T(8,128)(2,1)S(1)} %collective-permute-done.13.u1), channel_id=1, source_target_pairs={{0,1},{1,2},{2,3},{4,5},{5,6},{6,7},{8,9},{9,10},{10,11},{12,13},{... | collective-permute-start | bytes 3145736 | tf_op jit(solution)/shard_map/ppermute | solution.py:751
  253.3 25.1 %collective-permute-start.17 = (bf16[512,1024]{1,0:T(8,128)(2,1)S(1)}, bf16[512,1024]{1,0:T(8,128)(2,1)}, u32[]{:S(2)}, u32[]{:S(2)}) collective-permute-start(bf16[512,1024]{1,0:T(8,128)(2,1)S(1)} %collective-permute-done.16.d1), channel_id=1, source_target_pairs={{3,2},{2,1},{1,0},{7,6},{6,5},{5,4},{11,10},{10,9},{9,8},{15,14},{... | collective-permute-start | bytes 3145736 | tf_op jit(solution)/shard_map/ppermute | solution.py:752
  255.7 22.8 %collective-permute-start.42 = (f32[2,128,768]{2,1,0:T(8,128)S(1)}, f32[2,128,768]{2,1,0:T(8,128)S(1)}, u32[]{:S(2)}, u32[]{:S(2)}) collective-permute-start(f32[2,128,768]{2,1,0:T(8,128)S(1)} %collective-permute-done.37.refs_1_), channel_id=1, source_target_pairs={{0,4},{4,0},{8,12},{12,8},{16,20},{20,16},{24,28},{28,24},{1,5},{5... | collective-permute-start | bytes 2359304 | tf_op jit(solution)/shard_map/ppermute | solution.py:662
  255.8 23.2 %collective-permute-start.43 = (f32[2,128,768]{2,1,0:T(8,128)S(1)}, f32[2,128,768]{2,1,0:T(8,128)S(1)}, u32[]{:S(2)}, u32[]{:S(2)}) collective-permute-start(f32[2,128,768]{2,1,0:T(8,128)S(1)} %collective-permute-done.38.refs_2_), channel_id=1, source_target_pairs={{0,4},{4,0},{8,12},{12,8},{16,20},{20,16},{24,28},{28,24},{1,5},{5... | collective-permute-start | bytes 2359304 | tf_op jit(solution)/shard_map/ppermute | solution.py:662
  273.2 18.9 %collective-permute-start.28 = (bf16[4,256,640]{2,1,0:T(8,128)(2,1)S(1)}, bf16[4,256,640]{2,1,0:T(8,128)(2,1)S(1)}, u32[]{:S(2)}, u32[]{:S(2)}) collective-permute-start(bf16[4,256,640]{2,1,0:T(8,128)(2,1)S(1)} %collective-permute-done.23.refs_1_), channel_id=1, source_target_pairs={{0,4},{4,0},{8,12},{12,8},{16,20},{20,16},{24,28},{28,24},{1,5},{5... | collective-permute-start | bytes 3932168 | tf_op jit(solution)/shard_map/ppermute | solution.py:662
  279.0 25.3 %collective-permute-start.15 = (bf16[512,1024]{1,0:T(8,128)(2,1)}, bf16[512,1024]{1,0:T(8,128)(2,1)}, u32[]{:S(2)}, u32[]{:S(2)}) collective-permute-start(bf16[512,1024]{1,0:T(8,128)(2,1)} %collective-permute-done.14.u2), channel_id=1, source_target_pairs={{0,1},{1,2},{2,3},{4,5},{5,6},{6,7},{8,9},{9,10},{10,11},{12,13},{... | collective-permute-start | bytes 3145736 | tf_op jit(solution)/shard_map/ppermute | solution.py:751
  282.3 27.1 %collective-permute-start.18 = (bf16[512,1024]{1,0:T(8,128)(2,1)}, bf16[512,1024]{1,0:T(8,128)(2,1)}, u32[]{:S(2)}, u32[]{:S(2)}) collective-permute-start(bf16[512,1024]{1,0:T(8,128)(2,1)} %collective-permute-done.17.d2), channel_id=1, source_target_pairs={{3,2},{2,1},{1,0},{7,6},{6,5},{5,4},{11,10},{10,9},{9,8},{15,14},{... | collective-permute-start | bytes 3145736 | tf_op jit(solution)/shard_map/ppermute | solution.py:752
  (57 other events, 1141.0 us)

commit v2 on v1

--- a/solution.py
+++ b/solution.py
@@ -204,14 +204,16 @@
 
 
 def norm_kernel(meta, x_ref, out_ref):
-    chip = meta[0]
+    chip, core = meta[0], meta[1]
     parts, rows, wide = out_ref.shape
+    half = wide // 2
     x = x_ref[...].astype(jnp.float32)
     scale = lax.rsqrt(jnp.mean(x * x, axis=-1, keepdims=True) + 1e-06)
     for j in range(parts):
-        at = pl.multiple_of((chip ^ j) * wide, wide)
-        piece = x_ref[:, pl.ds(at, wide)].astype(jnp.float32)
-        out_ref[j] = (piece * scale).astype(jnp.bfloat16)
+        for side in range(2):
+            at = pl.multiple_of(((chip ^ j) * 2 + (core ^ side)) * half, half)
+            piece = x_ref[:, pl.ds(at, half)].astype(jnp.float32)
+            out_ref[j, :, side * half : (side + 1) * half] = (piece * scale).astype(jnp.bfloat16)
 
 
 def normalise(meta, flat, parts):
@@ -232,15 +234,16 @@
     )(meta, flat)
 
 
-def product(x, weights):
+def product(ref, weights, swapped):
     w0, w1, w2, wx, wy = weights
     half = wx.shape[0]
-    total = nn(x(0), w0[...])
-    total += nn(x(1), w1[...])
-    total += nn(x(2), w2[...])
-    last = x(3)
-    total += nn(last[:, :half], wx[...])
-    total += nn(last[:, half:], wy[...])
+    first, second = slice(0, half), slice(half, 2 * half)
+    if not swapped:
+        total = nn(ref[0], w0[...]) + nn(ref[1], w1[...]) + nn(ref[2], w2[...])
+        return total + nn(ref[3, :, first], wx[...]) + nn(ref[3, :, second], wy[...])
+    total = nn(ref[3, :, second], wx[...]) + nn(ref[3, :, first], wy[...])
+    for j, weight in enumerate((w0, w1, w2)):
+        total += nn(ref[j, :, second], weight[first]) + nn(ref[j, :, first], weight[second])
     return total
 
 
@@ -251,19 +254,19 @@
 
     @pl.when(step < half)
     def _():
-        out_ref[...] = product(lambda j: own_ref[j], weights).astype(jnp.bfloat16)
+        out_ref[...] = product(own_ref, weights, False).astype(jnp.bfloat16)
 
     @pl.when(step >= half)
     def _():
-        out_ref[...] = product(lambda j: sib_ref[j], weights).astype(jnp.bfloat16)
-
-
-def pair_specs(parts, block, wide, steps):
-    own = pl.BlockSpec(
+        out_ref[...] = product(sib_ref, weights, True).astype(jnp.bfloat16)
+
+
+def pair_specs(parts, block, wide, steps, sib_first=False):
+    first = pl.BlockSpec(
         (parts, block, wide), lambda i, *m: (0, jnp.minimum(i, steps // 2 - 1), 0)
     )
-    sib = pl.BlockSpec((parts, block, wide), lambda i, *m: (0, jnp.maximum(i - steps // 2, 0), 0))
-    return [own, sib]
+    then = pl.BlockSpec((parts, block, wide), lambda i, *m: (0, jnp.maximum(i - steps // 2, 0), 0))
+    return [then, first] if sib_first else [first, then]
 
 
 def project_kv(own, sib, weights):
@@ -283,52 +286,66 @@
     )(own, sib, *weights)
 
 
-def attend_kernel(factor, meta, own_ref, sib_ref, w0, w1, w2, wx, wy, kv_ref, out_ref, query):
+def attend_kernel(factor, meta, own_ref, sib_ref, w0, w1, w2, wx, wy, kv_ref, own_out, sib_out, query, context):
     step = pl.program_id(0)
     half = pl.num_programs(0) // 2
     weights = (w0, w1, w2, wx, wy)
 
+    @pl.when(step >= half)
+    def _():
+        query[...] = product(own_ref, weights, False).astype(jnp.bfloat16)
+
     @pl.when(step < half)
     def _():
-        query[...] = product(lambda j: own_ref[j], weights).astype(jnp.bfloat16)
-
-    @pl.when(step >= half)
-    def _():
-        query[...] = product(lambda j: sib_ref[j], weights).astype(jnp.bfloat16)
-
-    length = meta[4 + step]
-    start = meta[8 + step]
-    positions = out_ref.shape[0]
+        query[...] = product(sib_ref, weights, True).astype(jnp.bfloat16)
+
+    sample = lax.rem(step + half, 2 * half)
+    length = meta[4 + sample]
+    start = meta[8 + sample]
+    positions = context.shape[0]
     keys = kv_ref[:, :HD]
     values = kv_ref[:, HD:]
     row = lax.broadcasted_iota(jnp.int32, (positions, positions), 0)
     column = lax.broadcasted_iota(jnp.int32, (positions, positions), 1)
     visible = (column < length) & ((column < start) | (column <= row))
-    for head in range(out_ref.shape[1] // HD):
+    for head in range(context.shape[1] // HD):
         at = slice(head * HD, (head + 1) * HD)
         scores = jnp.where(visible, nt(query[:, at], keys) * factor, NEG)
         top = jnp.max(scores, axis=-1, keepdims=True)
         weight = jnp.where(visible, jnp.exp(scores - top), 0.0)
         weight = (weight / jnp.sum(weight, axis=-1, keepdims=True)).astype(jnp.bfloat16)
-        out_ref[:, at] = nn(weight, values).astype(jnp.bfloat16)
+        context[:, at] = nn(weight, values).astype(jnp.bfloat16)
+
+    @pl.when(step >= half)
+    def _():
+        own_out[...] = context[...]
+
+    @pl.when(step < half)
+    def _():
+        sib_out[...] = context[...]
 
 
 def attend(meta, own, sib, weights, kv, positions, factor):
     parts, count, wide = own.shape
     columns = weights[0].shape[1]
     steps = 2 * count // positions
+    half = steps // 2
+    out = jax.ShapeDtypeStruct((count, columns), jnp.bfloat16)
     return pl.pallas_call(
         functools.partial(attend_kernel, factor),
         grid_spec=pltpu.PrefetchScalarGridSpec(
             num_scalar_prefetch=1,
             grid=(steps,),
-            in_specs=pair_specs(parts, positions, wide, steps)
+            in_specs=pair_specs(parts, positions, wide, steps, True)
             + [whole()] * 5
-            + [pl.BlockSpec((positions, 2 * HD), lambda i, m: (i, 0))],
-            out_specs=pl.BlockSpec((positions, columns), lambda i, m: (i, 0)),
-            scratch_shapes=[pltpu.VMEM((positions, columns), jnp.bfloat16)],
+            + [pl.BlockSpec((positions, 2 * HD), lambda i, m: ((i + half) % steps, 0))],
+            out_specs=[
+                pl.BlockSpec((positions, columns), lambda i, m: (jnp.maximum(i - half, 0), 0)),
+                pl.BlockSpec((positions, columns), lambda i, m: (jnp.minimum(i, half - 1), 0)),
+            ],
+            scratch_shapes=[pltpu.VMEM((positions, columns), jnp.bfloat16)] * 2,
         ),
-        out_shape=jax.ShapeDtypeStruct((2 * count, columns), jnp.bfloat16),
+        out_shape=[out, out],
         compiler_params=params(),
         cost_estimate=cost(8 * count * parts * wide * columns, 4 * count * parts * wide),
         name="attend",
@@ -516,8 +533,8 @@
     )(meta, own, sib, ctx, grad)
 
 
-def place_kernel(meta, *refs):
-    own, sib, outs = refs[:5], refs[5:10], refs[10:]
+def place_kernel(pieces, groups, meta, *refs):
+    own, sib, outs = refs[:groups], refs[groups : 2 * groups], refs[-4:]
     step = pl.program_id(0)
     first = meta[1] == 0
     wq, wk, wv, wo = outs
@@ -528,12 +545,12 @@
     def pick(group, route, j):
         if j < 3:
             return group[j][route]
-        return group[3 + route][...]
+        return group[route][...]
 
     for route in range(2):
-        for j in range(4):
-
-            @pl.when(step == route * 4 + j)
+        for place, j in enumerate(pieces):
+
+            @pl.when(step == route * len(pieces) + place)
             def _():
                 mine, other = pick(own, route, j), pick(sib, route, j)
                 for side, block in enumerate(
@@ -548,90 +565,126 @@
                         wo[row : row + HD] = block[:, cut : cut + tall]
 
 
-def place_grads(meta, own, sib, shapes):
-    tall = own[0].shape[1]
+def place_grads(meta, own, sib, shapes, pieces, into=()):
+    tall = own[0].shape[-2]
+    size = len(pieces)
 
     def spot(i, m):
-        return (i // 4) * 4 + (m[0] ^ (i % 4))
+        return (i // size) * 4 + (m[0] ^ (i % size + pieces[0]))
 
     rows = lambda s: pl.BlockSpec((tall, s[1]), lambda i, m: (spot(i, m), 0))
     specs = [rows(s) for s in shapes[:3]]
     specs.append(pl.BlockSpec((shapes[3][0], tall), lambda i, m: (0, spot(i, m))))
+    inputs = 2 * len(own)
     return pl.pallas_call(
-        place_kernel,
+        functools.partial(place_kernel, tuple(pieces), len(own)),
         grid_spec=pltpu.PrefetchScalarGridSpec(
             num_scalar_prefetch=1,
-            grid=(8,),
-            in_specs=[whole()] * 10,
+            grid=(2 * size,),
+            in_specs=[whole()] * inputs + [pl.BlockSpec(memory_space=pl.ANY)] * len(into),
             out_specs=specs,
         ),
         out_shape=[jax.ShapeDtypeStruct(s, jnp.float32) for s in shapes],
+        input_output_aliases={1 + inputs + n: n for n in range(len(into))},
         compiler_params=params(),
-        cost_estimate=cost(0, 2 * 4 * sum(s[0] * s[1] for s in shapes)),
+        cost_estimate=cost(0, size * 2 * sum(s[0] * s[1] for s in shapes)),
         name="place_grads",
-    )(meta, *own, *sib)
-
-
-def output_kernel(meta, tok_ref, mid, u1, u2, u3, d1, d2, d3, *refs):
-    wos, out_ref, ctx = refs[:10], refs[10], refs[11]
-    chip, plane = meta[0], meta[2]
+    )(meta, *own, *sib, *into)
+
+
+def context_part(meta, ref, j, quarter):
+    side = ref.shape[1] // 2
+    at = (meta[0] ^ j) * quarter
+    head = ((at // side) ^ meta[1]) * side + at % side
+    return ref[:, pl.ds(pl.multiple_of(head, quarter), quarter)]
+
+
+def near_kernel(meta, tok_ref, *refs):
+    contexts, own, sib, out_ref = refs[:3], refs[3:6], refs[6:9], refs[9]
     step = pl.program_id(0)
-    quarter = wos[0].shape[1]
+    quarter = own[0].shape[1]
+
+    def run(group):
+        for k, ref in enumerate(contexts):
+            total = nn(context_part(meta, ref, 0, quarter), group[0][k])
+            for j in range(1, 3):
+                total += nn(context_part(meta, ref, j, quarter), group[j][k])
+            if k == 0:
+                out_ref[...] = tok_ref[...].astype(jnp.float32) + total
+            else:
+                out_ref[...] += total
 
     @pl.when(step == 0)
     def _():
-        ctx[plane] = mid[...]
-        for k, (up, down) in enumerate(((u1, d1), (u2, d2), (u3, d3)), 1):
-
-            @pl.when(plane >= k)
-            def _():
-                ctx[plane - k] = up[...]
-
-            @pl.when(plane + k <= 3)
-            def _():
-                ctx[plane + k] = down[...]
-
-    def run(group):
-        total = tok_ref[...].astype(jnp.float32)
-        for j in range(4):
-            column = pl.multiple_of((chip ^ j) * quarter, quarter)
-            for r in range(4):
-                source = (chip ^ j) ^ plane ^ r
-                if j < 3:
-                    weight = group[j][r]
-                else:
-                    weight = group[3 + r // 2][r % 2]
-                total += nn(ctx[source, :, pl.ds(column, quarter)], weight)
-        out_ref[...] = total.astype(jnp.bfloat16)
-
-    @pl.when(step == 0)
-    def _():
-        run(wos[:5])
+        run(own)
 
     @pl.when(step == 1)
     def _():
-        run(wos[5:])
-
-
-def output(meta, flat, contexts, own, sib):
+        run(sib)
+
+
+def output_near(meta, flat, contexts, own, sib):
     count = flat.shape[0]
     half = own[0].shape[2]
     wide = contexts[0].shape[1]
     return pl.pallas_call(
-        output_kernel,
+        near_kernel,
         grid_spec=pltpu.PrefetchScalarGridSpec(
             num_scalar_prefetch=1,
             grid=(2,),
             in_specs=[pl.BlockSpec((count, half), lambda i, m: (0, 2 * m[2] + (m[1] ^ i)))]
-            + [whole()] * 17,
+            + [whole()] * 9,
             out_specs=pl.BlockSpec((count, half), lambda i, m: (0, m[1] ^ i)),
-            scratch_shapes=[pltpu.VMEM((4, count, wide), jnp.bfloat16)],
         ),
-        out_shape=jax.ShapeDtypeStruct((count, 2 * half), jnp.bfloat16),
+        out_shape=jax.ShapeDtypeStruct((count, 2 * half), jnp.float32),
         compiler_params=params(),
-        cost_estimate=cost(16 * count * wide * half, 32 * wide * half),
-        name="output",
-    )(meta, flat, *contexts, *own, *sib)
+        cost_estimate=cost(12 * count * wide * half, 32 * wide * half),
+        name="output_near",
+    )(meta, flat, *contexts, *own[:3], *sib[:3])
+
+
+def far_kernel(meta, sum_ref, c0, c1, c2, c3, *refs):
+    own, sib, out_ref = refs[:5], refs[5:10], refs[10]
+    step = pl.program_id(0)
+    quarter = own[0].shape[1]
+
+    def run(group):
+        total = sum_ref[...]
+        for k, ref in enumerate((c0, c1, c2, c3)):
+            total += nn(context_part(meta, ref, 3, quarter), group[3 + k // 2][k % 2])
+        for j in range(3):
+            total += nn(context_part(meta, c3, j, quarter), group[j][0])
+        out_ref[...] = total.astype(jnp.bfloat16)
+
+    @pl.when(step == 0)
+    def _():
+        run(own)
+
+    @pl.when(step == 1)
+    def _():
+        run(sib)
+
+
+def output_far(meta, near, contexts, own, sib):
+    count, columns = near.shape
+    half = columns // 2
+    quarter = own[0].shape[1]
+    slots = [pl.BlockSpec((1, quarter, half), lambda i, m: (3, 0, 0))] * 3 + [whole()] * 2
+    return pl.pallas_call(
+        far_kernel,
+        grid_spec=pltpu.PrefetchScalarGridSpec(
+            num_scalar_prefetch=1,
+            grid=(2,),
+            in_specs=[pl.BlockSpec((count, half), lambda i, m: (0, m[1] ^ i))]
+            + [whole()] * 4
+            + slots * 2,
+            out_specs=pl.BlockSpec((count, half), lambda i, m: (0, m[1] ^ i)),
+        ),
+        out_shape=jax.ShapeDtypeStruct((count, columns), jnp.bfloat16),
+        compiler_params=params(),
+        cost_estimate=cost(4 * count * 7 * quarter * half, 8 * count * columns),
+        name="output_far",
+    )(meta, near, *contexts, *own, *sib)
 
 
 def plane_body(
@@ -663,10 +716,8 @@
 
     swap, over_x, over_y = across(1), across(2), across(4)
 
-    def spread(x):
-        from_x, from_y = over_x(x), over_y(x)
-        half = x.shape[0] // 2
-        return x, from_x, from_y, over_x(from_y[:half]), over_y(from_x[half:])
+    def after(x, *others):
+        return lax.optimization_barrier((x, *others))[0]
 
     local = jnp.concatenate([prefix_len, causal_start, span_sample])
     remote = swap(local)
@@ -689,71 +740,86 @@
         other = lax.dynamic_slice_in_dim(weight, (1 - core) * size, size, 1)
         return mine, other
 
-    def joined(mine, got):
-        return jnp.where(
-            core == 0, jnp.concatenate([mine, got]), jnp.concatenate([got, mine])
-        )
-
     k_mine, k_other = halves(bb_wk)
     v_mine, v_other = halves(bb_wv)
+    q_mine, q_other = halves(bb_wq)
     kv_got = swap(jnp.concatenate([k_other, v_other], axis=1))
-    kv_shard = joined(jnp.concatenate([k_mine, v_mine], axis=1), kv_got)
-    q_mine, q_other = halves(bb_wq)
-    q_shard = joined(q_mine, swap(q_other))
-    kv_weights = spread(kv_shard)
-    q_weights = spread(q_shard)
-
-    normed = normalise(chip_meta, flat, 4)
-    normed_sib = swap(normed)
-
+    kv_shard = jnp.concatenate([jnp.concatenate([k_mine, v_mine], axis=1), kv_got])
+    kv_x, kv_y = over_x(kv_shard), over_y(kv_shard)
+
+    q_got = swap(after(q_other, kv_shard))
     spans = action_tokens.shape[0]
     pad = ((0, 0), (0, PAD - STEPS), (0, 0))
     pair = jnp.stack([jnp.pad(action_tokens, pad), jnp.pad(action_cot, pad)])
     pair = pair.reshape(2, spans * PAD, action_tokens.shape[2])
-    pair_sib = swap(pair)
-    proj, dctx = expert_project(chip_meta, pair, pair_sib, ex_wq, ex_wk, ex_wv, ex_wo)
-
-    kv = project_kv(normed, normed_sib, kv_weights)
+    pair_sib = swap(after(pair, kv_shard))
+    normed = normalise(chip_meta, after(flat, q_got, pair_sib), 4)
+    normed_sib = swap(after(normed, kv_x, kv_y))
+    half = kv_x.shape[0] // 2
+    low, high = kv_y[:half], kv_x[half:]
+    kv_dx, kv_dy = over_x(low), over_y(high)
+    proj, dctx = expert_project(
+        chip_meta, after(pair, low, high), pair_sib, ex_wq, ex_wk, ex_wv, ex_wo
+    )
+    q_shard = after(jnp.concatenate([q_mine, q_got]), kv_dx, kv_dy, normed_sib, proj)
+    q_x, q_y = over_x(q_shard), over_y(q_shard)
+
+    quarter = bb_wo.shape[0] // 4
+    wo_rows = after(bb_wo, q_shard)
+    by_chip = [
+        lax.dynamic_slice_in_dim(wo_rows, (chip ^ m) * quarter, quarter, 0) for m in range(4)
+    ]
+    wo_a = [by_chip[0], over_x(by_chip[1]), over_y(by_chip[2]), across(6)(by_chip[3])]
+
+    kv = project_kv(normed, normed_sib, (kv_shard, kv_x, kv_y, kv_dx, kv_dy))
     ectx, egrad = expert_attend(meta, proj, dctx, kv, factor)
-    ax, ak, by, bk = weight_grads(chip_meta, pair, pair_sib, ectx, egrad)
-    a_sum = ak + over_x(ax)
-    b_sum = bk + over_y(by)
-    mine = jnp.stack([a_sum[0] + over_y(a_sum[1]), b_sum[0] + over_x(b_sum[1])])
-    from_x, from_y = over_x(mine), over_y(mine)
-    full = (mine, from_x, from_y, over_x(from_y[0]), over_y(from_x[1]))
-    full_sib = tuple(swap(x) for x in full)
+    low, high = after(q_y, ectx, *wo_a)[:half], after(q_x, ectx, *wo_a)[half:]
+    q_dx, q_dy = over_x(low), over_y(high)
+    wo_a = jnp.stack(wo_a)
+    wo_b = []
+    for s in range(4):
+        piece = lax.dynamic_index_in_dim(
+            wo_a, chip ^ lax.rem(plane + s, 4), 0, keepdims=False
+        )
+        perm = [(i, (i + s) % 4) for i in range(4)]
+        wo_b.append(lax.ppermute(piece, "tensor", perm) if s else piece)
+
+    ax, ak, by, bk = weight_grads(chip_meta, pair, pair_sib, after(ectx, low, high), egrad)
+    a_got, b_got = over_x(ax), over_y(by)
+    ctx = attend(
+        meta, normed, normed_sib, (q_shard, q_x, q_y, q_dx, q_dy), after(kv, ax), positions, factor
+    )
+    ctx_own, ctx_other = ctx
+    wo_b = [after(x, ctx_own) for x in wo_b]
+    a_got, b_got = after(a_got, ctx_own), after(b_got, ctx_own)
+    ctx_got = swap(after(ctx_other, a_got, b_got, *wo_b))
+    ctx_rows = jnp.concatenate([ctx_own, ctx_got], axis=1)
+    turn = lambda x: lax.ppermute(x, "tensor", [(i, (i + 1) % 4) for i in range(4)])
+    ctx_1 = turn(ctx_rows)
+    a_sum, b_sum = ak + a_got, bk + b_got
+    a_rest, b_rest = over_y(a_sum[1]), over_x(b_sum[1])
+    mine = jnp.stack([a_sum[0] + a_rest, b_sum[0] + b_rest])
+    wo = after(jnp.stack([after(x, ctx_got) for x in wo_b]), a_rest, b_rest)
+    wo_x, wo_y = over_x(wo), over_y(wo)
+    sent = after(mine, wo_x, wo_y)
+    from_x, from_y = over_x(sent), over_y(sent)
+    ctx_2 = turn(ctx_1)
+    wo_sib = [swap(after(wo, wo_x)), swap(wo_x), swap(wo_y)]
+    wo_dx = over_x(after(wo_y, from_x, from_y)[:2])
+    wo_dy = over_y(after(wo_x, from_x, from_y)[2:])
+    ctx_3 = turn(ctx_2)
+    near = output_near(chip_meta, flat, (ctx_rows, ctx_1, ctx_2), (wo, wo_x, wo_y), wo_sib)
+    far_x = over_x(after(from_y, wo_dx, wo_dy)[0])
+    far_y = over_y(after(from_x, wo_dx, wo_dy)[1])
+    near_grads = (mine, from_x, from_y)
+    near_sib = tuple(swap(x) for x in near_grads)
     shapes = (ex_wq.shape, ex_wk.shape, ex_wv.shape, ex_wo.shape)
-    grads = place_grads(chip_meta, full, full_sib, shapes)
-
-    quarter = bb_wo.shape[0] // 4
-    got = []
-    for r in range(4):
-        to = chip ^ plane ^ r
-        perm = [
-            (((a * 2 + k) * 4 + z), (((a ^ z ^ r) * 2 + k) * 4 + a))
-            for a in range(4)
-            for k in range(2)
-            for z in range(4)
-        ]
-        piece = lax.dynamic_slice_in_dim(bb_wo, to * quarter, quarter, 0)
-        got.append(lax.ppermute(piece, ("dp", "tensor"), perm))
-    wo_own = spread(jnp.stack(got))
-    wo_sib = tuple(swap(x) for x in wo_own)
-
-    ctx = attend(meta, normed, normed_sib, q_weights, kv, positions, factor)
-    ctx_own, ctx_other = ctx[:count], ctx[count:]
-    ctx_got = swap(ctx_other)
-    ctx_rows = jnp.where(
-        core == 0,
-        jnp.concatenate([ctx_own, ctx_got], axis=1),
-        jnp.concatenate([ctx_got, ctx_own], axis=1),
-    )
-    up = lambda x: lax.ppermute(x, "tensor", [(0, 1), (1, 2), (2, 3)])
-    down = lambda x: lax.ppermute(x, "tensor", [(3, 2), (2, 1), (1, 0)])
-    u1, d1 = up(ctx_rows), down(ctx_rows)
-    u2, d2 = up(u1), down(d1)
-    u3, d3 = up(u2), down(d2)
-    out = output(chip_meta, flat, (ctx_rows, u1, u2, u3, d1, d2, d3), wo_own, wo_sib)
+    grads = place_grads(chip_meta, near_grads, near_sib, shapes, range(3))
+    wo_own = (wo, wo_x, wo_y, wo_dx, wo_dy)
+    wo_sib += [swap(wo_dx), swap(wo_dy)]
+    far = (far_x, far_y)
+    grads = place_grads(chip_meta, far, [swap(x) for x in far], shapes, range(3, 4), grads)
+    out = output_far(chip_meta, near, (ctx_rows, ctx_1, ctx_2, ctx_3), wo_own, wo_sib)
     return (out.reshape(samples, positions, -1), *grads)
 
 

time: 325 us -> 246 us (0.76)
  starting transfers between devices: 97.5 us -> 36.7 us
  waiting for transfers between devices: 122 us -> 101 us
  Pallas kernels: 83 us -> 89.6 us
  other arithmetic: 7.91 us -> 2.97 us
    ppermute x10 -> x6, waiting for transfers between devices: 63.3 us -> 15.5 us  [the longest x3 15.5 us: plane_body(): lax.ppermute(x, 'tensor', [(i, (i + 1) % 4) for i in range(4)])]
    ppermute x36 -> x39, starting transfers between devices: 70.4 us -> 30.6 us  [across(): return lambda x: lax.ppermute(x, 'dp', [(i, i ^ mask) for i in range(8)])]
    ppermute x36 -> x39, waiting for transfers between devices: 58.9 us -> 85.5 us  [across(): return lambda x: lax.ppermute(x, 'dp', [(i, i ^ mask) for i in range(8)])]
    ppermute x10 -> x6, starting transfers between devices: 27.1 us -> 6.05 us  [the longest x3 4.67 us: plane_body(): wo_b.append(lax.ppermute(piece, 'tensor', perm) if s else piece)]
    pallas_call x2 -> x4, Pallas kernels: 22.7 us -> 28.5 us  [the longest x1 10.3 us: output_near(): pl.pallas_call(near_kernel, grid_spec=pltpu.PrefetchScalarGridSpec(num_sc...]
    select_n x3 -> x0, other arithmetic: 4.42 us -> none  [the longest x2 4.12 us: joined(): jnp.where(core == 0, jnp.concatenate([mine, got]), jnp.concatenate([got,...]
    slice x7 -> x6, local copies, waits for them, and re-layouts: 7.36 us -> 4.36 us  [the longest x2 2.26 us: plane_body(): low, high = (after(q_y, ectx, *wo_a)[:half], after(q_x, ectx, *wo_a)[half:])]
  transfers between devices with their start and end apart: 46 -> 45, of which waited for: 16 -> 17; matrix products, arithmetic and copies ran while one was open for 6% -> 5% of each run, Pallas kernels for 19% -> 35%
where the time goes in v2:
time: 246 us; the launch traced here: 245 us
  waiting for transfers between devices  101 us (41%)
  Pallas kernels  89.6 us (36%)
  starting transfers between devices  36.7 us (15%)
  local copies, waits for them, and re-layouts  13.6 us (6%)
  other arithmetic  2.97 us (1%)
    ppermute x39, waiting for transfers between devices, across(): return lambda x: lax.ppermute(x, 'dp', [(i, i ^ mask) for i in range(8)])  85.5 us
    ppermute x39, starting transfers between devices, across(): return lambda x: lax.ppermute(x, 'dp', [(i, i ^ mask) for i in range(8)])  30.6 us
    pallas_call x1, Pallas kernels, attend(): pl.pallas_call(functools.partial(attend_kernel, factor), grid_spec=pltpu....  17.2 us
    ppermute x3, waiting for transfers between devices, plane_body(): lax.ppermute(x, 'tensor', [(i, (i + 1) % 4) for i in range(4)])  15.5 us
    pallas_call x1, Pallas kernels, expert_attend(): pl.pallas_call(functools.partial(expert_kernel, factor, spans), grid_spec...  13.7 us
    pallas_call x1, Pallas kernels, output_near(): pl.pallas_call(near_kernel, grid_spec=pltpu.PrefetchScalarGridSpec(num_sc...  10.3 us
    pallas_call x2, Pallas kernels, place_grads(): pl.pallas_call(functools.partial(place_kernel, tuple(pieces), len(own)),...  9.51 us
    pallas_call x1, Pallas kernels, output_far(): pl.pallas_call(far_kernel, grid_spec=pltpu.PrefetchScalarGridSpec(num_sca...  8.71 us
  transfers between devices with their start and end apart: 45, of which 17 were waited for; matrix products, arithmetic and copies ran while one was open for 5% of the time, Pallas kernels for 35%

profile of v2, /device:TPU:0, one launch (start us, length us, event | category | flops | bytes accessed | tf_op | source)
XLA Modules:
  0.0 245.1 jit_solution(4291387981594327514)
XLA Ops:
  4.6 2.5 %constant_dynamic-slice_fusion.4 = (bf16[640,512]{1,0:T(8,128)(2,1)S(1)}, bf16[640,512]{1,0:T(8,128)(2,1)}) fusion(bf16[640,1024]{1,0:T(8,128)(2,1)} %param.18, s32[]{:T(128)S(6)} %select_n.55, s32[]{:T(128)S(6)} %select_n.52), kind=kLoop, calls=%fused_computation.27 | loop fusion | bytes 2621448 | tf_op jit(solution)/shard_map/dynamic_slice | solution.py:739
  7.7 2.5 %collective-permute-start.4 = (bf16[1280,256]{1,0:T(8,128)(2,1)S(1)}, bf16[1280,256]{1,0:T(8,128)(2,1)}, u32[]{:S(2)}, u32[]{:S(2)}) collective-permute-start(bf16[1280,256]{1,0:T(8,128)(2,1)S(1)} %pad_maximum_fusion.5.w0), channel_id=1, source_target_pairs={{0,8},{4,12},{8,0},{12,4},{16,24},{20,28},{24,16},{28,20},{1,9},{5... | collective-permute-start | bytes 1966088 | tf_op jit(solution)/shard_map/ppermute | solution.py:715
  10.2 1.5 collective-permute-start.5
  12.3 7.1 %normalise.1.own_ref = bf16[4,512,1280]{2,1,0:T(8,128)(2,1)} custom-call(s32[4]{0:T(128)} %pad_add_fusion.meta, bf16[512,5120]{1,0:T(8,128)(2,1)} %bitcast.47), custom_call_target="tpu_custom_call" | custom-call | flops 10485760 | bytes 10485760 | tf_op jit(solution)/shard_map/normalise/pallas_call | solution.py:222
  19.5 6.2 %collective-permute-done.4.w1 = bf16[1280,256]{1,0:T(8,128)(2,1)} collective-permute-done((bf16[1280,256]{1,0:T(8,128)(2,1)S(1)}, bf16[1280,256]{1,0:T(8,128)(2,1)}, u32[]{:S(2)}, u32[]{:S(2)}) %collective-permute-start.4) | collective-permute-done | bytes 655392 | tf_op jit(solution)/shard_map/ppermute | solution.py:715
  29.5 1.8 collective-permute-start.8
  32.5 7.2 %expert_project.1 = (bf16[1024,512]{1,0:T(8,128)(2,1)}, bf16[1024,256]{1,0:T(8,128)(2,1)}) custom-call(s32[4]{0:T(128)} %pad_add_fusion.meta, bf16[2,512,1024]{2,1,0:T(8,128)(2,1)} %copy-done.1, bf16[2,512,1024]{2,1,0:T(8,128)(2,1)} %collective-permute-done.3.sib_ref, bf16[1024,512]{1,0:T(8,128)(2,1)} %wq.1, bf16[1024,256]{1,0:T(8,128)(2,1)} %wk.1, ...), custom_call_target="tpu_custom_call" | custom-call | flops 1610612736 | bytes 4194304 | tf_op jit(solution)/shard_map/expert_project/pallas_call | solution.py:381
  39.8 1.6 collective-permute-start.9
  46.1 2.2 collective-permute-start.13
  48.4 8.5 %project_kv.1.kv_ref = bf16[1024,256]{1,0:T(8,128)(2,1)} custom-call(bf16[4,512,1280]{2,1,0:T(8,128)(2,1)} %normalise.1.own_ref, bf16[4,512,1280]{2,1,0:T(8,128)(2,1)} %collective-permute-done.6.sib_ref, bf16[1280,256]{1,0:T(8,128)(2,1)} %copy-done.10, bf16[1280,256]{1,0:T(8,128)(2,1)} %collective-permute-done.4.w1, ...), custom_call_target="tpu_custom_call" | custom-call | flops 2684354560 | bytes 10485760 | tf_op jit(solution)/shard_map/project_kv/pallas_call | solution.py:277
  56.9 13.7 %expert_attend.1 = (bf16[1024,256]{1,0:T(8,128)(2,1)}, bf16[1024,512]{1,0:T(8,128)(2,1)}) custom-call(s32[28]{0:T(128)} %concatenate.23.meta, bf16[1024,512]{1,0:T(8,128)(2,1)} %get-tuple-element.57.proj_ref, bf16[1024,256]{1,0:T(8,128)(2,1)} %get-tuple-element.59.dctx_ref, bf16[1024,256]{1,0:T(8,128)(2,1)} %project_kv.1.kv_ref), custom_call_target="tpu_custom_call" | custom-call | flops 3355443200 | bytes 4194304 | tf_op jit(solution)/shard_map/expert_attend/pallas_call | solution.py:466
  70.6 7.9 %collective-permute-done.11 = bf16[256,640]{1,0:T(8,128)(2,1)S(1)} collective-permute-done((bf16[256,640]{1,0:T(8,128)(2,1)S(1)}, bf16[256,640]{1,0:T(8,128)(2,1)S(1)}, u32[]{:S(2)}, u32[]{:S(2)}) %collective-permute-start.11) | collective-permute-done | bytes 327712 | tf_op jit(solution)/shard_map/ppermute | solution.py:715
  78.5 7.2 %collective-permute-done.12 = bf16[256,640]{1,0:T(8,128)(2,1)S(1)} collective-permute-done((bf16[256,640]{1,0:T(8,128)(2,1)S(1)}, bf16[256,640]{1,0:T(8,128)(2,1)S(1)}, u32[]{:S(2)}, u32[]{:S(2)}) %collective-permute-start.12) | collective-permute-done | bytes 327712 | tf_op jit(solution)/shard_map/ppermute | solution.py:715
  90.2 3.7 %collective-permute-start.20 = (bf16[256,640]{1,0:T(8,128)(2,1)S(1)}, bf16[256,640]{1,0:T(8,128)(2,1)S(1)}, u32[]{:S(2)}, u32[]{:S(2)}) collective-permute-start(bf16[256,640]{1,0:T(8,128)(2,1)S(1)} %get-tuple-element.99), channel_id=1, source_target_pairs={{0,3},{1,0},{2,1},{3,2},{4,7},{5,4},{6,5},{7,6},{8,11},{9,8},{10,9... | collective-permute-start | bytes 983048 | tf_op jit(solution)/shard_map/ppermute | solution.py:785
  94.9 7.3 %weight_grads.1 = (f32[2,128,768]{2,1,0:T(8,128)}, f32[2,128,768]{2,1,0:T(8,128)}, f32[2,128,768]{2,1,0:T(8,128)}, f32[2,128,768]{2,1,0:T(8,128)}) custom-call(s32[4]{0:T(128)} %pad_add_fusion.meta, bf16[2,512,1024]{2,1,0:T(8,128)(2,1)} %copy-done.1, bf16[2,512,1024]{2,1,0:T(8,128)(2,1)} %collective-permute-done.3.sib_ref, ...), custom_call_target="tpu_custom_call" | custom-call | flops 1610612736 | bytes 12582912 | tf_op jit(solution)/shard_map/weight_grads/pallas_call | solution.py:521
  103.3 1.8 collective-permute-done.14.wx
  105.1 17.2 %attend.1 = (bf16[512,512]{1,0:T(8,128)(2,1)}, bf16[512,512]{1,0:T(8,128)(2,1)}) custom-call(s32[28]{0:T(128)} %concatenate.23.meta, bf16[4,512,1280]{2,1,0:T(8,128)(2,1)} %normalise.1.own_ref, bf16[4,512,1280]{2,1,0:T(8,128)(2,1)} %collective-permute-done.6.sib_ref, bf16[1280,512]{1,0:T(8,128)(2,1)} %copy-done.13, ...), custom_call_target="tpu_custom_call" | custom-call | flops 10737418240 | bytes 10485760 | tf_op jit(solution)/shard_map/attend/pallas_call | solution.py:334
  123.4 2.0 collective-permute-start.24
  125.5 2.4 collective-permute-start.25
  129.1 6.1 %collective-permute-done.24 = f32[128,768]{1,0:T(8,128)S(1)} collective-permute-done((f32[128,768]{1,0:T(8,128)S(1)}, f32[128,768]{1,0:T(8,128)S(1)}, u32[]{:S(2)}, u32[]{:S(2)}) %collective-permute-start.24) | collective-permute-done | bytes 393248 | tf_op jit(solution)/shard_map/ppermute | solution.py:715
  135.2 2.3 collective-permute-done.25
  137.4 1.7 collective-permute-start.26
  139.5 15.5 %collective-permute-done.22.refs_1_.c1 = bf16[512,1024]{1,0:T(8,128)(2,1)S(1)} collective-permute-done((bf16[512,1024]{1,0:T(8,128)(2,1)S(1)}, bf16[512,1024]{1,0:T(8,128)(2,1)S(1)}, u32[]{:S(2)}, u32[]{:S(2)}) %collective-permute-start.22) | collective-permute-done | bytes 1048608 | tf_op jit(solution)/shard_map/ppermute | solution.py:797
  156.1 11.8 %collective-permute-done.26.refs_4_.refs_1_ = bf16[4,256,640]{2,1,0:T(8,128)(2,1)S(1)} collective-permute-done((bf16[4,256,640]{2,1,0:T(8,128)(2,1)S(1)}, bf16[4,256,640]{2,1,0:T(8,128)(2,1)S(1)}, u32[]{:S(2)}, u32[]{:S(2)}) %collective-permute-start.26) | collective-permute-done | bytes 1310752 | tf_op jit(solution)/shard_map/ppermute | solution.py:715
  170.5 16.2 %collective-permute-done.32.refs_1_ = f32[2,128,768]{2,1,0:T(8,128)S(1)} collective-permute-done((f32[2,128,768]{2,1,0:T(8,128)S(1)}, f32[2,128,768]{2,1,0:T(8,128)S(1)}, u32[]{:S(2)}, u32[]{:S(2)}) %collective-permute-start.32) | collective-permute-done | bytes 786464 | tf_op jit(solution)/shard_map/ppermute | solution.py:715
  189.9 11.6 %collective-permute-done.35.refs_4_ = bf16[2,256,640]{2,1,0:T(8,128)(2,1)S(1)} collective-permute-done((bf16[2,256,640]{2,1,0:T(8,128)(2,1)S(1)}, bf16[2,256,640]{2,1,0:T(8,128)(2,1)S(1)}, u32[]{:S(2)}, u32[]{:S(2)}) %collective-permute-start.35) | collective-permute-done | bytes 655392 | tf_op jit(solution)/shard_map/ppermute | solution.py:715
  202.9 1.8 collective-permute-start.39
  206.1 7.9 %collective-permute-done.39.refs_1_ = f32[128,768]{1,0:T(8,128)} collective-permute-done((f32[128,768]{1,0:T(8,128)S(1)}, f32[128,768]{1,0:T(8,128)}, u32[]{:S(2)}, u32[]{:S(2)}) %collective-permute-start.39) | collective-permute-done | bytes 393248 | tf_op jit(solution)/shard_map/ppermute | solution.py:715
  215.5 10.3 %output_near.1.sum_ref = f32[512,1280]{1,0:T(8,128)} custom-call(s32[4]{0:T(128)} %pad_add_fusion.meta, bf16[512,5120]{1,0:T(8,128)(2,1)} %bitcast.48, bf16[512,1024]{1,0:T(8,128)(2,1)} %copy-done.4, bf16[512,1024]{1,0:T(8,128)(2,1)} %copy-done.8, bf16[512,1024]{1,0:T(8,128)(2,1)} %collective-permute-done.23.refs_2_.c2, bf16[4,256,640]{2,1,0:T(8,128)(2,1)} %copy-done, ...), custom_call_target="tpu_custom_call" | custom-call | flops 4026531840 | bytes 20971520 | tf_op jit(solution)/shard_map/output_near/pallas_call | solution.py:630
  225.8 6.2 %place_grads.2 = (f32[1024,512]{1,0:T(8,128)}, f32[1024,256]{1,0:T(8,128)}, f32[1024,256]{1,0:T(8,128)}, f32[512,1024]{1,0:T(8,128)}) custom-call(s32[4]{0:T(128)} %pad_add_fusion.meta, f32[2,128,768]{2,1,0:T(8,128)} %copy-done.9, f32[2,128,768]{2,1,0:T(8,128)} %copy-done.11, f32[2,128,768]{2,1,0:T(8,128)} %copy-done.12, f32[2,128,768]{2,1,0:T(8,128)} %copy-done.18, ...), custom_call_target="tpu_custom_call" | custom-call | bytes 9437184 | tf_op jit(solution)/shard_map/place_grads/pallas_call | solution.py:579
  233.0 8.7 %output_far.1 = bf16[512,1280]{1,0:T(8,128)(2,1)} custom-call(s32[4]{0:T(128)} %pad_add_fusion.meta, f32[512,1280]{1,0:T(8,128)} %output_near.1.sum_ref, bf16[512,1024]{1,0:T(8,128)(2,1)} %copy-done.4, bf16[512,1024]{1,0:T(8,128)(2,1)} %copy-done.8, bf16[512,1024]{1,0:T(8,128)(2,1)} %collective-permute-done.23.refs_2_.c2, bf16[512,1024]{1,0:T(8,128)(2,1)} %copy-done.15, ...), custom_call_target="tpu_custom_call" | custom-call | flops 2348810240 | bytes 5242880 | tf_op jit(solution)/shard_map/output_far/pallas_call | solution.py:673
  241.8 3.3 %place_grads.3 = (f32[1024,512]{1,0:T(8,128)}, f32[1024,256]{1,0:T(8,128)}, f32[1024,256]{1,0:T(8,128)}, f32[512,1024]{1,0:T(8,128)}) custom-call(s32[4]{0:T(128)} %pad_add_fusion.meta, f32[128,768]{1,0:T(8,128)} %collective-permute-done.38.refs_0_, ...), custom_call_target="tpu_custom_call", output_to_operand_aliasing={{0}: (5, {}), {1}: (6, {}), {2}: (7, {}), {3}: (8, {})} | custom-call | bytes 3145728 | tf_op jit(solution)/shard_map/place_grads/pallas_call | solution.py:579
  (166 shorter events, 35.9 us)
Async XLA Ops:
  7.7 18.0 %collective-permute-start.4 = (bf16[1280,256]{1,0:T(8,128)(2,1)S(1)}, bf16[1280,256]{1,0:T(8,128)(2,1)}, u32[]{:S(2)}, u32[]{:S(2)}) collective-permute-start(bf16[1280,256]{1,0:T(8,128)(2,1)S(1)} %pad_maximum_fusion.5.w0), channel_id=1, source_target_pairs={{0,8},{4,12},{8,0},{12,4},{16,24},{20,28},{24,16},{28,20},{1,9},{5... | collective-permute-start | bytes 1966088 | tf_op jit(solution)/shard_map/ppermute | solution.py:715
  10.2 17.0 %collective-permute-start.5 = (bf16[1280,256]{1,0:T(8,128)(2,1)S(1)}, bf16[1280,256]{1,0:T(8,128)(2,1)}, u32[]{:S(2)}, u32[]{:S(2)}) collective-permute-start(bf16[1280,256]{1,0:T(8,128)(2,1)S(1)} %pad_maximum_fusion.5.w0), channel_id=1, source_target_pairs={{0,16},{4,20},{8,24},{12,28},{16,0},{20,4},{24,8},{28,12},{1,17},{... | collective-permute-start | bytes 1966088 | tf_op jit(solution)/shard_map/ppermute | solution.py:715
  27.1 12.7 %collective-permute-start.6 = (bf16[4,512,1280]{2,1,0:T(8,128)(2,1)}, bf16[4,512,1280]{2,1,0:T(8,128)(2,1)}, u32[]{:S(2)}, u32[]{:S(2)}) collective-permute-start(bf16[4,512,1280]{2,1,0:T(8,128)(2,1)} %normalise.1.own_ref), channel_id=1, source_target_pairs={{0,4},{4,0},{8,12},{12,8},{16,20},{20,16},{24,28},{28,24},{1,5},{5... | collective-permute-start | bytes 15728648 | tf_op jit(solution)/shard_map/ppermute | solution.py:715
  39.8 46.0 %collective-permute-start.9 = (bf16[1280,512]{1,0:T(8,128)(2,1)S(1)}, bf16[1280,512]{1,0:T(8,128)(2,1)}, u32[]{:S(2)}, u32[]{:S(2)}) collective-permute-start(bf16[1280,512]{1,0:T(8,128)(2,1)S(1)} %pad_maximum_fusion.1.w0), channel_id=1, source_target_pairs={{0,8},{4,12},{8,0},{12,4},{16,24},{20,28},{24,16},{28,20},{1,9},{5... | collective-permute-start | bytes 3932168 | tf_op jit(solution)/shard_map/ppermute | solution.py:715
  41.4 45.5 %collective-permute-start.10 = (bf16[1280,512]{1,0:T(8,128)(2,1)S(1)}, bf16[1280,512]{1,0:T(8,128)(2,1)}, u32[]{:S(2)}, u32[]{:S(2)}) collective-permute-start(bf16[1280,512]{1,0:T(8,128)(2,1)S(1)} %pad_maximum_fusion.1.w0), channel_id=1, source_target_pairs={{0,16},{4,20},{8,24},{12,28},{16,0},{20,4},{24,8},{28,12},{1,17},{... | collective-permute-start | bytes 3932168 | tf_op jit(solution)/shard_map/ppermute | solution.py:715
  44.8 33.7 %collective-permute-start.11 = (bf16[256,640]{1,0:T(8,128)(2,1)S(1)}, bf16[256,640]{1,0:T(8,128)(2,1)S(1)}, u32[]{:S(2)}, u32[]{:S(2)}) collective-permute-start(bf16[256,640]{1,0:T(8,128)(2,1)S(1)} %get-tuple-element.105), channel_id=1, source_target_pairs={{0,8},{4,12},{8,0},{12,4},{16,24},{20,28},{24,16},{28,20},{1,9},{5... | collective-permute-start | bytes 983048 | tf_op jit(solution)/shard_map/ppermute | solution.py:715
  45.4 40.3 %collective-permute-start.12 = (bf16[256,640]{1,0:T(8,128)(2,1)S(1)}, bf16[256,640]{1,0:T(8,128)(2,1)S(1)}, u32[]{:S(2)}, u32[]{:S(2)}) collective-permute-start(bf16[256,640]{1,0:T(8,128)(2,1)S(1)} %get-tuple-element.104), channel_id=1, source_target_pairs={{0,16},{4,20},{8,24},{12,28},{16,0},{20,4},{24,8},{28,12},{1,17},{... | collective-permute-start | bytes 983048 | tf_op jit(solution)/shard_map/ppermute | solution.py:715
  46.1 39.6 %collective-permute-start.13 = (bf16[256,640]{1,0:T(8,128)(2,1)S(1)}, bf16[256,640]{1,0:T(8,128)(2,1)S(1)}, u32[]{:S(2)}, u32[]{:S(2)}) collective-permute-start(bf16[256,640]{1,0:T(8,128)(2,1)S(1)} %get-tuple-element.103), channel_id=1, source_target_pairs={{0,24},{4,28},{8,16},{12,20},{16,8},{20,12},{24,0},{28,4},{1,25},{... | collective-permute-start | bytes 983048 | tf_op jit(solution)/shard_map/ppermute | solution.py:715
  86.9 15.3 %collective-permute-start.15 = (bf16[640,512]{1,0:T(8,128)(2,1)S(1)}, bf16[640,512]{1,0:T(8,128)(2,1)}, u32[]{:S(2)}, u32[]{:S(2)}) collective-permute-start(bf16[640,512]{1,0:T(8,128)(2,1)S(1)} %slice.51), channel_id=1, source_target_pairs={{0,16},{4,20},{8,24},{12,28},{16,0},{20,4},{24,8},{28,12},{1,17},{... | collective-permute-start | bytes 1966088 | tf_op jit(solution)/shard_map/ppermute | solution.py:715
  88.9 16.2 %collective-permute-start.14 = (bf16[640,512]{1,0:T(8,128)(2,1)S(1)}, bf16[640,512]{1,0:T(8,128)(2,1)}, u32[]{:S(2)}, u32[]{:S(2)}) collective-permute-start(bf16[640,512]{1,0:T(8,128)(2,1)S(1)} %slice.50), channel_id=1, source_target_pairs={{0,8},{4,12},{8,0},{12,4},{16,24},{20,28},{24,16},{28,20},{1,9},{5... | collective-permute-start | bytes 1966088 | tf_op jit(solution)/shard_map/ppermute | solution.py:715
  90.2 32.1 %collective-permute-start.20 = (bf16[256,640]{1,0:T(8,128)(2,1)S(1)}, bf16[256,640]{1,0:T(8,128)(2,1)S(1)}, u32[]{:S(2)}, u32[]{:S(2)}) collective-permute-start(bf16[256,640]{1,0:T(8,128)(2,1)S(1)} %get-tuple-element.99), channel_id=1, source_target_pairs={{0,3},{1,0},{2,1},{3,2},{4,7},{5,4},{6,5},{7,6},{8,11},{9,8},{10,9... | collective-permute-start | bytes 983048 | tf_op jit(solution)/shard_map/ppermute | solution.py:785
  93.9 28.5 %collective-permute-start.19 = (bf16[256,640]{1,0:T(8,128)(2,1)S(1)}, bf16[256,640]{1,0:T(8,128)(2,1)S(1)}, u32[]{:S(2)}, u32[]{:S(2)}) collective-permute-start(bf16[256,640]{1,0:T(8,128)(2,1)S(1)} %get-tuple-element.100), channel_id=1, source_target_pairs={{0,2},{1,3},{2,0},{3,1},{4,6},{5,7},{6,4},{7,5},{8,10},{9,11},{10,... | collective-permute-start | bytes 983048 | tf_op jit(solution)/shard_map/ppermute | solution.py:785
  93.9 28.5 %collective-permute-start.18 = (bf16[256,640]{1,0:T(8,128)(2,1)S(1)}, bf16[256,640]{1,0:T(8,128)(2,1)S(1)}, u32[]{:S(2)}, u32[]{:S(2)}) collective-permute-start(bf16[256,640]{1,0:T(8,128)(2,1)S(1)} %get-tuple-element.101), channel_id=1, source_target_pairs={{0,1},{1,2},{2,3},{3,0},{4,5},{5,6},{6,7},{7,4},{8,9},{9,10},{10,1... | collective-permute-start | bytes 983048 | tf_op jit(solution)/shard_map/ppermute | solution.py:785
  102.2 20.2 %collective-permute-start.16 = (f32[2,128,768]{2,1,0:T(8,128)}, f32[2,128,768]{2,1,0:T(8,128)S(1)}, u32[]{:S(2)}, u32[]{:S(2)}) collective-permute-start(f32[2,128,768]{2,1,0:T(8,128)} %get-tuple-element.66), channel_id=1, source_target_pairs={{0,8},{4,12},{8,0},{12,4},{16,24},{20,28},{24,16},{28,20},{1,9},{5... | collective-permute-start | bytes 2359304 | tf_op jit(solution)/shard_map/ppermute | solution.py:715
  105.1 17.3 %collective-permute-start.17 = (f32[2,128,768]{2,1,0:T(8,128)}, f32[2,128,768]{2,1,0:T(8,128)S(1)}, u32[]{:S(2)}, u32[]{:S(2)}) collective-permute-start(f32[2,128,768]{2,1,0:T(8,128)} %get-tuple-element.71), channel_id=1, source_target_pairs={{0,16},{4,20},{8,24},{12,28},{16,0},{20,4},{24,8},{28,12},{1,17},{... | collective-permute-start | bytes 2359304 | tf_op jit(solution)/shard_map/ppermute | solution.py:715
  128.1 27.0 %collective-permute-start.22 = (bf16[512,1024]{1,0:T(8,128)(2,1)S(1)}, bf16[512,1024]{1,0:T(8,128)(2,1)S(1)}, u32[]{:S(2)}, u32[]{:S(2)}) collective-permute-start(bf16[512,1024]{1,0:T(8,128)(2,1)S(1)} %constant_dynamic-update-slice_fusion.refs_0_.c0), channel_id=1, source_target_pairs={{0,1},{1,2},{2,3},{3,0},{4,5},{5,6},{6,7},{7,4},{8,9},{9,10},{10,1... | collective-permute-start | bytes 3145736 | tf_op jit(solution)/shard_map/ppermute | solution.py:797
  137.4 30.4 %collective-permute-start.26 = (bf16[4,256,640]{2,1,0:T(8,128)(2,1)S(1)}, bf16[4,256,640]{2,1,0:T(8,128)(2,1)S(1)}, u32[]{:S(2)}, u32[]{:S(2)}) collective-permute-start(bf16[4,256,640]{2,1,0:T(8,128)(2,1)S(1)} %pad_maximum_fusion.3.refs_3_.refs_0_), channel_id=1, source_target_pairs={{0,8},{4,12},{8,0},{12,4},{16,24},{20,28},{24,16},{28,20},{1,9},{5... | collective-permute-start | bytes 3932168 | tf_op jit(solution)/shard_map/ppermute | solution.py:715
  139.2 29.8 %collective-permute-start.27 = (bf16[4,256,640]{2,1,0:T(8,128)(2,1)S(1)}, bf16[4,256,640]{2,1,0:T(8,128)(2,1)S(1)}, u32[]{:S(2)}, u32[]{:S(2)}) collective-permute-start(bf16[4,256,640]{2,1,0:T(8,128)(2,1)S(1)} %pad_maximum_fusion.3.refs_3_.refs_0_), channel_id=1, source_target_pairs={{0,16},{4,20},{8,24},{12,28},{16,0},{20,4},{24,8},{28,12},{1,17},{... | collective-permute-start | bytes 3932168 | tf_op jit(solution)/shard_map/ppermute | solution.py:715
  155.0 34.4 %collective-permute-start.23 = (bf16[512,1024]{1,0:T(8,128)(2,1)S(1)}, bf16[512,1024]{1,0:T(8,128)(2,1)}, u32[]{:S(2)}, u32[]{:S(2)}) collective-permute-start(bf16[512,1024]{1,0:T(8,128)(2,1)S(1)} %collective-permute-done.22.refs_1_.c1), channel_id=1, source_target_pairs={{0,1},{1,2},{2,3},{3,0},{4,5},{5,6},{6,7},{7,4},{8,9},{9,10},{10,1... | collective-permute-start | bytes 3145736 | tf_op jit(solution)/shard_map/ppermute | solution.py:797
  169.0 17.8 %collective-permute-start.32 = (f32[2,128,768]{2,1,0:T(8,128)S(1)}, f32[2,128,768]{2,1,0:T(8,128)S(1)}, u32[]{:S(2)}, u32[]{:S(2)}) collective-permute-start(f32[2,128,768]{2,1,0:T(8,128)S(1)} %pad_maximum_fusion.4.refs_0_), channel_id=1, source_target_pairs={{0,8},{4,12},{8,0},{12,4},{16,24},{20,28},{24,16},{28,20},{1,9},{5... | collective-permute-start | bytes 2359304 | tf_op jit(solution)/shard_map/ppermute | solution.py:715
  169.6 17.8 %collective-permute-start.33 = (f32[2,128,768]{2,1,0:T(8,128)S(1)}, f32[2,128,768]{2,1,0:T(8,128)S(1)}, u32[]{:S(2)}, u32[]{:S(2)}) collective-permute-start(f32[2,128,768]{2,1,0:T(8,128)S(1)} %pad_maximum_fusion.4.refs_0_), channel_id=1, source_target_pairs={{0,16},{4,20},{8,24},{12,28},{16,0},{20,4},{24,8},{28,12},{1,17},{... | collective-permute-start | bytes 2359304 | tf_op jit(solution)/shard_map/ppermute | solution.py:715
  170.0 19.4 %collective-permute-start.42 = (f32[2,128,768]{2,1,0:T(8,128)S(1)}, f32[2,128,768]{2,1,0:T(8,128)S(1)}, u32[]{:S(2)}, u32[]{:S(2)}) collective-permute-start(f32[2,128,768]{2,1,0:T(8,128)S(1)} %pad_maximum_fusion.4.refs_0_), channel_id=1, source_target_pairs={{0,4},{4,0},{8,12},{12,8},{16,20},{20,16},{24,28},{28,24},{1,5},{5... | collective-permute-start | bytes 2359304 | tf_op jit(solution)/shard_map/ppermute | solution.py:715
  170.0 32.1 %collective-permute-start.28 = (bf16[4,256,640]{2,1,0:T(8,128)(2,1)S(1)}, bf16[4,256,640]{2,1,0:T(8,128)(2,1)S(1)}, u32[]{:S(2)}, u32[]{:S(2)}) collective-permute-start(bf16[4,256,640]{2,1,0:T(8,128)(2,1)S(1)} %pad_maximum_fusion.3.refs_3_.refs_0_), channel_id=1, source_target_pairs={{0,4},{4,0},{8,12},{12,8},{16,20},{20,16},{24,28},{28,24},{1,5},{5... | collective-permute-start | bytes 3932168 | tf_op jit(solution)/shard_map/ppermute | solution.py:715
  187.4 14.1 %collective-permute-start.35 = (bf16[2,256,640]{2,1,0:T(8,128)(2,1)S(1)}, bf16[2,256,640]{2,1,0:T(8,128)(2,1)S(1)}, u32[]{:S(2)}, u32[]{:S(2)}) collective-permute-start(bf16[2,256,640]{2,1,0:T(8,128)(2,1)S(1)} %slice.57), channel_id=1, source_target_pairs={{0,16},{4,20},{8,24},{12,28},{16,0},{20,4},{24,8},{28,12},{1,17},{... | collective-permute-start | bytes 1966088 | tf_op jit(solution)/shard_map/ppermute | solution.py:715
  188.0 14.0 %collective-permute-start.34 = (bf16[2,256,640]{2,1,0:T(8,128)(2,1)S(1)}, bf16[2,256,640]{2,1,0:T(8,128)(2,1)}, u32[]{:S(2)}, u32[]{:S(2)}) collective-permute-start(bf16[2,256,640]{2,1,0:T(8,128)(2,1)S(1)} %slice.56), channel_id=1, source_target_pairs={{0,8},{4,12},{8,0},{12,4},{16,24},{20,28},{24,16},{28,20},{1,9},{5... | collective-permute-start | bytes 1966088 | tf_op jit(solution)/shard_map/ppermute | solution.py:715
  189.4 13.5 %collective-permute-start.29 = (bf16[4,256,640]{2,1,0:T(8,128)(2,1)S(1)}, bf16[4,256,640]{2,1,0:T(8,128)(2,1)S(1)}, u32[]{:S(2)}, u32[]{:S(2)}) collective-permute-start(bf16[4,256,640]{2,1,0:T(8,128)(2,1)S(1)} %collective-permute-done.26.refs_4_.refs_1_), channel_id=1, source_target_pairs={{0,4},{4,0},{8,12},{12,8},{16,20},{20,16},{24,28},{28,24},{1,5},{5... | collective-permute-start | bytes 3932168 | tf_op jit(solution)/shard_map/ppermute | solution.py:715
  189.5 15.2 %collective-permute-start.30 = (bf16[4,256,640]{2,1,0:T(8,128)(2,1)S(1)}, bf16[4,256,640]{2,1,0:T(8,128)(2,1)S(1)}, u32[]{:S(2)}, u32[]{:S(2)}) collective-permute-start(bf16[4,256,640]{2,1,0:T(8,128)(2,1)S(1)} %collective-permute-done.27.refs_5_.refs_2_), channel_id=1, source_target_pairs={{0,4},{4,0},{8,12},{12,8},{16,20},{20,16},{24,28},{28,24},{1,5},{5... | collective-permute-start | bytes 3932168 | tf_op jit(solution)/shard_map/ppermute | solution.py:715
  202.1 29.9 %collective-permute-start.31 = (bf16[512,1024]{1,0:T(8,128)(2,1)}, bf16[512,1024]{1,0:T(8,128)(2,1)S(1)}, u32[]{:S(2)}, u32[]{:S(2)}) collective-permute-start(bf16[512,1024]{1,0:T(8,128)(2,1)} %collective-permute-done.23.refs_2_.c2), channel_id=1, source_target_pairs={{0,1},{1,2},{2,3},{3,0},{4,5},{5,6},{6,7},{7,4},{8,9},{9,10},{10,1... | collective-permute-start | bytes 3145736 | tf_op jit(solution)/shard_map/ppermute | solution.py:797
  205.5 26.6 %collective-permute-start.37 = (bf16[2,256,640]{2,1,0:T(8,128)(2,1)S(1)}, bf16[2,256,640]{2,1,0:T(8,128)(2,1)}, u32[]{:S(2)}, u32[]{:S(2)}) collective-permute-start(bf16[2,256,640]{2,1,0:T(8,128)(2,1)S(1)} %collective-permute-done.35.refs_4_), channel_id=1, source_target_pairs={{0,4},{4,0},{8,12},{12,8},{16,20},{20,16},{24,28},{28,24},{1,5},{5... | collective-permute-start | bytes 1966088 | tf_op jit(solution)/shard_map/ppermute | solution.py:715
  205.6 26.5 %collective-permute-start.36 = (bf16[2,256,640]{2,1,0:T(8,128)(2,1)}, bf16[2,256,640]{2,1,0:T(8,128)(2,1)}, u32[]{:S(2)}, u32[]{:S(2)}) collective-permute-start(bf16[2,256,640]{2,1,0:T(8,128)(2,1)} %collective-permute-done.34.refs_3_), channel_id=1, source_target_pairs={{0,4},{4,0},{8,12},{12,8},{16,20},{20,16},{24,28},{28,24},{1,5},{5... | collective-permute-start | bytes 1966088 | tf_op jit(solution)/shard_map/ppermute | solution.py:715
  214.0 27.7 %collective-permute-start.41 = (f32[128,768]{1,0:T(8,128)}, f32[128,768]{1,0:T(8,128)}, u32[]{:S(2)}, u32[]{:S(2)}) collective-permute-start(f32[128,768]{1,0:T(8,128)} %collective-permute-done.39.refs_1_), channel_id=1, source_target_pairs={{0,4},{4,0},{8,12},{12,8},{16,20},{20,16},{24,28},{28,24},{1,5},{5... | collective-permute-start | bytes 1179656 | tf_op jit(solution)/shard_map/ppermute | solution.py:715
  215.5 26.3 %collective-permute-start.40 = (f32[128,768]{1,0:T(8,128)}, f32[128,768]{1,0:T(8,128)}, u32[]{:S(2)}, u32[]{:S(2)}) collective-permute-start(f32[128,768]{1,0:T(8,128)} %collective-permute-done.38.refs_0_), channel_id=1, source_target_pairs={{0,4},{4,0},{8,12},{12,8},{16,20},{20,16},{24,28},{28,24},{1,5},{5... | collective-permute-start | bytes 1179656 | tf_op jit(solution)/shard_map/ppermute | solution.py:715
  (44 other events, 499.2 us)

commit v3 on v2

--- a/solution.py
+++ b/solution.py
@@ -177,10 +177,11 @@
 NEG = -1e30
 PAD = 64
 HIGH = 56 * 1024 * 1024
-
-
-def params():
-    return pltpu.CompilerParams(vmem_limit_bytes=HIGH)
+LOW = 32 * 1024 * 1024
+
+
+def params(limit=HIGH):
+    return pltpu.CompilerParams(vmem_limit_bytes=limit)
 
 
 def cost(flops, moved):
@@ -482,7 +483,7 @@
             jax.ShapeDtypeStruct((rows, width), jnp.bfloat16),
             jax.ShapeDtypeStruct((rows, columns), jnp.bfloat16),
         ],
-        compiler_params=params(),
+        compiler_params=params(LOW),
         cost_estimate=cost(40 * rows * 320 * width, 8 * rows * columns),
         name="expert_attend",
     )(meta, proj, dctx, kv)
@@ -527,7 +528,7 @@
             out_specs=[pl.BlockSpec((1, tall, columns), lambda i, m: (i, 0, 0))] * 4,
         ),
         out_shape=[out] * 4,
-        compiler_params=params(),
+        compiler_params=params(LOW),
         cost_estimate=cost(4 * rows * width * columns, 16 * width * columns),
         name="weight_grads",
     )(meta, own, sib, ctx, grad)
@@ -586,7 +587,7 @@
         ),
         out_shape=[jax.ShapeDtypeStruct(s, jnp.float32) for s in shapes],
         input_output_aliases={1 + inputs + n: n for n in range(len(into))},
-        compiler_params=params(),
+        compiler_params=params(LOW),
         cost_estimate=cost(0, size * 2 * sum(s[0] * s[1] for s in shapes)),
         name="place_grads",
     )(meta, *own, *sib, *into)
@@ -637,7 +638,7 @@
             out_specs=pl.BlockSpec((count, half), lambda i, m: (0, m[1] ^ i)),
         ),
         out_shape=jax.ShapeDtypeStruct((count, 2 * half), jnp.float32),
-        compiler_params=params(),
+        compiler_params=params(LOW),
         cost_estimate=cost(12 * count * wide * half, 32 * wide * half),
         name="output_near",
     )(meta, flat, *contexts, *own[:3], *sib[:3])
@@ -681,7 +682,7 @@
             out_specs=pl.BlockSpec((count, half), lambda i, m: (0, m[1] ^ i)),
         ),
         out_shape=jax.ShapeDtypeStruct((count, columns), jnp.bfloat16),
-        compiler_params=params(),
+        compiler_params=params(LOW),
         cost_estimate=cost(4 * count * 7 * quarter * half, 8 * count * columns),
         name="output_far",
     )(meta, near, *contexts, *own, *sib)
@@ -753,8 +754,8 @@
     pair = jnp.stack([jnp.pad(action_tokens, pad), jnp.pad(action_cot, pad)])
     pair = pair.reshape(2, spans * PAD, action_tokens.shape[2])
     pair_sib = swap(after(pair, kv_shard))
-    normed = normalise(chip_meta, after(flat, q_got, pair_sib), 4)
-    normed_sib = swap(after(normed, kv_x, kv_y))
+    normed = normalise(chip_meta, after(flat, q_other, pair), 4)
+    normed_sib = swap(after(normed, kv_x, kv_y, q_got, pair_sib))
     half = kv_x.shape[0] // 2
     low, high = kv_y[:half], kv_x[half:]
     kv_dx, kv_dy = over_x(low), over_y(high)
@@ -805,8 +806,8 @@
     from_x, from_y = over_x(sent), over_y(sent)
     ctx_2 = turn(ctx_1)
     wo_sib = [swap(after(wo, wo_x)), swap(wo_x), swap(wo_y)]
-    wo_dx = over_x(after(wo_y, from_x, from_y)[:2])
-    wo_dy = over_y(after(wo_x, from_x, from_y)[2:])
+    wo_dx = over_x(after(wo_y, from_x, from_y, wo_sib[0])[:2])
+    wo_dy = over_y(after(wo_x, from_x, from_y, wo_sib[0])[2:])
     ctx_3 = turn(ctx_2)
     near = output_near(chip_meta, flat, (ctx_rows, ctx_1, ctx_2), (wo, wo_x, wo_y), wo_sib)
     far_x = over_x(after(from_y, wo_dx, wo_dy)[0])

time: 246 us -> 241 us (0.980)
  Pallas kernels: 89.6 us -> 72.2 us
  waiting for transfers between devices: 101 us -> 109 us
  other arithmetic: 2.97 us -> 6.12 us
    ppermute x39, waiting for transfers between devices: 85.5 us -> 104 us  [across(): return lambda x: lax.ppermute(x, 'dp', [(i, i ^ mask) for i in range(8)])]
    ppermute x3, waiting for transfers between devices: 15.5 us -> 4.55 us  [plane_body(): lax.ppermute(x, 'tensor', [(i, (i + 1) % 4) for i in range(4)])]
    pallas_call x1, Pallas kernels: 10.3 us -> 4.97 us  [output_near(): pl.pallas_call(near_kernel, grid_spec=pltpu.PrefetchScalarGridSpec(num_sc...]
    pallas_call x2, Pallas kernels: 9.51 us -> 5.57 us  [place_grads(): pl.pallas_call(functools.partial(place_kernel, tuple(pieces), len(own)),...]
    pallas_call x1, Pallas kernels: 8.71 us -> 4.86 us  [output_far(): pl.pallas_call(far_kernel, grid_spec=pltpu.PrefetchScalarGridSpec(num_sca...]
    ppermute x3, starting transfers between devices: 1.38 us -> 4.79 us  [plane_body(): lax.ppermute(x, 'tensor', [(i, (i + 1) % 4) for i in range(4)])]
    ppermute x39, starting transfers between devices: 30.6 us -> 27.5 us  [across(): return lambda x: lax.ppermute(x, 'dp', [(i, i ^ mask) for i in range(8)])]
    unnamed x65 -> x49, local copies, waits for them, and re-layouts: 4.09 us -> 4.99 us
  transfers between devices with their start and end apart: 45 -> 45, of which waited for: 17 -> 20; matrix products, arithmetic and copies ran while one was open for 5% -> 6% of each run, Pallas kernels for 35% -> 29%
where the time goes in v3:
time: 241 us; the launch traced here: 240 us
  waiting for transfers between devices  109 us (45%)
  Pallas kernels  72.2 us (30%)
  starting transfers between devices  37.1 us (15%)
  local copies, waits for them, and re-layouts  14.8 us (6%)
  other arithmetic  6.12 us (3%)
    ppermute x39, waiting for transfers between devices, across(): return lambda x: lax.ppermute(x, 'dp', [(i, i ^ mask) for i in range(8)])  104 us
    ppermute x39, starting transfers between devices, across(): return lambda x: lax.ppermute(x, 'dp', [(i, i ^ mask) for i in range(8)])  27.5 us
    pallas_call x1, Pallas kernels, attend(): pl.pallas_call(functools.partial(attend_kernel, factor), grid_spec=pltpu....  17.1 us
    pallas_call x1, Pallas kernels, expert_attend(): pl.pallas_call(functools.partial(expert_kernel, factor, spans), grid_spec...  11.6 us
    pallas_call x1, Pallas kernels, project_kv(): pl.pallas_call(kv_kernel, grid=(steps,), in_specs=pair_specs(parts, block...  8.48 us
    pallas_call x1, Pallas kernels, normalise(): pl.pallas_call(norm_kernel, grid_spec=pltpu.PrefetchScalarGridSpec(num_sc...  7.19 us
    pallas_call x1, Pallas kernels, expert_project(): pl.pallas_call(expert_project_kernel, grid_spec=pltpu.PrefetchScalarGridS...  7.17 us
    pallas_call x2, Pallas kernels, place_grads(): pl.pallas_call(functools.partial(place_kernel, tuple(pieces), len(own)),...  5.57 us
  transfers between devices with their start and end apart: 45, of which 20 were waited for; matrix products, arithmetic and copies ran while one was open for 6% of the time, Pallas kernels for 29%

profile of v3, /device:TPU:0, one launch (start us, length us, event | category | flops | bytes accessed | tf_op | source)
XLA Modules:
  0.0 240.3 jit_solution(16970178168531004918)
XLA Ops:
  4.6 2.5 %constant_dynamic-slice_fusion.4 = (bf16[640,512]{1,0:T(8,128)(2,1)S(1)}, bf16[640,512]{1,0:T(8,128)(2,1)}) fusion(bf16[640,1024]{1,0:T(8,128)(2,1)} %param.18, s32[]{:T(128)S(6)} %select_n.55, s32[]{:T(128)S(6)} %select_n.52), kind=kLoop, calls=%fused_computation.27 | loop fusion | bytes 2621448 | tf_op jit(solution)/shard_map/dynamic_slice | solution.py:740
  7.2 3.0 %collective-permute-start.3 = (bf16[1280,256]{1,0:T(8,128)(2,1)S(1)}, bf16[1280,256]{1,0:T(8,128)(2,1)}, u32[]{:S(2)}, u32[]{:S(2)}) collective-permute-start(bf16[1280,256]{1,0:T(8,128)(2,1)S(1)} %pad_maximum_fusion.5.w0), channel_id=1, source_target_pairs={{0,16},{4,20},{8,24},{12,28},{16,0},{20,4},{24,8},{28,12},{1,17},{... | collective-permute-start | bytes 1966088 | tf_op jit(solution)/shard_map/ppermute | solution.py:716
  12.3 7.2 %normalise.1.own_ref = bf16[4,512,1280]{2,1,0:T(8,128)(2,1)} custom-call(s32[4]{0:T(128)} %pad_add_fusion.meta, bf16[512,5120]{1,0:T(8,128)(2,1)} %bitcast.47), custom_call_target="tpu_custom_call" | custom-call | flops 10485760 | bytes 10485760 | tf_op jit(solution)/shard_map/normalise/pallas_call | solution.py:223
  19.5 5.6 %collective-permute-done.3.w2 = bf16[1280,256]{1,0:T(8,128)(2,1)} collective-permute-done((bf16[1280,256]{1,0:T(8,128)(2,1)S(1)}, bf16[1280,256]{1,0:T(8,128)(2,1)}, u32[]{:S(2)}, u32[]{:S(2)}) %collective-permute-start.3) | collective-permute-done | bytes 655392 | tf_op jit(solution)/shard_map/ppermute | solution.py:716
  27.5 1.6 collective-permute-start.7
  30.7 2.2 pad_maximum_fusion.1.w0
  32.9 7.2 %expert_project.1 = (bf16[1024,512]{1,0:T(8,128)(2,1)}, bf16[1024,256]{1,0:T(8,128)(2,1)}) custom-call(s32[4]{0:T(128)} %pad_add_fusion.meta, bf16[2,512,1024]{2,1,0:T(8,128)(2,1)} %copy-done, bf16[2,512,1024]{2,1,0:T(8,128)(2,1)} %collective-permute-done.5.sib_ref, bf16[1024,512]{1,0:T(8,128)(2,1)} %wq.1, bf16[1024,256]{1,0:T(8,128)(2,1)} %wk.1, ...), custom_call_target="tpu_custom_call" | custom-call | flops 1610612736 | bytes 4194304 | tf_op jit(solution)/shard_map/expert_project/pallas_call | solution.py:382
  40.9 1.5 collective-permute-start.10
  44.6 1.5 collective-permute-start.13
  46.1 1.5 collective-permute-start.12
  48.1 8.5 %project_kv.1.kv_ref = bf16[1024,256]{1,0:T(8,128)(2,1)} custom-call(bf16[4,512,1280]{2,1,0:T(8,128)(2,1)} %normalise.1.own_ref, bf16[4,512,1280]{2,1,0:T(8,128)(2,1)} %collective-permute-done.6.sib_ref, bf16[1280,256]{1,0:T(8,128)(2,1)} %copy-done.7, bf16[1280,256]{1,0:T(8,128)(2,1)} %collective-permute-done.2.w1, ...), custom_call_target="tpu_custom_call" | custom-call | flops 2684354560 | bytes 10485760 | tf_op jit(solution)/shard_map/project_kv/pallas_call | solution.py:278
  57.7 11.6 %expert_attend.1 = (bf16[1024,256]{1,0:T(8,128)(2,1)S(1)}, bf16[1024,512]{1,0:T(8,128)(2,1)S(1)}) custom-call(s32[28]{0:T(128)S(1)} %concatenate.23.meta, bf16[1024,512]{1,0:T(8,128)(2,1)S(1)} %copy-done.5, bf16[1024,256]{1,0:T(8,128)(2,1)S(1)} %copy-done.6, bf16[1024,256]{1,0:T(8,128)(2,1)S(1)} %copy-done.2), custom_call_target="tpu_custom_call" | custom-call | flops 3355443200 | bytes 4194304 | tf_op jit(solution)/shard_map/expert_attend/pallas_call | solution.py:467
  69.3 12.0 %collective-permute-done.13 = bf16[256,640]{1,0:T(8,128)(2,1)S(1)} collective-permute-done((bf16[256,640]{1,0:T(8,128)(2,1)S(1)}, bf16[256,640]{1,0:T(8,128)(2,1)S(1)}, u32[]{:S(2)}, u32[]{:S(2)}) %collective-permute-start.13) | collective-permute-done | bytes 327712 | tf_op jit(solution)/shard_map/ppermute | solution.py:716
  81.4 4.4 %collective-permute-done.12 = bf16[256,640]{1,0:T(8,128)(2,1)S(1)} collective-permute-done((bf16[256,640]{1,0:T(8,128)(2,1)S(1)}, bf16[256,640]{1,0:T(8,128)(2,1)S(1)}, u32[]{:S(2)}, u32[]{:S(2)}) %collective-permute-start.12) | collective-permute-done | bytes 327712 | tf_op jit(solution)/shard_map/ppermute | solution.py:716
  93.8 3.7 %collective-permute-start.20 = (bf16[256,640]{1,0:T(8,128)(2,1)}, bf16[256,640]{1,0:T(8,128)(2,1)S(1)}, u32[]{:S(2)}, u32[]{:S(2)}) collective-permute-start(bf16[256,640]{1,0:T(8,128)(2,1)} %get-tuple-element.99), channel_id=1, source_target_pairs={{0,3},{1,0},{2,1},{3,2},{4,7},{5,4},{6,5},{7,6},{8,11},{9,8},{10,9... | collective-permute-start | bytes 983048 | tf_op jit(solution)/shard_map/ppermute | solution.py:786
  98.5 5.2 %weight_grads.1 = (f32[2,128,768]{2,1,0:T(8,128)S(1)}, f32[2,128,768]{2,1,0:T(8,128)S(1)}, f32[2,128,768]{2,1,0:T(8,128)S(1)}, f32[2,128,768]{2,1,0:T(8,128)S(1)}) custom-call(s32[4]{0:T(128)S(1)} %copy-done.3, bf16[2,512,1024]{2,1,0:T(8,128)(2,1)S(1)} %copy-done.1, bf16[2,512,1024]{2,1,0:T(8,128)(2,1)} %collective-permute-done.5.sib_ref, ...), custom_call_target="tpu_custom_call" | custom-call | flops 1610612736 | bytes 12582912 | tf_op jit(solution)/shard_map/weight_grads/pallas_call | solution.py:522
  106.9 17.1 %attend.1 = (bf16[512,512]{1,0:T(8,128)(2,1)}, bf16[512,512]{1,0:T(8,128)(2,1)}) custom-call(s32[28]{0:T(128)} %copy-done.4, bf16[4,512,1280]{2,1,0:T(8,128)(2,1)} %normalise.1.own_ref, bf16[4,512,1280]{2,1,0:T(8,128)(2,1)} %collective-permute-done.6.sib_ref, bf16[1280,512]{1,0:T(8,128)(2,1)} %pad_maximum_fusion.1.w0, ...), custom_call_target="tpu_custom_call" | custom-call | flops 10737418240 | bytes 10485760 | tf_op jit(solution)/shard_map/attend/pallas_call | solution.py:335
  125.1 1.6 collective-permute-start.25
  126.8 1.5 collective-permute-start.24
  129.6 7.1 %collective-permute-done.25 = f32[128,768]{1,0:T(8,128)S(1)} collective-permute-done((f32[128,768]{1,0:T(8,128)S(1)}, f32[128,768]{1,0:T(8,128)S(1)}, u32[]{:S(2)}, u32[]{:S(2)}) %collective-permute-start.25) | collective-permute-done | bytes 393248 | tf_op jit(solution)/shard_map/ppermute | solution.py:716
  140.3 1.6 collective-permute-start.22
  141.9 26.3 %collective-permute-done.26.refs_4_.refs_1_ = bf16[4,256,640]{2,1,0:T(8,128)(2,1)S(1)} collective-permute-done((bf16[4,256,640]{2,1,0:T(8,128)(2,1)S(1)}, bf16[4,256,640]{2,1,0:T(8,128)(2,1)S(1)}, u32[]{:S(2)}, u32[]{:S(2)}) %collective-permute-start.26) | collective-permute-done | bytes 1310752 | tf_op jit(solution)/shard_map/ppermute | solution.py:716
  171.4 1.6 collective-permute-start.23
  173.0 15.4 %collective-permute-done.33.refs_2_ = f32[2,128,768]{2,1,0:T(8,128)S(1)} collective-permute-done((f32[2,128,768]{2,1,0:T(8,128)S(1)}, f32[2,128,768]{2,1,0:T(8,128)S(1)}, u32[]{:S(2)}, u32[]{:S(2)}) %collective-permute-start.33) | collective-permute-done | bytes 786464 | tf_op jit(solution)/shard_map/ppermute | solution.py:716
  191.5 14.3 %collective-permute-done.35.refs_4_ = bf16[2,256,640]{2,1,0:T(8,128)(2,1)S(1)} collective-permute-done((bf16[2,256,640]{2,1,0:T(8,128)(2,1)S(1)}, bf16[2,256,640]{2,1,0:T(8,128)(2,1)S(1)}, u32[]{:S(2)}, u32[]{:S(2)}) %collective-permute-start.35) | collective-permute-done | bytes 655392 | tf_op jit(solution)/shard_map/ppermute | solution.py:716
  206.3 1.6 collective-permute-start.31
  210.2 9.0 %collective-permute-done.39.refs_1_ = f32[128,768]{1,0:T(8,128)S(1)} collective-permute-done((f32[128,768]{1,0:T(8,128)S(1)}, f32[128,768]{1,0:T(8,128)S(1)}, u32[]{:S(2)}, u32[]{:S(2)}) %collective-permute-start.39) | collective-permute-done | bytes 393248 | tf_op jit(solution)/shard_map/ppermute | solution.py:716
  220.3 5.0 %output_near.1.sum_ref = f32[512,1280]{1,0:T(8,128)S(1)} custom-call(s32[4]{0:T(128)S(1)} %copy-done.3, bf16[512,5120]{1,0:T(8,128)(2,1)S(1)} %bitcast.50, bf16[512,1024]{1,0:T(8,128)(2,1)S(1)} %constant_dynamic-update-slice_fusion.refs_0_.c0, bf16[512,1024]{1,0:T(8,128)(2,1)S(1)} %collective-permute-done.22.refs_1_.c1, ...), custom_call_target="tpu_custom_call" | custom-call | flops 4026531840 | bytes 20971520 | tf_op jit(solution)/shard_map/output_near/pallas_call | solution.py:631
  225.3 3.8 %place_grads.2 = (f32[1024,512]{1,0:T(8,128)}, f32[1024,256]{1,0:T(8,128)}, f32[1024,256]{1,0:T(8,128)}, f32[512,1024]{1,0:T(8,128)}) custom-call(s32[4]{0:T(128)S(1)} %copy-done.3, f32[2,128,768]{2,1,0:T(8,128)S(1)} %pad_maximum_fusion.4.refs_0_, f32[2,128,768]{2,1,0:T(8,128)S(1)} %collective-permute-done.32.refs_1_, ...), custom_call_target="tpu_custom_call" | custom-call | bytes 9437184 | tf_op jit(solution)/shard_map/place_grads/pallas_call | solution.py:580
  229.1 4.5 %collective-permute-done.31.c3 = bf16[512,1024]{1,0:T(8,128)(2,1)S(1)} collective-permute-done((bf16[512,1024]{1,0:T(8,128)(2,1)S(1)}, bf16[512,1024]{1,0:T(8,128)(2,1)S(1)}, u32[]{:S(2)}, u32[]{:S(2)}) %collective-permute-start.31) | collective-permute-done | bytes 1048608 | tf_op jit(solution)/shard_map/ppermute | solution.py:798
  233.6 4.9 %output_far.1 = bf16[512,1280]{1,0:T(8,128)(2,1)} custom-call(s32[4]{0:T(128)S(1)} %copy-done.3, f32[512,1280]{1,0:T(8,128)S(1)} %output_near.1.sum_ref, bf16[512,1024]{1,0:T(8,128)(2,1)S(1)} %constant_dynamic-update-slice_fusion.refs_0_.c0, bf16[512,1024]{1,0:T(8,128)(2,1)S(1)} %collective-permute-done.22.refs_1_.c1, ...), custom_call_target="tpu_custom_call" | custom-call | flops 2348810240 | bytes 5242880 | tf_op jit(solution)/shard_map/output_far/pallas_call | solution.py:674
  238.5 1.8 place_grads.3
  (151 shorter events, 42.8 us)
Async XLA Ops:
  4.1 22.4 %collective-permute-start.5 = (bf16[2,512,1024]{2,1,0:T(8,128)(2,1)S(1)}, bf16[2,512,1024]{2,1,0:T(8,128)(2,1)}, u32[]{:S(2)}, u32[]{:S(2)}) collective-permute-start(bf16[2,512,1024]{2,1,0:T(8,128)(2,1)S(1)} %pad_maximum_fusion.own_ref), channel_id=1, source_target_pairs={{0,4},{4,0},{8,12},{12,8},{16,20},{20,16},{24,28},{28,24},{1,5},{5... | collective-permute-start | bytes 6291464 | tf_op jit(solution)/shard_map/ppermute | solution.py:716
  7.2 17.9 %collective-permute-start.3 = (bf16[1280,256]{1,0:T(8,128)(2,1)S(1)}, bf16[1280,256]{1,0:T(8,128)(2,1)}, u32[]{:S(2)}, u32[]{:S(2)}) collective-permute-start(bf16[1280,256]{1,0:T(8,128)(2,1)S(1)} %pad_maximum_fusion.5.w0), channel_id=1, source_target_pairs={{0,16},{4,20},{8,24},{12,28},{16,0},{20,4},{24,8},{28,12},{1,17},{... | collective-permute-start | bytes 1966088 | tf_op jit(solution)/shard_map/ppermute | solution.py:716
  10.2 16.3 %collective-permute-start.2 = (bf16[1280,256]{1,0:T(8,128)(2,1)S(1)}, bf16[1280,256]{1,0:T(8,128)(2,1)}, u32[]{:S(2)}, u32[]{:S(2)}) collective-permute-start(bf16[1280,256]{1,0:T(8,128)(2,1)S(1)} %pad_maximum_fusion.5.w0), channel_id=1, source_target_pairs={{0,8},{4,12},{8,0},{12,4},{16,24},{20,28},{24,16},{28,20},{1,9},{5... | collective-permute-start | bytes 1966088 | tf_op jit(solution)/shard_map/ppermute | solution.py:716
  40.9 46.2 %collective-permute-start.10 = (bf16[1280,512]{1,0:T(8,128)(2,1)}, bf16[1280,512]{1,0:T(8,128)(2,1)S(1)}, u32[]{:S(2)}, u32[]{:S(2)}) collective-permute-start(bf16[1280,512]{1,0:T(8,128)(2,1)} %pad_maximum_fusion.1.w0), channel_id=1, source_target_pairs={{0,16},{4,20},{8,24},{12,28},{16,0},{20,4},{24,8},{28,12},{1,17},{... | collective-permute-start | bytes 3932168 | tf_op jit(solution)/shard_map/ppermute | solution.py:716
  42.4 47.5 %collective-permute-start.9 = (bf16[1280,512]{1,0:T(8,128)(2,1)}, bf16[1280,512]{1,0:T(8,128)(2,1)}, u32[]{:S(2)}, u32[]{:S(2)}) collective-permute-start(bf16[1280,512]{1,0:T(8,128)(2,1)} %pad_maximum_fusion.1.w0), channel_id=1, source_target_pairs={{0,8},{4,12},{8,0},{12,4},{16,24},{20,28},{24,16},{28,20},{1,9},{5... | collective-permute-start | bytes 3932168 | tf_op jit(solution)/shard_map/ppermute | solution.py:716
  44.6 36.8 %collective-permute-start.13 = (bf16[256,640]{1,0:T(8,128)(2,1)S(1)}, bf16[256,640]{1,0:T(8,128)(2,1)S(1)}, u32[]{:S(2)}, u32[]{:S(2)}) collective-permute-start(bf16[256,640]{1,0:T(8,128)(2,1)S(1)} %get-tuple-element.103), channel_id=1, source_target_pairs={{0,24},{4,28},{8,16},{12,20},{16,8},{20,12},{24,0},{28,4},{1,25},{... | collective-permute-start | bytes 983048 | tf_op jit(solution)/shard_map/ppermute | solution.py:716
  46.1 39.7 %collective-permute-start.12 = (bf16[256,640]{1,0:T(8,128)(2,1)S(1)}, bf16[256,640]{1,0:T(8,128)(2,1)S(1)}, u32[]{:S(2)}, u32[]{:S(2)}) collective-permute-start(bf16[256,640]{1,0:T(8,128)(2,1)S(1)} %get-tuple-element.104), channel_id=1, source_target_pairs={{0,16},{4,20},{8,24},{12,28},{16,0},{20,4},{24,8},{28,12},{1,17},{... | collective-permute-start | bytes 983048 | tf_op jit(solution)/shard_map/ppermute | solution.py:716
  47.6 39.5 %collective-permute-start.11 = (bf16[256,640]{1,0:T(8,128)(2,1)S(1)}, bf16[256,640]{1,0:T(8,128)(2,1)S(1)}, u32[]{:S(2)}, u32[]{:S(2)}) collective-permute-start(bf16[256,640]{1,0:T(8,128)(2,1)S(1)} %get-tuple-element.105), channel_id=1, source_target_pairs={{0,8},{4,12},{8,0},{12,4},{16,24},{20,28},{24,16},{28,20},{1,9},{5... | collective-permute-start | bytes 983048 | tf_op jit(solution)/shard_map/ppermute | solution.py:716
  89.3 15.6 %collective-permute-start.14 = (bf16[640,512]{1,0:T(8,128)(2,1)S(1)}, bf16[640,512]{1,0:T(8,128)(2,1)}, u32[]{:S(2)}, u32[]{:S(2)}) collective-permute-start(bf16[640,512]{1,0:T(8,128)(2,1)S(1)} %slice.50), channel_id=1, source_target_pairs={{0,8},{4,12},{8,0},{12,4},{16,24},{20,28},{24,16},{28,20},{1,9},{5... | collective-permute-start | bytes 1966088 | tf_op jit(solution)/shard_map/ppermute | solution.py:716
  91.1 15.3 %collective-permute-start.15 = (bf16[640,512]{1,0:T(8,128)(2,1)S(1)}, bf16[640,512]{1,0:T(8,128)(2,1)}, u32[]{:S(2)}, u32[]{:S(2)}) collective-permute-start(bf16[640,512]{1,0:T(8,128)(2,1)S(1)} %slice.51), channel_id=1, source_target_pairs={{0,16},{4,20},{8,24},{12,28},{16,0},{20,4},{24,8},{28,12},{1,17},{... | collective-permute-start | bytes 1966088 | tf_op jit(solution)/shard_map/ppermute | solution.py:716
  93.8 30.2 %collective-permute-start.20 = (bf16[256,640]{1,0:T(8,128)(2,1)}, bf16[256,640]{1,0:T(8,128)(2,1)S(1)}, u32[]{:S(2)}, u32[]{:S(2)}) collective-permute-start(bf16[256,640]{1,0:T(8,128)(2,1)} %get-tuple-element.99), channel_id=1, source_target_pairs={{0,3},{1,0},{2,1},{3,2},{4,7},{5,4},{6,5},{7,6},{8,11},{9,8},{10,9... | collective-permute-start | bytes 983048 | tf_op jit(solution)/shard_map/ppermute | solution.py:786
  97.5 26.6 %collective-permute-start.19 = (bf16[256,640]{1,0:T(8,128)(2,1)}, bf16[256,640]{1,0:T(8,128)(2,1)S(1)}, u32[]{:S(2)}, u32[]{:S(2)}) collective-permute-start(bf16[256,640]{1,0:T(8,128)(2,1)} %get-tuple-element.100), channel_id=1, source_target_pairs={{0,2},{1,3},{2,0},{3,1},{4,6},{5,7},{6,4},{7,5},{8,10},{9,11},{10,... | collective-permute-start | bytes 983048 | tf_op jit(solution)/shard_map/ppermute | solution.py:786
  97.5 26.6 %collective-permute-start.18 = (bf16[256,640]{1,0:T(8,128)(2,1)}, bf16[256,640]{1,0:T(8,128)(2,1)}, u32[]{:S(2)}, u32[]{:S(2)}) collective-permute-start(bf16[256,640]{1,0:T(8,128)(2,1)} %get-tuple-element.101), channel_id=1, source_target_pairs={{0,1},{1,2},{2,3},{3,0},{4,5},{5,6},{6,7},{7,4},{8,9},{9,10},{10,1... | collective-permute-start | bytes 983048 | tf_op jit(solution)/shard_map/ppermute | solution.py:786
  104.9 19.2 %collective-permute-start.16 = (f32[2,128,768]{2,1,0:T(8,128)S(1)}, f32[2,128,768]{2,1,0:T(8,128)S(1)}, u32[]{:S(2)}, u32[]{:S(2)}) collective-permute-start(f32[2,128,768]{2,1,0:T(8,128)S(1)} %get-tuple-element.66), channel_id=1, source_target_pairs={{0,8},{4,12},{8,0},{12,4},{16,24},{20,28},{24,16},{28,20},{1,9},{5... | collective-permute-start | bytes 2359304 | tf_op jit(solution)/shard_map/ppermute | solution.py:716
  106.4 17.7 %collective-permute-start.17 = (f32[2,128,768]{2,1,0:T(8,128)S(1)}, f32[2,128,768]{2,1,0:T(8,128)S(1)}, u32[]{:S(2)}, u32[]{:S(2)}) collective-permute-start(f32[2,128,768]{2,1,0:T(8,128)S(1)} %get-tuple-element.71), channel_id=1, source_target_pairs={{0,16},{4,20},{8,24},{12,28},{16,0},{20,4},{24,8},{28,12},{1,17},{... | collective-permute-start | bytes 2359304 | tf_op jit(solution)/shard_map/ppermute | solution.py:716
  138.1 30.1 %collective-permute-start.26 = (bf16[4,256,640]{2,1,0:T(8,128)(2,1)S(1)}, bf16[4,256,640]{2,1,0:T(8,128)(2,1)S(1)}, u32[]{:S(2)}, u32[]{:S(2)}) collective-permute-start(bf16[4,256,640]{2,1,0:T(8,128)(2,1)S(1)} %pad_maximum_fusion.3.refs_3_.refs_0_), channel_id=1, source_target_pairs={{0,8},{4,12},{8,0},{12,4},{16,24},{20,28},{24,16},{28,20},{1,9},{5... | collective-permute-start | bytes 3932168 | tf_op jit(solution)/shard_map/ppermute | solution.py:716
  138.7 29.8 %collective-permute-start.27 = (bf16[4,256,640]{2,1,0:T(8,128)(2,1)S(1)}, bf16[4,256,640]{2,1,0:T(8,128)(2,1)S(1)}, u32[]{:S(2)}, u32[]{:S(2)}) collective-permute-start(bf16[4,256,640]{2,1,0:T(8,128)(2,1)S(1)} %pad_maximum_fusion.3.refs_3_.refs_0_), channel_id=1, source_target_pairs={{0,16},{4,20},{8,24},{12,28},{16,0},{20,4},{24,8},{28,12},{1,17},{... | collective-permute-start | bytes 3932168 | tf_op jit(solution)/shard_map/ppermute | solution.py:716
  140.3 31.2 %collective-permute-start.22 = (bf16[512,1024]{1,0:T(8,128)(2,1)S(1)}, bf16[512,1024]{1,0:T(8,128)(2,1)S(1)}, u32[]{:S(2)}, u32[]{:S(2)}) collective-permute-start(bf16[512,1024]{1,0:T(8,128)(2,1)S(1)} %constant_dynamic-update-slice_fusion.refs_0_.c0), channel_id=1, source_target_pairs={{0,1},{1,2},{2,3},{3,0},{4,5},{5,6},{6,7},{7,4},{8,9},{9,10},{10,1... | collective-permute-start | bytes 3145736 | tf_op jit(solution)/shard_map/ppermute | solution.py:798
  168.2 21.4 %collective-permute-start.28 = (bf16[4,256,640]{2,1,0:T(8,128)(2,1)S(1)}, bf16[4,256,640]{2,1,0:T(8,128)(2,1)S(1)}, u32[]{:S(2)}, u32[]{:S(2)}) collective-permute-start(bf16[4,256,640]{2,1,0:T(8,128)(2,1)S(1)} %pad_maximum_fusion.3.refs_3_.refs_0_), channel_id=1, source_target_pairs={{0,4},{4,0},{8,12},{12,8},{16,20},{20,16},{24,28},{28,24},{1,5},{5... | collective-permute-start | bytes 3932168 | tf_op jit(solution)/shard_map/ppermute | solution.py:716
  168.5 19.9 %collective-permute-start.33 = (f32[2,128,768]{2,1,0:T(8,128)S(1)}, f32[2,128,768]{2,1,0:T(8,128)S(1)}, u32[]{:S(2)}, u32[]{:S(2)}) collective-permute-start(f32[2,128,768]{2,1,0:T(8,128)S(1)} %pad_maximum_fusion.4.refs_0_), channel_id=1, source_target_pairs={{0,16},{4,20},{8,24},{12,28},{16,0},{20,4},{24,8},{28,12},{1,17},{... | collective-permute-start | bytes 2359304 | tf_op jit(solution)/shard_map/ppermute | solution.py:716
  169.9 19.7 %collective-permute-start.32 = (f32[2,128,768]{2,1,0:T(8,128)S(1)}, f32[2,128,768]{2,1,0:T(8,128)S(1)}, u32[]{:S(2)}, u32[]{:S(2)}) collective-permute-start(f32[2,128,768]{2,1,0:T(8,128)S(1)} %pad_maximum_fusion.4.refs_0_), channel_id=1, source_target_pairs={{0,8},{4,12},{8,0},{12,4},{16,24},{20,28},{24,16},{28,20},{1,9},{5... | collective-permute-start | bytes 2359304 | tf_op jit(solution)/shard_map/ppermute | solution.py:716
  171.4 19.5 %collective-permute-start.42 = (f32[2,128,768]{2,1,0:T(8,128)S(1)}, f32[2,128,768]{2,1,0:T(8,128)S(1)}, u32[]{:S(2)}, u32[]{:S(2)}) collective-permute-start(f32[2,128,768]{2,1,0:T(8,128)S(1)} %pad_maximum_fusion.4.refs_0_), channel_id=1, source_target_pairs={{0,4},{4,0},{8,12},{12,8},{16,20},{20,16},{24,28},{28,24},{1,5},{5... | collective-permute-start | bytes 2359304 | tf_op jit(solution)/shard_map/ppermute | solution.py:716
  171.4 34.8 %collective-permute-start.23 = (bf16[512,1024]{1,0:T(8,128)(2,1)S(1)}, bf16[512,1024]{1,0:T(8,128)(2,1)S(1)}, u32[]{:S(2)}, u32[]{:S(2)}) collective-permute-start(bf16[512,1024]{1,0:T(8,128)(2,1)S(1)} %collective-permute-done.22.refs_1_.c1), channel_id=1, source_target_pairs={{0,1},{1,2},{2,3},{3,0},{4,5},{5,6},{6,7},{7,4},{8,9},{9,10},{10,1... | collective-permute-start | bytes 3145736 | tf_op jit(solution)/shard_map/ppermute | solution.py:798
  189.6 16.1 %collective-permute-start.35 = (bf16[2,256,640]{2,1,0:T(8,128)(2,1)S(1)}, bf16[2,256,640]{2,1,0:T(8,128)(2,1)S(1)}, u32[]{:S(2)}, u32[]{:S(2)}) collective-permute-start(bf16[2,256,640]{2,1,0:T(8,128)(2,1)S(1)} %slice.57), channel_id=1, source_target_pairs={{0,16},{4,20},{8,24},{12,28},{16,0},{20,4},{24,8},{28,12},{1,17},{... | collective-permute-start | bytes 1966088 | tf_op jit(solution)/shard_map/ppermute | solution.py:716
  190.3 15.9 %collective-permute-start.34 = (bf16[2,256,640]{2,1,0:T(8,128)(2,1)S(1)}, bf16[2,256,640]{2,1,0:T(8,128)(2,1)S(1)}, u32[]{:S(2)}, u32[]{:S(2)}) collective-permute-start(bf16[2,256,640]{2,1,0:T(8,128)(2,1)S(1)} %slice.56), channel_id=1, source_target_pairs={{0,8},{4,12},{8,0},{12,4},{16,24},{20,28},{24,16},{28,20},{1,9},{5... | collective-permute-start | bytes 1966088 | tf_op jit(solution)/shard_map/ppermute | solution.py:716
  190.9 17.0 %collective-permute-start.30 = (bf16[4,256,640]{2,1,0:T(8,128)(2,1)S(1)}, bf16[4,256,640]{2,1,0:T(8,128)(2,1)S(1)}, u32[]{:S(2)}, u32[]{:S(2)}) collective-permute-start(bf16[4,256,640]{2,1,0:T(8,128)(2,1)S(1)} %collective-permute-done.27.refs_5_.refs_2_), channel_id=1, source_target_pairs={{0,4},{4,0},{8,12},{12,8},{16,20},{20,16},{24,28},{28,24},{1,5},{5... | collective-permute-start | bytes 3932168 | tf_op jit(solution)/shard_map/ppermute | solution.py:716
  190.9 18.4 %collective-permute-start.29 = (bf16[4,256,640]{2,1,0:T(8,128)(2,1)S(1)}, bf16[4,256,640]{2,1,0:T(8,128)(2,1)S(1)}, u32[]{:S(2)}, u32[]{:S(2)}) collective-permute-start(bf16[4,256,640]{2,1,0:T(8,128)(2,1)S(1)} %collective-permute-done.26.refs_4_.refs_1_), channel_id=1, source_target_pairs={{0,4},{4,0},{8,12},{12,8},{16,20},{20,16},{24,28},{28,24},{1,5},{5... | collective-permute-start | bytes 3932168 | tf_op jit(solution)/shard_map/ppermute | solution.py:716
  206.3 27.4 %collective-permute-start.31 = (bf16[512,1024]{1,0:T(8,128)(2,1)S(1)}, bf16[512,1024]{1,0:T(8,128)(2,1)S(1)}, u32[]{:S(2)}, u32[]{:S(2)}) collective-permute-start(bf16[512,1024]{1,0:T(8,128)(2,1)S(1)} %collective-permute-done.23.refs_2_.c2), channel_id=1, source_target_pairs={{0,1},{1,2},{2,3},{3,0},{4,5},{5,6},{6,7},{7,4},{8,9},{9,10},{10,1... | collective-permute-start | bytes 3145736 | tf_op jit(solution)/shard_map/ppermute | solution.py:798
  209.7 23.9 %collective-permute-start.37 = (bf16[2,256,640]{2,1,0:T(8,128)(2,1)S(1)}, bf16[2,256,640]{2,1,0:T(8,128)(2,1)S(1)}, u32[]{:S(2)}, u32[]{:S(2)}) collective-permute-start(bf16[2,256,640]{2,1,0:T(8,128)(2,1)S(1)} %collective-permute-done.35.refs_4_), channel_id=1, source_target_pairs={{0,4},{4,0},{8,12},{12,8},{16,20},{20,16},{24,28},{28,24},{1,5},{5... | collective-permute-start | bytes 1966088 | tf_op jit(solution)/shard_map/ppermute | solution.py:716
  209.7 23.9 %collective-permute-start.36 = (bf16[2,256,640]{2,1,0:T(8,128)(2,1)S(1)}, bf16[2,256,640]{2,1,0:T(8,128)(2,1)S(1)}, u32[]{:S(2)}, u32[]{:S(2)}) collective-permute-start(bf16[2,256,640]{2,1,0:T(8,128)(2,1)S(1)} %collective-permute-done.34.refs_3_), channel_id=1, source_target_pairs={{0,4},{4,0},{8,12},{12,8},{16,20},{20,16},{24,28},{28,24},{1,5},{5... | collective-permute-start | bytes 1966088 | tf_op jit(solution)/shard_map/ppermute | solution.py:716
  219.2 19.3 %collective-permute-start.41 = (f32[128,768]{1,0:T(8,128)S(1)}, f32[128,768]{1,0:T(8,128)S(1)}, u32[]{:S(2)}, u32[]{:S(2)}) collective-permute-start(f32[128,768]{1,0:T(8,128)S(1)} %collective-permute-done.39.refs_1_), channel_id=1, source_target_pairs={{0,4},{4,0},{8,12},{12,8},{16,20},{20,16},{24,28},{28,24},{1,5},{5... | collective-permute-start | bytes 1179656 | tf_op jit(solution)/shard_map/ppermute | solution.py:716
  220.3 18.2 %collective-permute-start.40 = (f32[128,768]{1,0:T(8,128)S(1)}, f32[128,768]{1,0:T(8,128)S(1)}, u32[]{:S(2)}, u32[]{:S(2)}) collective-permute-start(f32[128,768]{1,0:T(8,128)S(1)} %collective-permute-done.38.refs_0_), channel_id=1, source_target_pairs={{0,4},{4,0},{8,12},{12,8},{16,20},{20,16},{24,28},{28,24},{1,5},{5... | collective-permute-start | bytes 1179656 | tf_op jit(solution)/shard_map/ppermute | solution.py:716
  (36 other events, 404.1 us)

commit v4 on v3

--- a/solution.py
+++ b/solution.py
@@ -743,18 +743,18 @@
 
     k_mine, k_other = halves(bb_wk)
     v_mine, v_other = halves(bb_wv)
-    q_mine, q_other = halves(bb_wq)
     kv_got = swap(jnp.concatenate([k_other, v_other], axis=1))
     kv_shard = jnp.concatenate([jnp.concatenate([k_mine, v_mine], axis=1), kv_got])
     kv_x, kv_y = over_x(kv_shard), over_y(kv_shard)
 
-    q_got = swap(after(q_other, kv_shard))
     spans = action_tokens.shape[0]
     pad = ((0, 0), (0, PAD - STEPS), (0, 0))
     pair = jnp.stack([jnp.pad(action_tokens, pad), jnp.pad(action_cot, pad)])
     pair = pair.reshape(2, spans * PAD, action_tokens.shape[2])
     pair_sib = swap(after(pair, kv_shard))
-    normed = normalise(chip_meta, after(flat, q_other, pair), 4)
+    normed = normalise(chip_meta, after(flat, kv_shard, pair), 4)
+    q_mine, q_other = halves(after(bb_wq, normed))
+    q_got = swap(q_other)
     normed_sib = swap(after(normed, kv_x, kv_y, q_got, pair_sib))
     half = kv_x.shape[0] // 2
     low, high = kv_y[:half], kv_x[half:]

time: 241 us -> 236 us (0.979)
  local copies, waits for them, and re-layouts: 14.8 us -> 10.4 us
    unnamed x49 -> x55, local copies, waits for them, and re-layouts: 4.99 us -> 4.91 us
  transfers between devices with their start and end apart: 45 -> 45, of which waited for: 20 -> 21; matrix products, arithmetic and copies ran while one was open for 6% -> 4% of each run, Pallas kernels for 29% -> 30%
where the time goes in v4:
time: 236 us
  waiting for transfers between devices  110 us (47%)
  Pallas kernels  72.2 us (31%)
  starting transfers between devices  36.7 us (16%)
  local copies, waits for them, and re-layouts  10.4 us (4%)
  other arithmetic  5.27 us (2%)
    ppermute x39, waiting for transfers between devices, across(): return lambda x: lax.ppermute(x, 'dp', [(i, i ^ mask) for i in range(8)])  105 us
    ppermute x39, starting transfers between devices, across(): return lambda x: lax.ppermute(x, 'dp', [(i, i ^ mask) for i in range(8)])  27.4 us
    pallas_call x1, Pallas kernels, attend(): pl.pallas_call(functools.partial(attend_kernel, factor), grid_spec=pltpu....  17.1 us
    pallas_call x1, Pallas kernels, expert_attend(): pl.pallas_call(functools.partial(expert_kernel, factor, spans), grid_spec...  11.6 us
    pallas_call x1, Pallas kernels, project_kv(): pl.pallas_call(kv_kernel, grid=(steps,), in_specs=pair_specs(parts, block...  8.46 us
    pallas_call x1, Pallas kernels, normalise(): pl.pallas_call(norm_kernel, grid_spec=pltpu.PrefetchScalarGridSpec(num_sc...  7.25 us
    pallas_call x1, Pallas kernels, expert_project(): pl.pallas_call(expert_project_kernel, grid_spec=pltpu.PrefetchScalarGridS...  7.17 us
    pallas_call x2, Pallas kernels, place_grads(): pl.pallas_call(functools.partial(place_kernel, tuple(pieces), len(own)),...  5.57 us
  transfers between devices with their start and end apart: 45, of which 21 were waited for; matrix products, arithmetic and copies ran while one was open for 4% of the time, Pallas kernels for 30%

profile of v4, /device:TPU:0, one launch (start us, length us, event | category | flops | bytes accessed | tf_op | source)
XLA Modules:
  0.0 235.6 jit_solution(528251123197202572)
XLA Ops:
  5.5 2.6 %collective-permute-start.3 = (bf16[1280,256]{1,0:T(8,128)(2,1)S(1)}, bf16[1280,256]{1,0:T(8,128)(2,1)S(1)}, u32[]{:S(2)}, u32[]{:S(2)}) collective-permute-start(bf16[1280,256]{1,0:T(8,128)(2,1)S(1)} %pad_maximum_fusion.5.w0), channel_id=1, source_target_pairs={{0,16},{4,20},{8,24},{12,28},{16,0},{20,4},{24,8},{28,12},{1,17},{... | collective-permute-start | bytes 1966088 | tf_op jit(solution)/shard_map/ppermute | solution.py:716
  8.1 1.5 collective-permute-start.2
  9.6 7.3 %normalise.1.own_ref = bf16[4,512,1280]{2,1,0:T(8,128)(2,1)} custom-call(s32[4]{0:T(128)} %pad_add_fusion.meta, bf16[512,5120]{1,0:T(8,128)(2,1)} %bitcast.47), custom_call_target="tpu_custom_call" | custom-call | flops 10485760 | bytes 10485760 | tf_op jit(solution)/shard_map/normalise/pallas_call | solution.py:223
  17.1 6.2 %collective-permute-done.3.w2 = bf16[1280,256]{1,0:T(8,128)(2,1)S(1)} collective-permute-done((bf16[1280,256]{1,0:T(8,128)(2,1)S(1)}, bf16[1280,256]{1,0:T(8,128)(2,1)S(1)}, u32[]{:S(2)}, u32[]{:S(2)}) %collective-permute-start.3) | collective-permute-done | bytes 655392 | tf_op jit(solution)/shard_map/ppermute | solution.py:716
  23.3 1.5 collective-permute-done.2.w1
  24.9 1.6 collective-permute-start.7
  28.2 7.2 %expert_project.1 = (bf16[1024,512]{1,0:T(8,128)(2,1)}, bf16[1024,256]{1,0:T(8,128)(2,1)}) custom-call(s32[4]{0:T(128)} %pad_add_fusion.meta, bf16[2,512,1024]{2,1,0:T(8,128)(2,1)} %copy-done, bf16[2,512,1024]{2,1,0:T(8,128)(2,1)} %collective-permute-done.5.sib_ref, bf16[1024,512]{1,0:T(8,128)(2,1)} %wq.1, bf16[1024,256]{1,0:T(8,128)(2,1)} %wk.1, ...), custom_call_target="tpu_custom_call" | custom-call | flops 1610612736 | bytes 4194304 | tf_op jit(solution)/shard_map/expert_project/pallas_call | solution.py:382
  39.9 2.3 collective-permute-start.13
  43.5 8.5 %project_kv.1.kv_ref = bf16[1024,256]{1,0:T(8,128)(2,1)} custom-call(bf16[4,512,1280]{2,1,0:T(8,128)(2,1)} %normalise.1.own_ref, bf16[4,512,1280]{2,1,0:T(8,128)(2,1)} %collective-permute-done.6.sib_ref, bf16[1280,256]{1,0:T(8,128)(2,1)} %copy-done.7, bf16[1280,256]{1,0:T(8,128)(2,1)} %copy-done.9, bf16[1280,256]{1,0:T(8,128)(2,1)} %copy-done.8, ...), custom_call_target="tpu_custom_call" | custom-call | flops 2684354560 | bytes 10485760 | tf_op jit(solution)/shard_map/project_kv/pallas_call | solution.py:278
  53.0 11.6 %expert_attend.1 = (bf16[1024,256]{1,0:T(8,128)(2,1)S(1)}, bf16[1024,512]{1,0:T(8,128)(2,1)S(1)}) custom-call(s32[28]{0:T(128)S(1)} %concatenate.23.meta, bf16[1024,512]{1,0:T(8,128)(2,1)S(1)} %copy-done.5, bf16[1024,256]{1,0:T(8,128)(2,1)S(1)} %copy-done.6, bf16[1024,256]{1,0:T(8,128)(2,1)S(1)} %copy-done.2), custom_call_target="tpu_custom_call" | custom-call | flops 3355443200 | bytes 4194304 | tf_op jit(solution)/shard_map/expert_attend/pallas_call | solution.py:467
  64.6 12.9 %collective-permute-done.13 = bf16[256,640]{1,0:T(8,128)(2,1)S(1)} collective-permute-done((bf16[256,640]{1,0:T(8,128)(2,1)S(1)}, bf16[256,640]{1,0:T(8,128)(2,1)S(1)}, u32[]{:S(2)}, u32[]{:S(2)}) %collective-permute-start.13) | collective-permute-done | bytes 327712 | tf_op jit(solution)/shard_map/ppermute | solution.py:716
  77.5 3.9 %collective-permute-done.12 = bf16[256,640]{1,0:T(8,128)(2,1)S(1)} collective-permute-done((bf16[256,640]{1,0:T(8,128)(2,1)S(1)}, bf16[256,640]{1,0:T(8,128)(2,1)S(1)}, u32[]{:S(2)}, u32[]{:S(2)}) %collective-permute-start.12) | collective-permute-done | bytes 327712 | tf_op jit(solution)/shard_map/ppermute | solution.py:716
  89.6 3.6 %collective-permute-start.20 = (bf16[256,640]{1,0:T(8,128)(2,1)}, bf16[256,640]{1,0:T(8,128)(2,1)S(1)}, u32[]{:S(2)}, u32[]{:S(2)}) collective-permute-start(bf16[256,640]{1,0:T(8,128)(2,1)} %get-tuple-element.99), channel_id=1, source_target_pairs={{0,3},{1,0},{2,1},{3,2},{4,7},{5,4},{6,5},{7,6},{8,11},{9,8},{10,9... | collective-permute-start | bytes 983048 | tf_op jit(solution)/shard_map/ppermute | solution.py:786
  94.2 5.2 %weight_grads.1 = (f32[2,128,768]{2,1,0:T(8,128)S(1)}, f32[2,128,768]{2,1,0:T(8,128)S(1)}, f32[2,128,768]{2,1,0:T(8,128)S(1)}, f32[2,128,768]{2,1,0:T(8,128)S(1)}) custom-call(s32[4]{0:T(128)S(1)} %copy-done.3, bf16[2,512,1024]{2,1,0:T(8,128)(2,1)S(1)} %copy-done.1, bf16[2,512,1024]{2,1,0:T(8,128)(2,1)} %collective-permute-done.5.sib_ref, ...), custom_call_target="tpu_custom_call" | custom-call | flops 1610612736 | bytes 12582912 | tf_op jit(solution)/shard_map/weight_grads/pallas_call | solution.py:522
  102.2 17.1 %attend.1 = (bf16[512,512]{1,0:T(8,128)(2,1)}, bf16[512,512]{1,0:T(8,128)(2,1)}) custom-call(s32[28]{0:T(128)} %copy-done.4, bf16[4,512,1280]{2,1,0:T(8,128)(2,1)} %normalise.1.own_ref, bf16[4,512,1280]{2,1,0:T(8,128)(2,1)} %collective-permute-done.6.sib_ref, bf16[1280,512]{1,0:T(8,128)(2,1)} %pad_maximum_fusion.1.w0, ...), custom_call_target="tpu_custom_call" | custom-call | flops 10737418240 | bytes 10485760 | tf_op jit(solution)/shard_map/attend/pallas_call | solution.py:335
  120.4 1.6 collective-permute-start.25
  122.1 1.5 collective-permute-start.24
  124.8 7.2 %collective-permute-done.25 = f32[128,768]{1,0:T(8,128)S(1)} collective-permute-done((f32[128,768]{1,0:T(8,128)S(1)}, f32[128,768]{1,0:T(8,128)S(1)}, u32[]{:S(2)}, u32[]{:S(2)}) %collective-permute-start.25) | collective-permute-done | bytes 393248 | tf_op jit(solution)/shard_map/ppermute | solution.py:716
  133.9 1.5 collective-permute-start.27
  135.5 1.8 collective-permute-start.22
  137.3 26.2 %collective-permute-done.26.refs_4_.refs_1_ = bf16[4,256,640]{2,1,0:T(8,128)(2,1)S(1)} collective-permute-done((bf16[4,256,640]{2,1,0:T(8,128)(2,1)S(1)}, bf16[4,256,640]{2,1,0:T(8,128)(2,1)S(1)}, u32[]{:S(2)}, u32[]{:S(2)}) %collective-permute-start.26) | collective-permute-done | bytes 1310752 | tf_op jit(solution)/shard_map/ppermute | solution.py:716
  163.7 1.5 collective-permute-start.33
  165.2 1.5 collective-permute-start.32
  166.7 1.6 collective-permute-start.23
  168.3 15.4 %collective-permute-done.33.refs_2_ = f32[2,128,768]{2,1,0:T(8,128)S(1)} collective-permute-done((f32[2,128,768]{2,1,0:T(8,128)S(1)}, f32[2,128,768]{2,1,0:T(8,128)S(1)}, u32[]{:S(2)}, u32[]{:S(2)}) %collective-permute-start.33) | collective-permute-done | bytes 786464 | tf_op jit(solution)/shard_map/ppermute | solution.py:716
  186.7 14.3 %collective-permute-done.35.refs_4_ = bf16[2,256,640]{2,1,0:T(8,128)(2,1)S(1)} collective-permute-done((bf16[2,256,640]{2,1,0:T(8,128)(2,1)S(1)}, bf16[2,256,640]{2,1,0:T(8,128)(2,1)S(1)}, u32[]{:S(2)}, u32[]{:S(2)}) %collective-permute-start.35) | collective-permute-done | bytes 655392 | tf_op jit(solution)/shard_map/ppermute | solution.py:716
  205.5 8.7 %collective-permute-done.39.refs_1_ = f32[128,768]{1,0:T(8,128)S(1)} collective-permute-done((f32[128,768]{1,0:T(8,128)S(1)}, f32[128,768]{1,0:T(8,128)S(1)}, u32[]{:S(2)}, u32[]{:S(2)}) %collective-permute-start.39) | collective-permute-done | bytes 393248 | tf_op jit(solution)/shard_map/ppermute | solution.py:716
  215.4 5.0 %output_near.1.sum_ref = f32[512,1280]{1,0:T(8,128)S(1)} custom-call(s32[4]{0:T(128)S(1)} %copy-done.3, bf16[512,5120]{1,0:T(8,128)(2,1)S(1)} %bitcast.50, bf16[512,1024]{1,0:T(8,128)(2,1)S(1)} %constant_dynamic-update-slice_fusion.refs_0_.c0, bf16[512,1024]{1,0:T(8,128)(2,1)S(1)} %collective-permute-done.22.refs_1_.c1, ...), custom_call_target="tpu_custom_call" | custom-call | flops 4026531840 | bytes 20971520 | tf_op jit(solution)/shard_map/output_near/pallas_call | solution.py:631
  220.4 3.8 %place_grads.2 = (f32[1024,512]{1,0:T(8,128)}, f32[1024,256]{1,0:T(8,128)}, f32[1024,256]{1,0:T(8,128)}, f32[512,1024]{1,0:T(8,128)}) custom-call(s32[4]{0:T(128)S(1)} %copy-done.3, f32[2,128,768]{2,1,0:T(8,128)S(1)} %pad_maximum_fusion.4.refs_0_, f32[2,128,768]{2,1,0:T(8,128)S(1)} %collective-permute-done.32.refs_1_, ...), custom_call_target="tpu_custom_call" | custom-call | bytes 9437184 | tf_op jit(solution)/shard_map/place_grads/pallas_call | solution.py:580
  224.2 4.7 %collective-permute-done.31.c3 = bf16[512,1024]{1,0:T(8,128)(2,1)S(1)} collective-permute-done((bf16[512,1024]{1,0:T(8,128)(2,1)S(1)}, bf16[512,1024]{1,0:T(8,128)(2,1)S(1)}, u32[]{:S(2)}, u32[]{:S(2)}) %collective-permute-start.31) | collective-permute-done | bytes 1048608 | tf_op jit(solution)/shard_map/ppermute | solution.py:798
  228.9 4.8 %output_far.1 = bf16[512,1280]{1,0:T(8,128)(2,1)} custom-call(s32[4]{0:T(128)S(1)} %copy-done.3, f32[512,1280]{1,0:T(8,128)S(1)} %output_near.1.sum_ref, bf16[512,1024]{1,0:T(8,128)(2,1)S(1)} %constant_dynamic-update-slice_fusion.refs_0_.c0, bf16[512,1024]{1,0:T(8,128)(2,1)S(1)} %collective-permute-done.22.refs_1_.c1, ...), custom_call_target="tpu_custom_call" | custom-call | flops 2348810240 | bytes 5242880 | tf_op jit(solution)/shard_map/output_far/pallas_call | solution.py:674
  233.7 1.8 place_grads.3
  (157 shorter events, 38.9 us)
Async XLA Ops:
  4.1 20.7 %collective-permute-start.5 = (bf16[2,512,1024]{2,1,0:T(8,128)(2,1)S(1)}, bf16[2,512,1024]{2,1,0:T(8,128)(2,1)}, u32[]{:S(2)}, u32[]{:S(2)}) collective-permute-start(bf16[2,512,1024]{2,1,0:T(8,128)(2,1)S(1)} %pad_maximum_fusion.own_ref), channel_id=1, source_target_pairs={{0,4},{4,0},{8,12},{12,8},{16,20},{20,16},{24,28},{28,24},{1,5},{5... | collective-permute-start | bytes 6291464 | tf_op jit(solution)/shard_map/ppermute | solution.py:716
  5.5 17.8 %collective-permute-start.3 = (bf16[1280,256]{1,0:T(8,128)(2,1)S(1)}, bf16[1280,256]{1,0:T(8,128)(2,1)S(1)}, u32[]{:S(2)}, u32[]{:S(2)}) collective-permute-start(bf16[1280,256]{1,0:T(8,128)(2,1)S(1)} %pad_maximum_fusion.5.w0), channel_id=1, source_target_pairs={{0,16},{4,20},{8,24},{12,28},{16,0},{20,4},{24,8},{28,12},{1,17},{... | collective-permute-start | bytes 1966088 | tf_op jit(solution)/shard_map/ppermute | solution.py:716
  8.1 16.7 %collective-permute-start.2 = (bf16[1280,256]{1,0:T(8,128)(2,1)S(1)}, bf16[1280,256]{1,0:T(8,128)(2,1)S(1)}, u32[]{:S(2)}, u32[]{:S(2)}) collective-permute-start(bf16[1280,256]{1,0:T(8,128)(2,1)S(1)} %pad_maximum_fusion.5.w0), channel_id=1, source_target_pairs={{0,8},{4,12},{8,0},{12,4},{16,24},{20,28},{24,16},{28,20},{1,9},{5... | collective-permute-start | bytes 1966088 | tf_op jit(solution)/shard_map/ppermute | solution.py:716
  37.1 45.3 %collective-permute-start.10 = (bf16[1280,512]{1,0:T(8,128)(2,1)}, bf16[1280,512]{1,0:T(8,128)(2,1)S(1)}, u32[]{:S(2)}, u32[]{:S(2)}) collective-permute-start(bf16[1280,512]{1,0:T(8,128)(2,1)} %pad_maximum_fusion.1.w0), channel_id=1, source_target_pairs={{0,16},{4,20},{8,24},{12,28},{16,0},{20,4},{24,8},{28,12},{1,17},{... | collective-permute-start | bytes 3932168 | tf_op jit(solution)/shard_map/ppermute | solution.py:716
  37.8 47.5 %collective-permute-start.9 = (bf16[1280,512]{1,0:T(8,128)(2,1)}, bf16[1280,512]{1,0:T(8,128)(2,1)}, u32[]{:S(2)}, u32[]{:S(2)}) collective-permute-start(bf16[1280,512]{1,0:T(8,128)(2,1)} %pad_maximum_fusion.1.w0), channel_id=1, source_target_pairs={{0,8},{4,12},{8,0},{12,4},{16,24},{20,28},{24,16},{28,20},{1,9},{5... | collective-permute-start | bytes 3932168 | tf_op jit(solution)/shard_map/ppermute | solution.py:716
  39.9 37.6 %collective-permute-start.13 = (bf16[256,640]{1,0:T(8,128)(2,1)S(1)}, bf16[256,640]{1,0:T(8,128)(2,1)S(1)}, u32[]{:S(2)}, u32[]{:S(2)}) collective-permute-start(bf16[256,640]{1,0:T(8,128)(2,1)S(1)} %get-tuple-element.103), channel_id=1, source_target_pairs={{0,24},{4,28},{8,16},{12,20},{16,8},{20,12},{24,0},{28,4},{1,25},{... | collective-permute-start | bytes 983048 | tf_op jit(solution)/shard_map/ppermute | solution.py:716
  42.2 39.2 %collective-permute-start.12 = (bf16[256,640]{1,0:T(8,128)(2,1)S(1)}, bf16[256,640]{1,0:T(8,128)(2,1)S(1)}, u32[]{:S(2)}, u32[]{:S(2)}) collective-permute-start(bf16[256,640]{1,0:T(8,128)(2,1)S(1)} %get-tuple-element.104), channel_id=1, source_target_pairs={{0,16},{4,20},{8,24},{12,28},{16,0},{20,4},{24,8},{28,12},{1,17},{... | collective-permute-start | bytes 983048 | tf_op jit(solution)/shard_map/ppermute | solution.py:716
  42.9 39.5 %collective-permute-start.11 = (bf16[256,640]{1,0:T(8,128)(2,1)S(1)}, bf16[256,640]{1,0:T(8,128)(2,1)S(1)}, u32[]{:S(2)}, u32[]{:S(2)}) collective-permute-start(bf16[256,640]{1,0:T(8,128)(2,1)S(1)} %get-tuple-element.105), channel_id=1, source_target_pairs={{0,8},{4,12},{8,0},{12,4},{16,24},{20,28},{24,16},{28,20},{1,9},{5... | collective-permute-start | bytes 983048 | tf_op jit(solution)/shard_map/ppermute | solution.py:716
  84.6 15.6 %collective-permute-start.14 = (bf16[640,512]{1,0:T(8,128)(2,1)S(1)}, bf16[640,512]{1,0:T(8,128)(2,1)}, u32[]{:S(2)}, u32[]{:S(2)}) collective-permute-start(bf16[640,512]{1,0:T(8,128)(2,1)S(1)} %slice.50), channel_id=1, source_target_pairs={{0,8},{4,12},{8,0},{12,4},{16,24},{20,28},{24,16},{28,20},{1,9},{5... | collective-permute-start | bytes 1966088 | tf_op jit(solution)/shard_map/ppermute | solution.py:716
  86.4 15.3 %collective-permute-start.15 = (bf16[640,512]{1,0:T(8,128)(2,1)S(1)}, bf16[640,512]{1,0:T(8,128)(2,1)}, u32[]{:S(2)}, u32[]{:S(2)}) collective-permute-start(bf16[640,512]{1,0:T(8,128)(2,1)S(1)} %slice.51), channel_id=1, source_target_pairs={{0,16},{4,20},{8,24},{12,28},{16,0},{20,4},{24,8},{28,12},{1,17},{... | collective-permute-start | bytes 1966088 | tf_op jit(solution)/shard_map/ppermute | solution.py:716
  89.6 29.7 %collective-permute-start.20 = (bf16[256,640]{1,0:T(8,128)(2,1)}, bf16[256,640]{1,0:T(8,128)(2,1)S(1)}, u32[]{:S(2)}, u32[]{:S(2)}) collective-permute-start(bf16[256,640]{1,0:T(8,128)(2,1)} %get-tuple-element.99), channel_id=1, source_target_pairs={{0,3},{1,0},{2,1},{3,2},{4,7},{5,4},{6,5},{7,6},{8,11},{9,8},{10,9... | collective-permute-start | bytes 983048 | tf_op jit(solution)/shard_map/ppermute | solution.py:786
  93.2 26.2 %collective-permute-start.19 = (bf16[256,640]{1,0:T(8,128)(2,1)}, bf16[256,640]{1,0:T(8,128)(2,1)S(1)}, u32[]{:S(2)}, u32[]{:S(2)}) collective-permute-start(bf16[256,640]{1,0:T(8,128)(2,1)} %get-tuple-element.100), channel_id=1, source_target_pairs={{0,2},{1,3},{2,0},{3,1},{4,6},{5,7},{6,4},{7,5},{8,10},{9,11},{10,... | collective-permute-start | bytes 983048 | tf_op jit(solution)/shard_map/ppermute | solution.py:786
  93.2 26.2 %collective-permute-start.18 = (bf16[256,640]{1,0:T(8,128)(2,1)}, bf16[256,640]{1,0:T(8,128)(2,1)}, u32[]{:S(2)}, u32[]{:S(2)}) collective-permute-start(bf16[256,640]{1,0:T(8,128)(2,1)} %get-tuple-element.101), channel_id=1, source_target_pairs={{0,1},{1,2},{2,3},{3,0},{4,5},{5,6},{6,7},{7,4},{8,9},{9,10},{10,1... | collective-permute-start | bytes 983048 | tf_op jit(solution)/shard_map/ppermute | solution.py:786
  100.2 19.2 %collective-permute-start.16 = (f32[2,128,768]{2,1,0:T(8,128)S(1)}, f32[2,128,768]{2,1,0:T(8,128)S(1)}, u32[]{:S(2)}, u32[]{:S(2)}) collective-permute-start(f32[2,128,768]{2,1,0:T(8,128)S(1)} %get-tuple-element.66), channel_id=1, source_target_pairs={{0,8},{4,12},{8,0},{12,4},{16,24},{20,28},{24,16},{28,20},{1,9},{5... | collective-permute-start | bytes 2359304 | tf_op jit(solution)/shard_map/ppermute | solution.py:716
  101.6 17.7 %collective-permute-start.17 = (f32[2,128,768]{2,1,0:T(8,128)S(1)}, f32[2,128,768]{2,1,0:T(8,128)S(1)}, u32[]{:S(2)}, u32[]{:S(2)}) collective-permute-start(f32[2,128,768]{2,1,0:T(8,128)S(1)} %get-tuple-element.71), channel_id=1, source_target_pairs={{0,16},{4,20},{8,24},{12,28},{16,0},{20,4},{24,8},{28,12},{1,17},{... | collective-permute-start | bytes 2359304 | tf_op jit(solution)/shard_map/ppermute | solution.py:716
  133.4 30.1 %collective-permute-start.26 = (bf16[4,256,640]{2,1,0:T(8,128)(2,1)S(1)}, bf16[4,256,640]{2,1,0:T(8,128)(2,1)S(1)}, u32[]{:S(2)}, u32[]{:S(2)}) collective-permute-start(bf16[4,256,640]{2,1,0:T(8,128)(2,1)S(1)} %pad_maximum_fusion.3.refs_3_.refs_0_), channel_id=1, source_target_pairs={{0,8},{4,12},{8,0},{12,4},{16,24},{20,28},{24,16},{28,20},{1,9},{5... | collective-permute-start | bytes 3932168 | tf_op jit(solution)/shard_map/ppermute | solution.py:716
  133.9 29.8 %collective-permute-start.27 = (bf16[4,256,640]{2,1,0:T(8,128)(2,1)S(1)}, bf16[4,256,640]{2,1,0:T(8,128)(2,1)S(1)}, u32[]{:S(2)}, u32[]{:S(2)}) collective-permute-start(bf16[4,256,640]{2,1,0:T(8,128)(2,1)S(1)} %pad_maximum_fusion.3.refs_3_.refs_0_), channel_id=1, source_target_pairs={{0,16},{4,20},{8,24},{12,28},{16,0},{20,4},{24,8},{28,12},{1,17},{... | collective-permute-start | bytes 3932168 | tf_op jit(solution)/shard_map/ppermute | solution.py:716
  135.5 31.2 %collective-permute-start.22 = (bf16[512,1024]{1,0:T(8,128)(2,1)S(1)}, bf16[512,1024]{1,0:T(8,128)(2,1)S(1)}, u32[]{:S(2)}, u32[]{:S(2)}) collective-permute-start(bf16[512,1024]{1,0:T(8,128)(2,1)S(1)} %constant_dynamic-update-slice_fusion.refs_0_.c0), channel_id=1, source_target_pairs={{0,1},{1,2},{2,3},{3,0},{4,5},{5,6},{6,7},{7,4},{8,9},{9,10},{10,1... | collective-permute-start | bytes 3145736 | tf_op jit(solution)/shard_map/ppermute | solution.py:798
  163.5 21.4 %collective-permute-start.28 = (bf16[4,256,640]{2,1,0:T(8,128)(2,1)S(1)}, bf16[4,256,640]{2,1,0:T(8,128)(2,1)S(1)}, u32[]{:S(2)}, u32[]{:S(2)}) collective-permute-start(bf16[4,256,640]{2,1,0:T(8,128)(2,1)S(1)} %pad_maximum_fusion.3.refs_3_.refs_0_), channel_id=1, source_target_pairs={{0,4},{4,0},{8,12},{12,8},{16,20},{20,16},{24,28},{28,24},{1,5},{5... | collective-permute-start | bytes 3932168 | tf_op jit(solution)/shard_map/ppermute | solution.py:716
  163.7 19.9 %collective-permute-start.33 = (f32[2,128,768]{2,1,0:T(8,128)S(1)}, f32[2,128,768]{2,1,0:T(8,128)S(1)}, u32[]{:S(2)}, u32[]{:S(2)}) collective-permute-start(f32[2,128,768]{2,1,0:T(8,128)S(1)} %pad_maximum_fusion.4.refs_0_), channel_id=1, source_target_pairs={{0,16},{4,20},{8,24},{12,28},{16,0},{20,4},{24,8},{28,12},{1,17},{... | collective-permute-start | bytes 2359304 | tf_op jit(solution)/shard_map/ppermute | solution.py:716
  165.2 19.7 %collective-permute-start.32 = (f32[2,128,768]{2,1,0:T(8,128)S(1)}, f32[2,128,768]{2,1,0:T(8,128)S(1)}, u32[]{:S(2)}, u32[]{:S(2)}) collective-permute-start(f32[2,128,768]{2,1,0:T(8,128)S(1)} %pad_maximum_fusion.4.refs_0_), channel_id=1, source_target_pairs={{0,8},{4,12},{8,0},{12,4},{16,24},{20,28},{24,16},{28,20},{1,9},{5... | collective-permute-start | bytes 2359304 | tf_op jit(solution)/shard_map/ppermute | solution.py:716
  166.7 19.5 %collective-permute-start.42 = (f32[2,128,768]{2,1,0:T(8,128)S(1)}, f32[2,128,768]{2,1,0:T(8,128)S(1)}, u32[]{:S(2)}, u32[]{:S(2)}) collective-permute-start(f32[2,128,768]{2,1,0:T(8,128)S(1)} %pad_maximum_fusion.4.refs_0_), channel_id=1, source_target_pairs={{0,4},{4,0},{8,12},{12,8},{16,20},{20,16},{24,28},{28,24},{1,5},{5... | collective-permute-start | bytes 2359304 | tf_op jit(solution)/shard_map/ppermute | solution.py:716
  166.7 34.8 %collective-permute-start.23 = (bf16[512,1024]{1,0:T(8,128)(2,1)S(1)}, bf16[512,1024]{1,0:T(8,128)(2,1)S(1)}, u32[]{:S(2)}, u32[]{:S(2)}) collective-permute-start(bf16[512,1024]{1,0:T(8,128)(2,1)S(1)} %collective-permute-done.22.refs_1_.c1), channel_id=1, source_target_pairs={{0,1},{1,2},{2,3},{3,0},{4,5},{5,6},{6,7},{7,4},{8,9},{9,10},{10,1... | collective-permute-start | bytes 3145736 | tf_op jit(solution)/shard_map/ppermute | solution.py:798
  184.9 16.1 %collective-permute-start.35 = (bf16[2,256,640]{2,1,0:T(8,128)(2,1)S(1)}, bf16[2,256,640]{2,1,0:T(8,128)(2,1)S(1)}, u32[]{:S(2)}, u32[]{:S(2)}) collective-permute-start(bf16[2,256,640]{2,1,0:T(8,128)(2,1)S(1)} %slice.57), channel_id=1, source_target_pairs={{0,16},{4,20},{8,24},{12,28},{16,0},{20,4},{24,8},{28,12},{1,17},{... | collective-permute-start | bytes 1966088 | tf_op jit(solution)/shard_map/ppermute | solution.py:716
  185.6 15.8 %collective-permute-start.34 = (bf16[2,256,640]{2,1,0:T(8,128)(2,1)S(1)}, bf16[2,256,640]{2,1,0:T(8,128)(2,1)S(1)}, u32[]{:S(2)}, u32[]{:S(2)}) collective-permute-start(bf16[2,256,640]{2,1,0:T(8,128)(2,1)S(1)} %slice.56), channel_id=1, source_target_pairs={{0,8},{4,12},{8,0},{12,4},{16,24},{20,28},{24,16},{28,20},{1,9},{5... | collective-permute-start | bytes 1966088 | tf_op jit(solution)/shard_map/ppermute | solution.py:716
  186.2 16.8 %collective-permute-start.30 = (bf16[4,256,640]{2,1,0:T(8,128)(2,1)S(1)}, bf16[4,256,640]{2,1,0:T(8,128)(2,1)S(1)}, u32[]{:S(2)}, u32[]{:S(2)}) collective-permute-start(bf16[4,256,640]{2,1,0:T(8,128)(2,1)S(1)} %collective-permute-done.27.refs_5_.refs_2_), channel_id=1, source_target_pairs={{0,4},{4,0},{8,12},{12,8},{16,20},{20,16},{24,28},{28,24},{1,5},{5... | collective-permute-start | bytes 3932168 | tf_op jit(solution)/shard_map/ppermute | solution.py:716
  186.2 18.2 %collective-permute-start.29 = (bf16[4,256,640]{2,1,0:T(8,128)(2,1)S(1)}, bf16[4,256,640]{2,1,0:T(8,128)(2,1)S(1)}, u32[]{:S(2)}, u32[]{:S(2)}) collective-permute-start(bf16[4,256,640]{2,1,0:T(8,128)(2,1)S(1)} %collective-permute-done.26.refs_4_.refs_1_), channel_id=1, source_target_pairs={{0,4},{4,0},{8,12},{12,8},{16,20},{20,16},{24,28},{28,24},{1,5},{5... | collective-permute-start | bytes 3932168 | tf_op jit(solution)/shard_map/ppermute | solution.py:716
  201.5 27.4 %collective-permute-start.31 = (bf16[512,1024]{1,0:T(8,128)(2,1)S(1)}, bf16[512,1024]{1,0:T(8,128)(2,1)S(1)}, u32[]{:S(2)}, u32[]{:S(2)}) collective-permute-start(bf16[512,1024]{1,0:T(8,128)(2,1)S(1)} %collective-permute-done.23.refs_2_.c2), channel_id=1, source_target_pairs={{0,1},{1,2},{2,3},{3,0},{4,5},{5,6},{6,7},{7,4},{8,9},{9,10},{10,1... | collective-permute-start | bytes 3145736 | tf_op jit(solution)/shard_map/ppermute | solution.py:798
  205.0 23.9 %collective-permute-start.37 = (bf16[2,256,640]{2,1,0:T(8,128)(2,1)S(1)}, bf16[2,256,640]{2,1,0:T(8,128)(2,1)S(1)}, u32[]{:S(2)}, u32[]{:S(2)}) collective-permute-start(bf16[2,256,640]{2,1,0:T(8,128)(2,1)S(1)} %collective-permute-done.35.refs_4_), channel_id=1, source_target_pairs={{0,4},{4,0},{8,12},{12,8},{16,20},{20,16},{24,28},{28,24},{1,5},{5... | collective-permute-start | bytes 1966088 | tf_op jit(solution)/shard_map/ppermute | solution.py:716
  205.0 23.9 %collective-permute-start.36 = (bf16[2,256,640]{2,1,0:T(8,128)(2,1)S(1)}, bf16[2,256,640]{2,1,0:T(8,128)(2,1)S(1)}, u32[]{:S(2)}, u32[]{:S(2)}) collective-permute-start(bf16[2,256,640]{2,1,0:T(8,128)(2,1)S(1)} %collective-permute-done.34.refs_3_), channel_id=1, source_target_pairs={{0,4},{4,0},{8,12},{12,8},{16,20},{20,16},{24,28},{28,24},{1,5},{5... | collective-permute-start | bytes 1966088 | tf_op jit(solution)/shard_map/ppermute | solution.py:716
  214.3 19.5 %collective-permute-start.41 = (f32[128,768]{1,0:T(8,128)S(1)}, f32[128,768]{1,0:T(8,128)S(1)}, u32[]{:S(2)}, u32[]{:S(2)}) collective-permute-start(f32[128,768]{1,0:T(8,128)S(1)} %collective-permute-done.39.refs_1_), channel_id=1, source_target_pairs={{0,4},{4,0},{8,12},{12,8},{16,20},{20,16},{24,28},{28,24},{1,5},{5... | collective-permute-start | bytes 1179656 | tf_op jit(solution)/shard_map/ppermute | solution.py:716
  215.4 18.3 %collective-permute-start.40 = (f32[128,768]{1,0:T(8,128)S(1)}, f32[128,768]{1,0:T(8,128)S(1)}, u32[]{:S(2)}, u32[]{:S(2)}) collective-permute-start(f32[128,768]{1,0:T(8,128)S(1)} %collective-permute-done.38.refs_0_), channel_id=1, source_target_pairs={{0,4},{4,0},{8,12},{12,8},{16,20},{20,16},{24,28},{28,24},{1,5},{5... | collective-permute-start | bytes 1179656 | tf_op jit(solution)/shard_map/ppermute | solution.py:716
  (39 other events, 424.2 us)
